TPU v7x, 256 devices: a whole 4x4x8 slice. The times are simulated.
256 devices in a mesh: ctx: 32 (over y, z), tp: 8 (over x, core).
Axes of the slice: x: 4, y: 4, z: 8, core: 2. Of those that a mesh axis runs over, the one named last changes fastest.
Arguments:
- qkv: bfloat16 [32768, 3, 8192], P(('ctx', 'tp')), may hold values from -60 to 60
- gain: float32 [8192], replicated, may hold values from 0.1 to 1.9
Outputs:
- normed: bfloat16 [32768, 8192], P(('ctx', 'tp'))
All inputs are finite; a program needn't handle non-finite values.
Results may differ from a plain program's by a relative error of at most 0.015.
Values may be sent and summed in bfloat16 or wider, within the bound.
No kernel may reach another device: no remote copies, remote signals or barrier semaphores. Data moves between devices by JAX's collectives and lax.ppermute only.
A program may use at most 128 MiB of HBM per device.

v0:
```python
import jax
import jax.numpy as jnp
from jax import lax
from jax.sharding import PartitionSpec as P

DH = 128
STRETCH = 256


def prefix(value, axis, join, neutral):
    place = lax.axis_index(axis)
    gathered = lax.all_gather(value.astype(jnp.bfloat16), axis)
    state = jnp.zeros_like(value) + jnp.asarray(neutral, value.dtype)

    def one(step, state):
        return join(state, lax.dynamic_index_in_dim(gathered, step, 0, False).astype(value.dtype))

    return lax.fori_loop(0, place, one, state)


def add_states(earlier, later):
    return earlier + later


def normalize(attended_output, gain, width):
    values_all = attended_output.astype(jnp.float32)
    meansq = jnp.sum(values_all * values_all, axis=-1, keepdims=True) / width
    return (values_all * lax.rsqrt(meansq + 1e-06) * gain[None, :]).astype(jnp.bfloat16)


def per_device(qkv, gain):
    width = qkv.shape[2]
    local = lax.all_to_all(qkv, "tp", split_axis=2, concat_axis=0, tiled=True)
    rows = local.shape[0]
    local_head_index = local.shape[2] // DH
    nblock = rows // STRETCH
    pieces = local.reshape(nblock, STRETCH, 3, local_head_index, DH)
    query_rows = pieces[:, :, 0]
    keys = pieces[:, :, 1]
    value_rows = pieces[:, :, 2]
    states = jnp.einsum("nchd,nche->nhde", keys, value_rows, preferred_element_type=jnp.float32)
    shard_total = jnp.sum(states, 0)
    inside = jnp.cumsum(states, 0) - states
    empty = jnp.zeros_like(shard_total)
    shard_offset = prefix(shard_total, "ctx", add_states, empty)
    prior_state_sum = (inside + shard_offset[None]).astype(jnp.bfloat16)
    score_matrix = jnp.einsum(
        "nihd,njhd->nhij", query_rows, keys, preferred_element_type=jnp.float32
    )
    row_pos = lax.broadcasted_iota(jnp.int32, (STRETCH, STRETCH), 0)
    col_pos = lax.broadcasted_iota(jnp.int32, (STRETCH, STRETCH), 1)
    score_matrix = jnp.where(
        (col_pos <= row_pos)[None, None], score_matrix, jnp.float32(0.0)
    ).astype(jnp.bfloat16)
    attended_output = jnp.einsum(
        "nhij,njhd->nihd", score_matrix, value_rows, preferred_element_type=jnp.float32
    )
    attended_output = attended_output + jnp.einsum(
        "nihd,nhde->nihe", query_rows, prior_state_sum, preferred_element_type=jnp.float32
    )
    attended_output = attended_output.astype(jnp.bfloat16).reshape(rows, local_head_index * DH)
    gathered = lax.all_to_all(attended_output, "tp", split_axis=0, concat_axis=1, tiled=True)
    return normalize(gathered, gain, width)


def solution(mesh):
    return jax.shard_map(
        per_device,
        mesh=mesh,
        in_specs=(P(("ctx", "tp"), None, None), P()),
        out_specs=P(("ctx", "tp"), None),
        check_vma=False,
    )
```

profile of v0, /device:TPU:248, one launch (start us, length us, event | category | flops | bytes accessed | tf_op | source)
XLA Modules:
  0.0 330.5 jit_solution(16050768003903366580)
XLA Ops:
  6.5 13.1 %copy.23 = bf16[128,3,8192]{0,1,2:T(4,128)(2,1)} copy(bf16[128,3,8192]{2,0,1:T(8,128)(2,1)} %param.4) | data formatting | bytes 12582912 | tf_op args[0]
  19.7 101.6 %all_to_all.28 = bf16[128,3,8192]{0,1,2:T(4,128)(2,1)} all-to-all(bf16[128,3,8192]{0,1,2:T(4,128)(2,1)} %copy.23), channel_id=1, replica_groups=mesh['ctx'=32,'tp'=8] {'tp'}, dimensions={2} | all-to-all | bytes 12582912 | tf_op jit(solution)/shard_map/all_to_all | solution.py:33
  121.3 13.0 %copy.24 = bf16[128,3,8,1024]{3,0,2,1:T(8,128)(2,1)} copy(bf16[128,3,8,1024]{0,1,3,2:T(4,128)(2,1)} %bitcast.51) | data formatting | bytes 12582912 | tf_op jit(solution)/shard_map/all_to_all | solution.py:33
  134.4 4.4 %copy.40 = bf16[384,8,8,128]{3,2,1,0:T(8,128)(2,1)S(1)} copy(bf16[384,8,8,128]{3,1,2,0:T(8,128)(2,1)} %bitcast.53) | data formatting | bytes 12582912
  138.8 1.8 fusion.11
  140.6 2.1 fusion.12
  142.7 7.2 %fusion.1 = f32[4,8,256,128]{3,2,1,0:T(8,128)} fusion(pred[256,256]{1,0:T(8,128)(4,1)S(1)} %iota_compare_fusion, bf16[4,256,1,8,128]{4,3,1,0,2:T(8,128)(2,1)} %get-tuple-element.39, bf16[4,256,1,8,128]{4,3,1,0,2:T(8,128)(2,1)} %copy-done.1, bf16[4,256,1,8,128]{4,3,1,0,2:T(8,128)(2,1)} %copy-done), kind=kOutput, calls=%fused_computation.5 | convolution fusion | flops 1077936128 | bytes 10551296 | tf_op jit(solution)/shard_map/nhij,njhd->nihd/dot_general | solution.py:55
  149.9 85.9 %all-gather.3.cloned.1.call-done = bf16[256,128,128]{2,1,0:T(8,128)(2,1)} async-done(((bf16[8,128,128]{2,1,0:T(8,128)(2,1)}), bf16[256,128,128]{2,1,0:T(8,128)(2,1)}) %all-gather.3.cloned.1.call-update) | async-done | bytes 8388624 | tf_op jit(solution)/shard_map/all_gather | solution.py:12
  235.9 33.8 %while.10 = (s32[]{:T(128)}, f32[8,128,128]{2,1,0:T(8,128)S(1)}, s32[]{:T(128)}, bf16[32,8,128,128]{3,2,1,0:T(8,128)(2,1)}, s32[]{:T(128)}, /*index=5*/s32[]{:T(128)}, s32[]{:T(128)}) while((s32[]{:T(128)}, f32[8,128,128]{2,1,0:T(8,128)S(1)}, s32[]{:T(128)}, bf16[32,8,128,128]{3,2,1,0:T(8,128)(2,1)}, s32[]{:T(128)}, /*index=5*/s32[]{:T(128)}, ...), condition=%wide.region_3.4_spmd, body=%wide.region_2.3_spmd.sunk | while | flops 262149 | bytes 1310843 | solution.py:18
  241.3 1.1 convert_add_fusion.2
  242.4 1.1 convert_add_fusion.2
  243.5 1.1 convert_add_fusion.2
  244.6 1.1 convert_add_fusion.2
  245.7 1.1 convert_add_fusion.2
  246.8 1.1 convert_add_fusion.2
  270.1 1.2 copy-done.2
  271.3 2.9 fusion.4
  274.2 1.4 copy.31
  275.6 2.3 all_to_all.24
  277.8 31.8 %all_to_all.29 = bf16[8,128,1024]{2,1,0:T(8,128)(2,1)S(1)} all-to-all(bf16[8,128,1024]{2,1,0:T(8,128)(2,1)} %all_to_all.24), channel_id=1, replica_groups=mesh['ctx'=32,'tp'=8] {'tp'}, dimensions={0} | all-to-all | bytes 4194304 | tf_op jit(solution)/shard_map/all_to_all | solution.py:62
  310.1 2.4 convert_bitcast_fusion
  312.5 5.3 %copy.32 = f32[128,8,1024]{0,2,1:T(8,128)} copy(f32[128,8,1024]{2,0,1:T(8,128)} %convert_bitcast_fusion) | data formatting | bytes 8388608 | tf_op jit(solution)/shard_map/convert_element_type | solution.py:26
  317.9 2.8 fusion.3
  320.7 2.9 copy.33
  (39 shorter events, 27.7 us)
Async XLA Ops:
  6.5 229.3 %all-gather.3.cloned.1.call-start = ((), (), s32[]{:S(2)}) async-start(), calls=%async_computation.2 | async-start | bytes 8650752 | tf_op jit(solution)/shard_map/all_gather | solution.py:12
  140.5 2.1 copy-start
  140.6 2.1 copy-start.1
  269.7 1.6 copy-start.2
  312.5 5.3 %copy-start.3 = (f32[8192]{0:T(1024)S(1)}, f32[8192]{0:T(1024)}, u32[]{:S(2)}) copy-start(f32[8192]{0:T(1024)} %param.5) | copy-start | bytes 98308
Sparse Core Ops, SparseCore 0:
  142.8 92.9 all-gather.2
where the time goes:
time: 332 us; the launch traced here: 330 us
  blocking collectives  133 us (40%)
  waiting for transfers between devices  85.9 us (26%)
  local copies, waits for them, and re-layouts  45.5 us (14%)
  other arithmetic  39.3 us (12%)
  between operations  13.5 us (4%)
  matrix products  12.2 us (4%)
    all_to_all x1, blocking collectives, per_device(): local = lax.all_to_all(qkv, 'tp', split_axis=2, concat_axis=0, tiled=True)  102 us
    all_gather x1, waiting for transfers between devices, prefix(): gathered = lax.all_gather(value.astype(jnp.bfloat16), axis)  85.9 us
    add x31, other arithmetic, add_states(): return earlier + later  33.2 us
    all_to_all x1, blocking collectives, per_device(): lax.all_to_all(attended_output, 'tp', split_axis=0, concat_axis=1, tiled=...  31.8 us
    unnamed x10, local copies, waits for them, and re-layouts  18.8 us
    all_to_all x1, local copies, waits for them, and re-layouts, per_device(): local = lax.all_to_all(qkv, 'tp', split_axis=2, concat_axis=0, tiled=True)  13 us
    dot_general x1, matrix products, per_device(): jnp.einsum('nhij,njhd->nihd', score_matrix, value_rows, preferred_element...  7.21 us
  transfers between devices with their start and end apart: 1, of which 1 were waited for; matrix products, arithmetic and copies ran while one was open for 2% of the time, Pallas kernels for 0%

commit v1 on v0

v1 whole, which is shorter than its diff:
```python
import functools

import jax
import jax.numpy as jnp
from jax import lax
from jax.experimental import pallas as pl
from jax.experimental.pallas import tpu as pltpu
from jax.sharding import PartitionSpec as P

DH = 128
F32 = jnp.float32
BF16 = jnp.bfloat16


def cost(flops, nbytes):
    return pl.CostEstimate(flops=flops, bytes_accessed=nbytes, transcendentals=0)


def head_state(keys, value_rows, h):
    cols = pl.ds(h * DH, DH)
    return lax.dot_general(
        keys[:, cols], value_rows[:, cols], (((0,), (0,)), ((), ())), preferred_element_type=F32
    )


def send_states_body(place, k_ref, v_ref, out_ref):
    for h in range(out_ref.shape[0]):
        out_ref[h] = head_state(k_ref, v_ref, h).astype(BF16)


def chip_states_body(place, k_ref, v_ref, got_ref, first_ref, *chip_refs):
    step = pl.program_id(0)
    core = place[1]
    for piece, chip_ref in enumerate(chip_refs):

        @pl.when(step == piece)
        def _():
            for h in range(chip_ref.shape[0]):
                mine = head_state(k_ref, v_ref, h)
                got = got_ref[h]
                chip_ref[h] = (mine + got.astype(F32)).astype(BF16)
                first_ref[h] = jnp.where(core == 0, mine.astype(BF16), got)


def inside_body(place, q_ref, k_ref, v_ref, out_ref):
    rows = q_ref.shape[0]
    allowed = lax.broadcasted_iota(jnp.int32, (rows, rows), 1) <= lax.broadcasted_iota(
        jnp.int32, (rows, rows), 0
    )
    for h in range(q_ref.shape[1] // DH):
        cols = pl.ds(h * DH, DH)
        scores = lax.dot_general(
            q_ref[:, cols], k_ref[:, cols], (((1,), (1,)), ((), ())), preferred_element_type=F32
        )
        scores = jnp.where(allowed, scores, 0.0).astype(BF16)
        out_ref[:, cols] = jnp.dot(scores, v_ref[:, cols], preferred_element_type=F32)


def running_sum_body(x_ref, out_ref):
    def one(i, acc):
        out_ref[i] = acc.astype(BF16)
        return acc + x_ref[i].astype(F32)

    lax.fori_loop(0, x_ref.shape[0], one, jnp.zeros(x_ref.shape[1:], F32), unroll=True)


def chip_priors_body(place, base_ref, *refs):
    n = len(refs) // 2
    chips, outs = refs[:n], refs[n:]
    x = place[0]
    where = [lax.rem(x - d + n, n) for d in range(n)]
    base = base_ref[...].astype(F32)
    terms = [c[...].astype(F32) for c in chips]
    for d in range(n):
        acc = base
        for e in range(n):
            if e != d:
                acc = acc + jnp.where(where[e] < where[d], terms[e], 0.0)
        outs[d][...] = acc.astype(BF16)


def core_priors_body(place, first_ref, *refs):
    n = len(refs) - 2
    parts, keep_ref, send_ref = refs[:n], refs[n], refs[n + 1]
    step = pl.program_id(0)
    core = place[1]
    for piece, part in enumerate(parts):

        @pl.when(step == piece)
        def _():
            prior = part[...]
            later = (prior.astype(F32) + first_ref[...].astype(F32)).astype(BF16)
            keep_ref[...] = jnp.where(core == 0, prior, later)
            send_ref[...] = jnp.where(core == 0, later, prior)


def attend_body(place, q_ref, inside_ref, prior_ref, out_ref, sq_ref):
    total = jnp.zeros((q_ref.shape[0], DH), F32)
    for h in range(q_ref.shape[1] // DH):
        cols = pl.ds(h * DH, DH)
        value = inside_ref[:, cols] + jnp.dot(
            q_ref[:, cols], prior_ref[h], preferred_element_type=F32
        )
        value = value.astype(BF16)
        out_ref[:, cols] = value
        value = value.astype(F32)
        total = total + value * value

    @pl.when(pl.program_id(0) == 0)
    def _():
        sq_ref[...] = total

    @pl.when(pl.program_id(0) > 0)
    def _():
        sq_ref[...] += total


def finish_body(nx, place, q_ref, inside_ref, prior_ref, kept_ref, sq_ref, gain_ref, out_ref, sum_ref):
    step = pl.program_id(0)
    core = place[1]
    width = q_ref.shape[1]
    group = (1 - core) * nx + lax.rem(place[0] + step, nx)

    @pl.when(step == 0)
    def _():
        sum_ref[...] = sq_ref[...]

    total = jnp.zeros((q_ref.shape[0], DH), F32)
    for h in range(width // DH):
        cols = pl.ds(h * DH, DH)
        value = inside_ref[:, cols] + jnp.dot(
            q_ref[:, cols], prior_ref[h], preferred_element_type=F32
        )
        value = value.astype(BF16)
        out_ref[:, pl.ds(pl.multiple_of(group * width + h * DH, DH), DH)] = value
        value = value.astype(F32)
        total = total + value * value
    sum_ref[...] += total

    @pl.when(step == nx - 1)
    def _():
        meansq = jnp.sum(sum_ref[...], axis=-1, keepdims=True) / out_ref.shape[1]
        scale = lax.rsqrt(meansq + 1e-06)
        for piece in range(nx):
            mine = pl.multiple_of((core * nx + lax.rem(place[0] + piece, nx)) * width, width)
            other = pl.multiple_of(((1 - core) * nx + piece) * width, width)
            for h in range(width // DH):
                cols = pl.ds(mine + h * DH, DH)
                value = kept_ref[:, pl.ds(piece * width + h * DH, DH)].astype(F32)
                out_ref[:, cols] = (value * scale * gain_ref[:, cols]).astype(BF16)
                cols = pl.ds(other + h * DH, DH)
                value = out_ref[:, cols].astype(F32)
                out_ref[:, cols] = (value * scale * gain_ref[:, cols]).astype(BF16)


def per_device(nx, nctx, qkv, gain):
    rows, _, width = qkv.shape
    heads = width // DH
    half = heads // 2
    each = half // nx
    block = each * DH
    tp = lax.axis_index("tp")
    place = jnp.stack([tp // 2, lax.rem(tp, 2)]).astype(jnp.int32)
    rolled = jnp.transpose(qkv, (1, 0, 2))
    swap = [(i, i ^ 1) for i in range(2 * nx)]

    def shift(d):
        return [(2 * x + c, 2 * ((x + d) % nx) + c) for x in range(nx) for c in range(2)]

    def columns(which, own):
        def index(i, place):
            side = place[1] if own else 1 - place[1]
            return (which, 0, side * nx + lax.rem(place[0] + i, nx))

        return pl.BlockSpec((None, rows, block), index)

    def flat(own):
        def index(i, place):
            side = place[1] if own else 1 - place[1]
            return (0, side * nx + lax.rem(place[0] + i, nx))

        return pl.BlockSpec((rows, block), index)

    by_step = pl.BlockSpec((each, DH, DH), lambda i, place: (i, 0, 0))
    fixed = pl.BlockSpec((each, DH, DH), lambda i, place: (0, 0, 0))
    half_states = jax.ShapeDtypeStruct((half, DH, DH), BF16)
    part_states = jax.ShapeDtypeStruct((each, DH, DH), BF16)

    def call(body, grid, in_specs, out_specs, out_shape, scratch=(), cost_estimate=None):
        return pl.pallas_call(
            body,
            grid_spec=pltpu.PrefetchScalarGridSpec(
                num_scalar_prefetch=1,
                grid=grid,
                in_specs=in_specs,
                out_specs=out_specs,
                scratch_shapes=scratch,
            ),
            out_shape=out_shape,
            cost_estimate=cost_estimate,
            compiler_params=pltpu.CompilerParams(vmem_limit_bytes=40 * 2**20),
        )

    flops = 2 * half * rows * DH * DH
    send = call(
        send_states_body,
        (nx,),
        [columns(1, False), columns(2, False)],
        by_step,
        half_states,
        cost_estimate=cost(flops, 3 * 2**20),
    )(place, rolled, rolled)
    got = lax.ppermute(send, "tp", swap)
    first, *chips = call(
        chip_states_body,
        (nx,),
        [columns(1, True), columns(2, True), by_step],
        [by_step] + [fixed] * nx,
        [half_states] + [part_states] * nx,
        cost_estimate=cost(flops, 5 * 2**20),
    )(place, rolled, rolled, got)
    chips = [chips[0]] + [lax.ppermute(chips[d], "tp", shift(d)) for d in range(1, nx)]

    inside = call(
        inside_body,
        (2 * nx,),
        [pl.BlockSpec((None, rows, block), lambda i, place, w=w: (w, 0, i)) for w in range(3)],
        pl.BlockSpec((rows, block), lambda i, place: (0, i)),
        jax.ShapeDtypeStruct((rows, width), F32),
        cost_estimate=cost(4 * flops, 10 * 2**20),
    )(place, rolled, rolled, rolled)

    total = sum(c.astype(F32) for c in chips).astype(BF16)
    piece = each * DH // nctx
    spread = lax.all_to_all(
        total.reshape(nctx, piece, DH), "ctx", split_axis=0, concat_axis=0, tiled=True
    )
    spread = pl.pallas_call(
        running_sum_body, out_shape=jax.ShapeDtypeStruct(spread.shape, BF16)
    )(spread)
    base = lax.all_to_all(spread, "ctx", split_axis=0, concat_axis=0, tiled=True)
    base = base.reshape(each, DH, DH)

    two = pl.BlockSpec((2, DH, DH), lambda i, place: (i, 0, 0))
    parts = call(
        chip_priors_body,
        (each // 2,),
        [two] * (nx + 1),
        [two] * nx,
        [part_states] * nx,
        cost_estimate=cost(0, 3 * 2**20),
    )(place, base, *chips)
    parts = [parts[0]] + [lax.ppermute(parts[d], "tp", shift(-d)) for d in range(1, nx)]
    keep, give = call(
        core_priors_body,
        (nx,),
        [by_step] + [fixed] * nx,
        [by_step, by_step],
        [half_states, half_states],
        cost_estimate=cost(0, 4 * 2**20),
    )(place, first, *parts)
    other = lax.ppermute(give, "tp", swap)

    kept, sq = call(
        attend_body,
        (nx,),
        [columns(0, True), flat(True), by_step],
        [
            pl.BlockSpec((rows, block), lambda i, place: (0, i)),
            pl.BlockSpec((rows, DH), lambda i, place: (0, 0)),
        ],
        [jax.ShapeDtypeStruct((rows, width // 2), BF16), jax.ShapeDtypeStruct((rows, DH), F32)],
        cost_estimate=cost(flops, 5 * 2**20),
    )(place, rolled, inside, keep)
    return call(
        functools.partial(finish_body, nx),
        (nx,),
        [
            columns(0, False),
            flat(False),
            by_step,
            pl.BlockSpec((rows, width // 2), lambda i, place: (0, 0)),
            pl.BlockSpec((rows, DH), lambda i, place: (0, 0)),
            pl.BlockSpec((1, width), lambda i, place: (0, 0)),
        ],
        pl.BlockSpec((rows, width), lambda i, place: (0, 0)),
        jax.ShapeDtypeStruct((rows, width), BF16),
        scratch=[pltpu.VMEM((rows, DH), F32)],
        cost_estimate=cost(flops, 7 * 2**20),
    )(place, rolled, inside, other, kept, sq, gain.reshape(1, width))


def solution(mesh):
    return jax.shard_map(
        functools.partial(per_device, mesh.shape["tp"] // 2, mesh.shape["ctx"]),
        mesh=mesh,
        in_specs=(P(("ctx", "tp"), None, None), P()),
        out_specs=P(("ctx", "tp"), None),
        check_vma=False,
    )
```

time: 332 us -> 107 us (0.32)
  the two profiles are of different devices: /device:TPU:248 before, /device:TPU:1 now
where the time goes in v1:
time: 107 us
  blocking collectives  35.5 us (33%)
  waiting for transfers between devices  26.5 us (25%)
  Pallas kernels  26.4 us (25%)
  starting transfers between devices  12.5 us (12%)
  local copies, waits for them, and re-layouts  5.57 us (5%)
    all_to_all x1, blocking collectives, per_device(): lax.all_to_all(total.reshape(nctx, piece, DH), 'ctx', split_axis=0, conca...  19.7 us
    all_to_all x1, blocking collectives, per_device(): lax.all_to_all(spread, 'ctx', split_axis=0, concat_axis=0, tiled=True)  15.8 us
    ppermute x3, waiting for transfers between devices, per_device(): lax.ppermute(parts[d], 'tp', shift(-d))  12.6 us
    pallas_call x1, Pallas kernels, per_device(): call(inside_body, (2 * nx,), [pl.BlockSpec((None, rows, block), lambda i,...  12 us
    ppermute x3, waiting for transfers between devices, per_device(): lax.ppermute(chips[d], 'tp', shift(d))  11.6 us
    unnamed x6, local copies, waits for them, and re-layouts  5.57 us
    pallas_call x1, Pallas kernels, per_device(): call(functools.partial(finish_body, nx), (nx,), [columns(0, False), flat(...  4.29 us
    ppermute x3, starting transfers between devices, per_device(): lax.ppermute(parts[d], 'tp', shift(-d))  3.69 us
  transfers between devices with their start and end apart: 8, of which 6 were waited for; matrix products, arithmetic and copies ran while one was open for 0% of the time, Pallas kernels for 13%

profile of v1, /device:TPU:1, one launch (start us, length us, event | category | flops | bytes accessed | tf_op | source)
XLA Modules:
  0.0 106.8 jit_solution(14990092579514946321)
XLA Ops:
  0.1 2.8 %copy-done = bf16[128,3,8192]{2,0,1:T(8,128)(2,1)S(1)} copy-done((bf16[128,3,8192]{2,0,1:T(8,128)(2,1)S(1)}, bf16[128,3,8192]{2,0,1:T(8,128)(2,1)}, u32[]{:S(2)}) %copy-start) | copy-done | bytes 6291480
  2.9 1.9 %shard_map.29 = bf16[32,128,128]{2,1,0:T(8,128)(2,1)S(1)} custom-call(s32[2]{0:T(128)S(1)} %pad_add_fusion.place, bf16[3,128,8192]{2,1,0:T(8,128)(2,1)S(1)} %bitcast.6, bf16[3,128,8192]{2,1,0:T(8,128)(2,1)S(1)} %bitcast.7), custom_call_target="tpu_custom_call" | custom-call | flops 134217728 | bytes 3145728 | tf_op jit(solution)/shard_map/pallas_call | solution.py:205
  4.8 3.3 %collective-permute-start = (bf16[32,128,128]{2,1,0:T(8,128)(2,1)S(1)}, bf16[32,128,128]{2,1,0:T(8,128)(2,1)S(1)}, u32[]{:S(2)}, u32[]{:S(2)}) collective-permute-start(bf16[32,128,128]{2,1,0:T(8,128)(2,1)S(1)} %shard_map.29), channel_id=1, source_target_pairs={{0,1},{1,0},{2,3},{3,2},{4,5},{5,4},{6,7},{7,6},{8,9},{9,8},{10,11... | collective-permute-start | bytes 3145736 | tf_op jit(solution)/shard_map/ppermute | solution.py:213
  8.1 2.3 %collective-permute-done.got_ref = bf16[32,128,128]{2,1,0:T(8,128)(2,1)S(1)} collective-permute-done((bf16[32,128,128]{2,1,0:T(8,128)(2,1)S(1)}, bf16[32,128,128]{2,1,0:T(8,128)(2,1)S(1)}, u32[]{:S(2)}, u32[]{:S(2)}) %collective-permute-start) | collective-permute-done | bytes 1048608 | tf_op jit(solution)/shard_map/ppermute | solution.py:213
  10.4 2.0 %shard_map.30 = (bf16[32,128,128]{2,1,0:T(8,128)(2,1)S(1)}, bf16[8,128,128]{2,1,0:T(8,128)(2,1)S(1)}, bf16[8,128,128]{2,1,0:T(8,128)(2,1)S(1)}, bf16[8,128,128]{2,1,0:T(8,128)(2,1)S(1)}, bf16[8,128,128]{2,1,0:T(8,128)(2,1)S(1)}) custom-call(s32[2]{0:T(128)S(1)} %pad_add_fusion.place, bf16[3,128,8192]{2,1,0:T(8,128)(2,1)S(1)} %bitcast.8, ...), custom_call_target="tpu_custom_call" | custom-call | flops 134217728 | bytes 5242880 | tf_op jit(solution)/shard_map/pallas_call | solution.py:214
  12.5 1.9 %collective-permute-start.2 = (bf16[8,128,128]{2,1,0:T(8,128)(2,1)S(1)}, bf16[8,128,128]{2,1,0:T(8,128)(2,1)S(1)}, u32[]{:S(2)}, u32[]{:S(2)}) collective-permute-start(bf16[8,128,128]{2,1,0:T(8,128)(2,1)S(1)} %get-tuple-element.21), channel_id=1, source_target_pairs={{0,4},{1,5},{2,6},{3,7},{4,0},{5,1},{6,2},{7,3},{8,12},{9,13},{10,... | collective-permute-start | bytes 786440 | tf_op jit(solution)/shard_map/ppermute | solution.py:222
  14.4 1.2 %collective-permute-start.3 = (bf16[8,128,128]{2,1,0:T(8,128)(2,1)S(1)}, bf16[8,128,128]{2,1,0:T(8,128)(2,1)S(1)}, u32[]{:S(2)}, u32[]{:S(2)}) collective-permute-start(bf16[8,128,128]{2,1,0:T(8,128)(2,1)S(1)} %get-tuple-element.22), channel_id=1, source_target_pairs={{0,6},{1,7},{2,0},{3,1},{4,2},{5,3},{6,4},{7,5},{8,14},{9,15},{10,... | collective-permute-start | bytes 786440 | tf_op jit(solution)/shard_map/ppermute | solution.py:222
  15.6 6.4 %collective-permute-done.1.refs_1_ = bf16[8,128,128]{2,1,0:T(8,128)(2,1)S(1)} collective-permute-done((bf16[8,128,128]{2,1,0:T(8,128)(2,1)S(1)}, bf16[8,128,128]{2,1,0:T(8,128)(2,1)S(1)}, u32[]{:S(2)}, u32[]{:S(2)}) %collective-permute-start.1) | collective-permute-done | bytes 262176 | tf_op jit(solution)/shard_map/ppermute | solution.py:222
  22.0 4.2 %collective-permute-done.2.refs_2_ = bf16[8,128,128]{2,1,0:T(8,128)(2,1)S(1)} collective-permute-done((bf16[8,128,128]{2,1,0:T(8,128)(2,1)S(1)}, bf16[8,128,128]{2,1,0:T(8,128)(2,1)S(1)}, u32[]{:S(2)}, u32[]{:S(2)}) %collective-permute-start.2) | collective-permute-done | bytes 262176 | tf_op jit(solution)/shard_map/ppermute | solution.py:222
  26.1 1.0 collective-permute-done.3.refs_3_
  27.3 19.7 %all_to_all.10.x_ref = bf16[32,32,128]{2,1,0:T(8,128)(2,1)} all-to-all(bf16[32,32,128]{2,1,0:T(8,128)(2,1)S(1)} %bitcast.17), channel_id=1, replica_groups=mesh['ctx'=32,'tp'=8] {'ctx'}, dimensions={0} | all-to-all | bytes 524288 | tf_op jit(solution)/shard_map/all_to_all | solution.py:235
  47.0 1.7 %shard_map.31 = bf16[32,32,128]{2,1,0:T(8,128)(2,1)} custom-call(bf16[32,32,128]{2,1,0:T(8,128)(2,1)} %all_to_all.10.x_ref), custom_call_target="tpu_custom_call" | custom-call | tf_op jit(solution)/shard_map/pallas_call | solution.py:238
  48.7 15.8 %all_to_all.11 = bf16[32,32,128]{2,1,0:T(8,128)(2,1)S(1)} all-to-all(bf16[32,32,128]{2,1,0:T(8,128)(2,1)} %shard_map.31), channel_id=1, replica_groups=mesh['ctx'=32,'tp'=8] {'ctx'}, dimensions={0} | all-to-all | bytes 524288 | tf_op jit(solution)/shard_map/all_to_all | solution.py:241
  64.5 1.2 %shard_map.32 = (bf16[8,128,128]{2,1,0:T(8,128)(2,1)S(1)}, bf16[8,128,128]{2,1,0:T(8,128)(2,1)S(1)}, bf16[8,128,128]{2,1,0:T(8,128)(2,1)S(1)}, bf16[8,128,128]{2,1,0:T(8,128)(2,1)S(1)}) custom-call(s32[2]{0:T(128)S(1)} %pad_add_fusion.place, bf16[8,128,128]{2,1,0:T(8,128)(2,1)S(1)} %bitcast.15, bf16[8,128,128]{2,1,0:T(8,128)(2,1)S(1)} %get-tuple-element.19.refs_0_, ...), custom_call_target="tpu_custom_call" | custom-call | bytes 3145728 | tf_op jit(solution)/shard_map/pallas_call | solution.py:245
  65.7 3.0 %collective-permute-start.4 = (bf16[8,128,128]{2,1,0:T(8,128)(2,1)S(1)}, bf16[8,128,128]{2,1,0:T(8,128)(2,1)S(1)}, u32[]{:S(2)}, u32[]{:S(2)}) collective-permute-start(bf16[8,128,128]{2,1,0:T(8,128)(2,1)S(1)} %get-tuple-element.24), channel_id=1, source_target_pairs={{0,6},{1,7},{2,0},{3,1},{4,2},{5,3},{6,4},{7,5},{8,14},{9,15},{10,... | collective-permute-start | bytes 786440 | tf_op jit(solution)/shard_map/ppermute | solution.py:253
  68.7 0.7 collective-permute-start.6
  69.4 6.1 %collective-permute-done.4.refs_1_ = bf16[8,128,128]{2,1,0:T(8,128)(2,1)S(1)} collective-permute-done((bf16[8,128,128]{2,1,0:T(8,128)(2,1)S(1)}, bf16[8,128,128]{2,1,0:T(8,128)(2,1)S(1)}, u32[]{:S(2)}, u32[]{:S(2)}) %collective-permute-start.4) | collective-permute-done | bytes 262176 | tf_op jit(solution)/shard_map/ppermute | solution.py:253
  75.5 6.5 %collective-permute-done.6.refs_3_ = bf16[8,128,128]{2,1,0:T(8,128)(2,1)S(1)} collective-permute-done((bf16[8,128,128]{2,1,0:T(8,128)(2,1)S(1)}, bf16[8,128,128]{2,1,0:T(8,128)(2,1)S(1)}, u32[]{:S(2)}, u32[]{:S(2)}) %collective-permute-start.6) | collective-permute-done | bytes 262176 | tf_op jit(solution)/shard_map/ppermute | solution.py:253
  82.0 1.3 %shard_map.33 = (bf16[32,128,128]{2,1,0:T(8,128)(2,1)S(1)}, bf16[32,128,128]{2,1,0:T(8,128)(2,1)S(1)}) custom-call(s32[2]{0:T(128)S(1)} %pad_add_fusion.place, bf16[32,128,128]{2,1,0:T(8,128)(2,1)S(1)} %get-tuple-element.18.first_ref, bf16[8,128,128]{2,1,0:T(8,128)(2,1)S(1)} %get-tuple-element.23.refs_0_, ...), custom_call_target="tpu_custom_call" | custom-call | bytes 4194304 | tf_op jit(solution)/shard_map/pallas_call | solution.py:254
  83.3 2.3 %collective-permute-start.7 = (bf16[32,128,128]{2,1,0:T(8,128)(2,1)S(1)}, bf16[32,128,128]{2,1,0:T(8,128)(2,1)S(1)}, u32[]{:S(2)}, u32[]{:S(2)}) collective-permute-start(bf16[32,128,128]{2,1,0:T(8,128)(2,1)S(1)} %get-tuple-element.27), channel_id=1, source_target_pairs={{0,1},{1,0},{2,3},{3,2},{4,5},{5,4},{6,7},{7,6},{8,9},{9,8},{10,11... | collective-permute-start | bytes 3145736 | tf_op jit(solution)/shard_map/ppermute | solution.py:262
  85.6 2.8 %copy-done.1 = bf16[128,3,8192]{2,0,1:T(8,128)(2,1)S(1)} copy-done((bf16[128,3,8192]{2,0,1:T(8,128)(2,1)S(1)}, bf16[128,3,8192]{2,0,1:T(8,128)(2,1)}, u32[]{:S(2)}) %copy-start.1) | copy-done | bytes 6291480
  88.4 12.0 %shard_map.28.inside_ref = f32[128,8192]{1,0:T(8,128)S(1)} custom-call(s32[2]{0:T(128)S(1)} %pad_add_fusion.place, bf16[3,128,8192]{2,1,0:T(8,128)(2,1)S(1)} %bitcast.10, bf16[3,128,8192]{2,1,0:T(8,128)(2,1)S(1)} %bitcast.11, bf16[3,128,8192]{2,1,0:T(8,128)(2,1)S(1)} %bitcast.12), custom_call_target="tpu_custom_call" | custom-call | flops 536870912 | bytes 10485760 | tf_op jit(solution)/shard_map/pallas_call | solution.py:224
  100.4 2.1 %shard_map.34 = (bf16[128,4096]{1,0:T(8,128)(2,1)S(1)}, f32[128,128]{1,0:T(8,128)S(1)}) custom-call(s32[2]{0:T(128)S(1)} %pad_add_fusion.place, bf16[3,128,8192]{2,1,0:T(8,128)(2,1)S(1)} %bitcast.13, f32[128,8192]{1,0:T(8,128)S(1)} %shard_map.28.inside_ref, bf16[32,128,128]{2,1,0:T(8,128)(2,1)S(1)} %get-tuple-element.28.prior_ref), custom_call_target="tpu_custom_call" | custom-call | flops 134217728 | bytes 5242880 | tf_op jit(solution)/shard_map/pallas_call | solution.py:264
  102.5 4.3 %shard_map.35 = bf16[128,8192]{1,0:T(8,128)(2,1)} custom-call(s32[2]{0:T(128)S(1)} %pad_add_fusion.place, bf16[3,128,8192]{2,1,0:T(8,128)(2,1)S(1)} %bitcast.14, f32[128,8192]{1,0:T(8,128)S(1)} %shard_map.28.inside_ref, bf16[32,128,128]{2,1,0:T(8,128)(2,1)S(1)} %collective-permute-done.7.prior_ref, bf16[128,4096]{1,0:T(8,128)(2,1)S(1)} %get-tuple-element.29.kept_ref, ...), custom_call_target="tpu_custom_call" | custom-call | flops 134217728 | bytes 7340032 | tf_op jit(solution)/shard_map/pallas_call | solution.py:275
  (10 shorter events, 0.4 us)
Async XLA Ops:
  0.1 2.8 %copy-start = (bf16[128,3,8192]{2,0,1:T(8,128)(2,1)S(1)}, bf16[128,3,8192]{2,0,1:T(8,128)(2,1)}, u32[]{:S(2)}) copy-start(bf16[128,3,8192]{2,0,1:T(8,128)(2,1)} %param.2) | copy-start | bytes 18874372
  4.8 5.6 %collective-permute-start = (bf16[32,128,128]{2,1,0:T(8,128)(2,1)S(1)}, bf16[32,128,128]{2,1,0:T(8,128)(2,1)S(1)}, u32[]{:S(2)}, u32[]{:S(2)}) collective-permute-start(bf16[32,128,128]{2,1,0:T(8,128)(2,1)S(1)} %shard_map.29), channel_id=1, source_target_pairs={{0,1},{1,0},{2,3},{3,2},{4,5},{5,4},{6,7},{7,6},{8,9},{9,8},{10,11... | collective-permute-start | bytes 3145736 | tf_op jit(solution)/shard_map/ppermute | solution.py:213
  12.4 9.6 %collective-permute-start.1 = (bf16[8,128,128]{2,1,0:T(8,128)(2,1)S(1)}, bf16[8,128,128]{2,1,0:T(8,128)(2,1)S(1)}, u32[]{:S(2)}, u32[]{:S(2)}) collective-permute-start(bf16[8,128,128]{2,1,0:T(8,128)(2,1)S(1)} %get-tuple-element.20), channel_id=1, source_target_pairs={{0,2},{1,3},{2,4},{3,5},{4,6},{5,7},{6,0},{7,1},{8,10},{9,11},{10,... | collective-permute-start | bytes 786440 | tf_op jit(solution)/shard_map/ppermute | solution.py:222
  12.5 13.6 %collective-permute-start.2 = (bf16[8,128,128]{2,1,0:T(8,128)(2,1)S(1)}, bf16[8,128,128]{2,1,0:T(8,128)(2,1)S(1)}, u32[]{:S(2)}, u32[]{:S(2)}) collective-permute-start(bf16[8,128,128]{2,1,0:T(8,128)(2,1)S(1)} %get-tuple-element.21), channel_id=1, source_target_pairs={{0,4},{1,5},{2,6},{3,7},{4,0},{5,1},{6,2},{7,3},{8,12},{9,13},{10,... | collective-permute-start | bytes 786440 | tf_op jit(solution)/shard_map/ppermute | solution.py:222
  14.4 12.7 %collective-permute-start.3 = (bf16[8,128,128]{2,1,0:T(8,128)(2,1)S(1)}, bf16[8,128,128]{2,1,0:T(8,128)(2,1)S(1)}, u32[]{:S(2)}, u32[]{:S(2)}) collective-permute-start(bf16[8,128,128]{2,1,0:T(8,128)(2,1)S(1)} %get-tuple-element.22), channel_id=1, source_target_pairs={{0,6},{1,7},{2,0},{3,1},{4,2},{5,3},{6,4},{7,5},{8,14},{9,15},{10,... | collective-permute-start | bytes 786440 | tf_op jit(solution)/shard_map/ppermute | solution.py:222
  65.7 9.8 %collective-permute-start.4 = (bf16[8,128,128]{2,1,0:T(8,128)(2,1)S(1)}, bf16[8,128,128]{2,1,0:T(8,128)(2,1)S(1)}, u32[]{:S(2)}, u32[]{:S(2)}) collective-permute-start(bf16[8,128,128]{2,1,0:T(8,128)(2,1)S(1)} %get-tuple-element.24), channel_id=1, source_target_pairs={{0,6},{1,7},{2,0},{3,1},{4,2},{5,3},{6,4},{7,5},{8,14},{9,15},{10,... | collective-permute-start | bytes 786440 | tf_op jit(solution)/shard_map/ppermute | solution.py:253
  68.7 6.8 %collective-permute-start.5 = (bf16[8,128,128]{2,1,0:T(8,128)(2,1)S(1)}, bf16[8,128,128]{2,1,0:T(8,128)(2,1)S(1)}, u32[]{:S(2)}, u32[]{:S(2)}) collective-permute-start(bf16[8,128,128]{2,1,0:T(8,128)(2,1)S(1)} %get-tuple-element.25), channel_id=1, source_target_pairs={{0,4},{1,5},{2,6},{3,7},{4,0},{5,1},{6,2},{7,3},{8,12},{9,13},{10,... | collective-permute-start | bytes 786440 | tf_op jit(solution)/shard_map/ppermute | solution.py:253
  68.7 13.3 %collective-permute-start.6 = (bf16[8,128,128]{2,1,0:T(8,128)(2,1)S(1)}, bf16[8,128,128]{2,1,0:T(8,128)(2,1)S(1)}, u32[]{:S(2)}, u32[]{:S(2)}) collective-permute-start(bf16[8,128,128]{2,1,0:T(8,128)(2,1)S(1)} %get-tuple-element.26), channel_id=1, source_target_pairs={{0,2},{1,3},{2,4},{3,5},{4,6},{5,7},{6,0},{7,1},{8,10},{9,11},{10,... | collective-permute-start | bytes 786440 | tf_op jit(solution)/shard_map/ppermute | solution.py:253
  83.3 19.2 %collective-permute-start.7 = (bf16[32,128,128]{2,1,0:T(8,128)(2,1)S(1)}, bf16[32,128,128]{2,1,0:T(8,128)(2,1)S(1)}, u32[]{:S(2)}, u32[]{:S(2)}) collective-permute-start(bf16[32,128,128]{2,1,0:T(8,128)(2,1)S(1)} %get-tuple-element.27), channel_id=1, source_target_pairs={{0,1},{1,0},{2,3},{3,2},{4,5},{5,4},{6,7},{7,6},{8,9},{9,8},{10,11... | collective-permute-start | bytes 3145736 | tf_op jit(solution)/shard_map/ppermute | solution.py:262
  85.6 2.8 %copy-start.1 = (bf16[128,3,8192]{2,0,1:T(8,128)(2,1)S(1)}, bf16[128,3,8192]{2,0,1:T(8,128)(2,1)}, u32[]{:S(2)}) copy-start(bf16[128,3,8192]{2,0,1:T(8,128)(2,1)} %param.2) | copy-start | bytes 18874372
  100.4 2.1 %copy-start.2 = (f32[8192]{0:T(1024)S(1)}, f32[8192]{0:T(1024)}, u32[]{:S(2)}) copy-start(f32[8192]{0:T(1024)} %param.3) | copy-start | bytes 98308

commit v2 on v0

v2 whole, which is shorter than its diff:
```python
import functools

import jax
import jax.numpy as jnp
from jax import lax
from jax.experimental import pallas as pl
from jax.experimental.pallas import tpu as pltpu
from jax.sharding import PartitionSpec as P

DH = 128
F32 = jnp.float32
BF16 = jnp.bfloat16
VMEM = pl.BlockSpec(memory_space=pltpu.VMEM)
SMEM = pl.BlockSpec(memory_space=pltpu.SMEM)
HBM = pl.BlockSpec(memory_space=pltpu.HBM)


def head_state(keys, value_rows):
    return lax.dot_general(
        keys, value_rows, (((0,), (0,)), ((), ())), preferred_element_type=F32
    )


def send_states_body(place, qkv_ref, out_ref, k_buf, v_buf, sems):
    n, _, block = k_buf.shape
    each = block // DH
    first = (1 - place[1]) * n
    copies = []
    for i in range(n):
        cols = pl.ds(pl.multiple_of((first + i) * block, block), block)
        pair = []
        for which, buf in ((1, k_buf), (2, v_buf)):
            copy = pltpu.make_async_copy(
                qkv_ref.at[which, :, cols], buf.at[i], sems.at[which - 1, i]
            )
            copy.start()
            pair.append(copy)
        copies.append(pair)
    for i in range(n):
        for copy in copies[i]:
            copy.wait()
        for h in range(each):
            cols = pl.ds(h * DH, DH)
            out_ref[i * each + h] = head_state(k_buf[i, :, cols], v_buf[i, :, cols]).astype(BF16)


def own_states_body(place, qkv_ref, out_ref):
    half = out_ref.shape[0]
    first = place[1] * half
    for h in range(half):
        cols = pl.ds(pl.multiple_of((first + h) * DH, DH), DH)
        out_ref[h] = head_state(qkv_ref[1, :, cols], qkv_ref[2, :, cols])


def chip_states_body(place, own_ref, got_ref, *chip_refs):
    n = len(chip_refs)
    each = chip_refs[0].shape[0]
    for d in range(n):
        first = lax.rem(place[0] + d, n) * each
        for h in range(each):
            chip_refs[d][h] = (own_ref[first + h] + got_ref[first + h].astype(F32)).astype(BF16)


def scores_body(place, qkv_ref, own_ref, got_ref, out_ref, first_ref):
    rows = out_ref.shape[0]
    allowed = lax.broadcasted_iota(jnp.int32, (rows, rows), 1) <= lax.broadcasted_iota(
        jnp.int32, (rows, rows), 0
    )
    for h in range(out_ref.shape[1] // DH):
        cols = pl.ds(h * DH, DH)
        scores = lax.dot_general(
            qkv_ref[0, :, cols],
            qkv_ref[1, :, cols],
            (((1,), (1,)), ((), ())),
            preferred_element_type=F32,
        )
        out_ref[:, cols] = jnp.where(allowed, scores, 0.0).astype(BF16)

    @pl.when(place[1] == 0)
    def _():
        first_ref[...] = own_ref[...].astype(BF16)

    @pl.when(place[1] != 0)
    def _():
        first_ref[...] = got_ref[...]


def running_sum_body(x_ref, out_ref):
    acc = jnp.zeros(x_ref.shape[1:], F32)
    for i in range(x_ref.shape[0]):
        out_ref[i] = acc.astype(BF16)
        acc = acc + x_ref[i].astype(F32)


def chip_priors_body(place, base_ref, *refs):
    n = len(refs) // 2
    chips, outs = refs[:n], refs[n:]
    x = place[0]
    where = [lax.rem(x - d + n, n) for d in range(n)]
    weight = [
        [None if e == d else jnp.where(where[e] < where[d], 1.0, 0.0) for e in range(n)]
        for d in range(n)
    ]
    for h in range(base_ref.shape[0]):
        base = base_ref[h].astype(F32)
        terms = [c[h].astype(F32) for c in chips]
        for d in range(n):
            acc = base
            for e in range(n):
                if e != d:
                    acc = acc + terms[e] * weight[d][e]
            outs[d][h] = acc.astype(BF16)


def core_priors_body(place, first_ref, *refs):
    n = len(refs) - 2
    parts, keep_ref, send_ref = refs[:n], refs[n], refs[n + 1]
    each = parts[0].shape[0]

    def fill(early, late):
        for d in range(n):
            group = lax.rem(place[0] + d, n) * each
            for h in range(each):
                prior = parts[d][h]
                early[group + h] = prior
                late[group + h] = (prior.astype(F32) + first_ref[group + h].astype(F32)).astype(BF16)

    @pl.when(place[1] == 0)
    def _():
        fill(keep_ref, send_ref)

    @pl.when(place[1] != 0)
    def _():
        fill(send_ref, keep_ref)


def attend(scores_ref, qkv_ref, prior_ref, first, h):
    cols = pl.ds(pl.multiple_of((first + h) * DH, DH), DH)
    left = jnp.concatenate([scores_ref[:, cols], qkv_ref[0, :, cols]], axis=1)
    right = jnp.concatenate([qkv_ref[2, :, cols], prior_ref[h]], axis=0)
    return jnp.dot(left, right, preferred_element_type=F32).astype(BF16)


def attend_body(place, qkv_ref, scores_ref, prior_ref, out_ref, sq_ref):
    half = prior_ref.shape[0]
    total = jnp.zeros(sq_ref.shape, F32)
    for h in range(half):
        value = attend(scores_ref, qkv_ref, prior_ref, place[1] * half, h)
        out_ref[:, pl.ds(h * DH, DH)] = value
        value = value.astype(F32)
        total = total + value * value
    sq_ref[...] = total


def finish_body(
    place, qkv_ref, scores_ref, prior_ref, kept_ref, sq_ref, gain_ref, out_ref, other, done, sems
):
    half = prior_ref.shape[0]
    mine, others = place[1] * half, (1 - place[1]) * half
    total = sq_ref[...]
    for h in range(half):
        value = attend(scores_ref, qkv_ref, prior_ref, others, h)
        other[:, pl.ds(h * DH, DH)] = value
        value = value.astype(F32)
        total = total + value * value
    meansq = jnp.sum(total, axis=-1, keepdims=True) / out_ref.shape[1]
    scale = jnp.broadcast_to(lax.rsqrt(meansq + 1e-06), total.shape)
    each = half // (sems.shape[0] // 2)
    copies = []
    for source, first in ((kept_ref, mine), (other, others)):
        for start in range(0, half, each):
            slot = len(copies)
            for h in range(start, start + each):
                cols = pl.ds(h * DH, DH)
                gain = gain_ref[:, pl.ds(pl.multiple_of((first + h) * DH, DH), DH)]
                value = source[:, cols].astype(F32)
                done[slot, :, pl.ds((h - start) * DH, DH)] = (value * scale * gain).astype(BF16)
            wide = each * DH
            cols = pl.ds(pl.multiple_of((first + start) * DH, wide), wide)
            copy = pltpu.make_async_copy(done.at[slot], out_ref.at[:, cols], sems.at[slot])
            copy.start()
            copies.append(copy)
    for copy in copies:
        copy.wait()


def per_device(nx, nctx, qkv, gain):
    rows, _, width = qkv.shape
    heads = width // DH
    half = heads // 2
    each = half // nx
    block = each * DH
    tp = lax.axis_index("tp")
    place = jnp.stack([tp // 2, lax.rem(tp, 2)]).astype(jnp.int32)
    qkv = jnp.transpose(qkv, (1, 0, 2))
    swap = [(i, i ^ 1) for i in range(2 * nx)]

    def shift(d):
        return [(2 * x + c, 2 * ((x + d) % nx) + c) for x in range(nx) for c in range(2)]

    def states(n, dtype=BF16):
        return jax.ShapeDtypeStruct((n, DH, DH), dtype)

    def call(body, in_specs, out_specs, out_shape, flops, nbytes, scratch=(), limit=16):
        return pl.pallas_call(
            body,
            in_specs=in_specs,
            out_specs=out_specs,
            out_shape=out_shape,
            scratch_shapes=scratch,
            cost_estimate=pl.CostEstimate(flops=flops, bytes_accessed=nbytes, transcendentals=0),
            compiler_params=pltpu.CompilerParams(vmem_limit_bytes=limit * 2**20),
        )

    product = 2 * half * rows * DH * DH
    mib = 2**20
    send = call(
        send_states_body,
        [SMEM, HBM],
        VMEM,
        states(half),
        product,
        3 * mib,
        scratch=[
            pltpu.VMEM((nx, rows, block), BF16),
            pltpu.VMEM((nx, rows, block), BF16),
            pltpu.SemaphoreType.DMA((2, nx)),
        ],
    )(place, pltpu.with_memory_space_constraint(qkv, pltpu.HBM))
    got = lax.ppermute(send, "tp", swap)
    own = call(own_states_body, [SMEM, VMEM], VMEM, states(half, F32), product, 4 * mib)(place, qkv)
    chips = call(
        chip_states_body, [SMEM, VMEM, VMEM], [VMEM] * nx, [states(each)] * nx, 0, 4 * mib
    )(place, own, got)
    later, *chips = lax.optimization_barrier((place, *chips))
    chips = [chips[0]] + [lax.ppermute(chips[d], "tp", shift(d)) for d in range(1, nx)]
    scores, first = call(
        scores_body,
        [SMEM, VMEM, VMEM, VMEM],
        [VMEM, VMEM],
        [jax.ShapeDtypeStruct((rows, width), BF16), states(half)],
        2 * product,
        10 * mib,
    )(later, qkv, own, got)
    scores, first, *chips = lax.optimization_barrier((scores, first, *chips))

    total = sum(c.astype(F32) for c in chips).astype(BF16)
    piece = each * DH // nctx
    spread = lax.all_to_all(
        total.reshape(nctx, piece, DH), "ctx", split_axis=0, concat_axis=0, tiled=True
    )
    spread = call(
        running_sum_body, [VMEM], VMEM, jax.ShapeDtypeStruct(spread.shape, BF16), 0, mib
    )(spread)
    base = lax.all_to_all(spread, "ctx", split_axis=0, concat_axis=0, tiled=True)
    base = base.reshape(each, DH, DH)

    parts = call(
        chip_priors_body,
        [SMEM] + [VMEM] * (nx + 1),
        [VMEM] * nx,
        [states(each)] * nx,
        0,
        3 * mib,
    )(place, base, *chips)
    parts = [parts[0]] + [lax.ppermute(parts[d], "tp", shift(-d)) for d in range(1, nx)]
    keep, give = call(
        core_priors_body,
        [SMEM] + [VMEM] * (nx + 1),
        [VMEM, VMEM],
        [states(half)] * 2,
        0,
        4 * mib,
    )(place, first, *parts)
    other = lax.ppermute(give, "tp", swap)

    kept, sq = call(
        attend_body,
        [SMEM] + [VMEM] * 3,
        [VMEM, VMEM],
        [jax.ShapeDtypeStruct((rows, width // 2), BF16), jax.ShapeDtypeStruct((rows, DH), F32)],
        2 * product,
        5 * mib,
    )(place, qkv, scores, keep)
    return call(
        finish_body,
        [SMEM] + [VMEM] * 6,
        HBM,
        jax.ShapeDtypeStruct((rows, width), BF16),
        2 * product,
        7 * mib,
        scratch=[
            pltpu.VMEM((rows, width // 2), BF16),
            pltpu.VMEM((2 * nx, rows, block), BF16),
            pltpu.SemaphoreType.DMA((2 * nx,)),
        ],
    )(place, qkv, scores, other, kept, sq, gain.reshape(1, width))


def solution(mesh):
    return jax.shard_map(
        functools.partial(per_device, mesh.shape["tp"] // 2, mesh.shape["ctx"]),
        mesh=mesh,
        in_specs=(P(("ctx", "tp"), None, None), P()),
        out_specs=P(("ctx", "tp"), None),
        check_vma=False,
    )
```

time: 332 us -> 86.4 us (0.26)
  the two profiles are of different devices: /device:TPU:248 before, /device:TPU:1 now
where the time goes in v2:
time: 86.4 us; the launch traced here: 86.3 us
  blocking collectives  35.2 us (41%)
  waiting for transfers between devices  23.6 us (27%)
  Pallas kernels  14.3 us (17%)
  starting transfers between devices  12.7 us (15%)
    all_to_all x1, blocking collectives, per_device(): lax.all_to_all(total.reshape(nctx, piece, DH), 'ctx', split_axis=0, conca...  19.6 us
    all_to_all x1, blocking collectives, per_device(): lax.all_to_all(spread, 'ctx', split_axis=0, concat_axis=0, tiled=True)  15.6 us
    ppermute x3, waiting for transfers between devices, per_device(): lax.ppermute(parts[d], 'tp', shift(-d))  12.6 us
    ppermute x3, waiting for transfers between devices, per_device(): lax.ppermute(chips[d], 'tp', shift(d))  9.37 us
    ppermute x3, starting transfers between devices, per_device(): lax.ppermute(parts[d], 'tp', shift(-d))  3.69 us
    pallas_call x1, Pallas kernels, per_device(): call(finish_body, [SMEM] + [VMEM] * 6, HBM, jax.ShapeDtypeStruct((rows, w...  3.44 us
    ppermute x1, starting transfers between devices, per_device(): got = lax.ppermute(send, 'tp', swap)  3.32 us
    ppermute x3, starting transfers between devices, per_device(): lax.ppermute(chips[d], 'tp', shift(d))  3.15 us
  transfers between devices with their start and end apart: 8, of which 7 were waited for; matrix products, arithmetic and copies ran while one was open for 0% of the time, Pallas kernels for 6%

profile of v2, /device:TPU:1, one launch (start us, length us, event | category | flops | bytes accessed | tf_op | source)
XLA Modules:
  0.0 86.3 jit_solution(10184228361874442660)
XLA Ops:
  0.1 2.9 %shard_map.29 = bf16[32,128,128]{2,1,0:T(8,128)(2,1)S(1)} custom-call(s32[2]{0:T(128)S(1)} %pad_add_fusion.place, bf16[3,128,8192]{2,1,0:T(8,128)(2,1)} %bitcast.6), custom_call_target="tpu_custom_call" | custom-call | flops 134217728 | bytes 3145728 | tf_op jit(solution)/shard_map/pallas_call | solution.py:217
  3.0 3.3 %collective-permute-start = (bf16[32,128,128]{2,1,0:T(8,128)(2,1)S(1)}, bf16[32,128,128]{2,1,0:T(8,128)(2,1)S(1)}, u32[]{:S(2)}, u32[]{:S(2)}) collective-permute-start(bf16[32,128,128]{2,1,0:T(8,128)(2,1)S(1)} %shard_map.29), channel_id=1, source_target_pairs={{0,1},{1,0},{2,3},{3,2},{4,5},{5,4},{6,7},{7,6},{8,9},{9,8},{10,11... | collective-permute-start | bytes 3145736 | tf_op jit(solution)/shard_map/ppermute | solution.py:230
  6.4 1.4 %shard_map.28.own_ref = f32[32,128,128]{2,1,0:T(8,128)S(1)} custom-call(s32[2]{0:T(128)S(1)} %pad_add_fusion.place, bf16[3,128,8192]{2,1,0:T(8,128)(2,1)S(1)} %bitcast.7), custom_call_target="tpu_custom_call" | custom-call | flops 134217728 | bytes 4194304 | tf_op jit(solution)/shard_map/pallas_call | solution.py:231
  7.7 0.9 %collective-permute-done.got_ref = bf16[32,128,128]{2,1,0:T(8,128)(2,1)S(1)} collective-permute-done((bf16[32,128,128]{2,1,0:T(8,128)(2,1)S(1)}, bf16[32,128,128]{2,1,0:T(8,128)(2,1)S(1)}, u32[]{:S(2)}, u32[]{:S(2)}) %collective-permute-start) | collective-permute-done | bytes 1048608 | tf_op jit(solution)/shard_map/ppermute | solution.py:230
  8.6 0.7 shard_map.30
  9.5 1.9 %collective-permute-start.2 = (bf16[8,128,128]{2,1,0:T(8,128)(2,1)S(1)}, bf16[8,128,128]{2,1,0:T(8,128)(2,1)S(1)}, u32[]{:S(2)}, u32[]{:S(2)}) collective-permute-start(bf16[8,128,128]{2,1,0:T(8,128)(2,1)S(1)} %get-tuple-element.39), channel_id=1, source_target_pairs={{0,4},{1,5},{2,6},{3,7},{4,0},{5,1},{6,2},{7,3},{8,12},{9,13},{10,... | collective-permute-start | bytes 786440 | tf_op jit(solution)/shard_map/ppermute | solution.py:236
  11.4 1.2 %collective-permute-start.3 = (bf16[8,128,128]{2,1,0:T(8,128)(2,1)S(1)}, bf16[8,128,128]{2,1,0:T(8,128)(2,1)S(1)}, u32[]{:S(2)}, u32[]{:S(2)}) collective-permute-start(bf16[8,128,128]{2,1,0:T(8,128)(2,1)S(1)} %get-tuple-element.40), channel_id=1, source_target_pairs={{0,6},{1,7},{2,0},{3,1},{4,2},{5,3},{6,4},{7,5},{8,14},{9,15},{10,... | collective-permute-start | bytes 786440 | tf_op jit(solution)/shard_map/ppermute | solution.py:236
  12.5 2.2 %shard_map.31 = (bf16[128,8192]{1,0:T(8,128)(2,1)S(1)}, bf16[32,128,128]{2,1,0:T(8,128)(2,1)S(1)}) custom-call(s32[2]{0:T(128)S(1)} %pad_add_fusion.place, bf16[3,128,8192]{2,1,0:T(8,128)(2,1)S(1)} %bitcast.8, f32[32,128,128]{2,1,0:T(8,128)S(1)} %shard_map.28.own_ref, bf16[32,128,128]{2,1,0:T(8,128)(2,1)S(1)} %collective-permute-done.got_ref), custom_call_target="tpu_custom_call" | custom-call | flops 268435456 | bytes 10485760 | tf_op jit(solution)/shard_map/pallas_call | solution.py:237
  14.7 4.2 %collective-permute-done.1.refs_1_ = bf16[8,128,128]{2,1,0:T(8,128)(2,1)S(1)} collective-permute-done((bf16[8,128,128]{2,1,0:T(8,128)(2,1)S(1)}, bf16[8,128,128]{2,1,0:T(8,128)(2,1)S(1)}, u32[]{:S(2)}, u32[]{:S(2)}) %collective-permute-start.1) | collective-permute-done | bytes 262176 | tf_op jit(solution)/shard_map/ppermute | solution.py:236
  18.9 4.2 %collective-permute-done.2.refs_2_ = bf16[8,128,128]{2,1,0:T(8,128)(2,1)S(1)} collective-permute-done((bf16[8,128,128]{2,1,0:T(8,128)(2,1)S(1)}, bf16[8,128,128]{2,1,0:T(8,128)(2,1)S(1)}, u32[]{:S(2)}, u32[]{:S(2)}) %collective-permute-start.2) | collective-permute-done | bytes 262176 | tf_op jit(solution)/shard_map/ppermute | solution.py:236
  23.1 1.0 %collective-permute-done.3.refs_3_ = bf16[8,128,128]{2,1,0:T(8,128)(2,1)S(1)} collective-permute-done((bf16[8,128,128]{2,1,0:T(8,128)(2,1)S(1)}, bf16[8,128,128]{2,1,0:T(8,128)(2,1)S(1)}, u32[]{:S(2)}, u32[]{:S(2)}) %collective-permute-start.3) | collective-permute-done | bytes 262176 | tf_op jit(solution)/shard_map/ppermute | solution.py:236
  24.1 0.1 add_convert_fusion
  24.2 19.6 %all_to_all.10.x_ref = bf16[32,32,128]{2,1,0:T(8,128)(2,1)S(1)} all-to-all(bf16[32,32,128]{2,1,0:T(8,128)(2,1)S(1)} %bitcast.13), channel_id=1, replica_groups=mesh['ctx'=32,'tp'=8] {'ctx'}, dimensions={0} | all-to-all | bytes 524288 | tf_op jit(solution)/shard_map/all_to_all | solution.py:249
  43.9 15.6 %all_to_all.11 = bf16[32,32,128]{2,1,0:T(8,128)(2,1)S(1)} all-to-all(bf16[32,32,128]{2,1,0:T(8,128)(2,1)S(1)} %shard_map.32), channel_id=1, replica_groups=mesh['ctx'=32,'tp'=8] {'ctx'}, dimensions={0} | all-to-all | bytes 524288 | tf_op jit(solution)/shard_map/all_to_all | solution.py:255
  59.5 1.1 %shard_map.33 = (bf16[8,128,128]{2,1,0:T(8,128)(2,1)S(1)}, bf16[8,128,128]{2,1,0:T(8,128)(2,1)S(1)}, bf16[8,128,128]{2,1,0:T(8,128)(2,1)S(1)}, bf16[8,128,128]{2,1,0:T(8,128)(2,1)S(1)}) custom-call(s32[2]{0:T(128)S(1)} %pad_add_fusion.place, bf16[8,128,128]{2,1,0:T(8,128)(2,1)S(1)} %bitcast.11, bf16[8,128,128]{2,1,0:T(8,128)(2,1)S(1)} %get-tuple-element.43.refs_0_, ...), custom_call_target="tpu_custom_call" | custom-call | bytes 3145728 | tf_op jit(solution)/shard_map/pallas_call | solution.py:258
  60.6 3.0 %collective-permute-start.4 = (bf16[8,128,128]{2,1,0:T(8,128)(2,1)S(1)}, bf16[8,128,128]{2,1,0:T(8,128)(2,1)S(1)}, u32[]{:S(2)}, u32[]{:S(2)}) collective-permute-start(bf16[8,128,128]{2,1,0:T(8,128)(2,1)S(1)} %get-tuple-element.48), channel_id=1, source_target_pairs={{0,6},{1,7},{2,0},{3,1},{4,2},{5,3},{6,4},{7,5},{8,14},{9,15},{10,... | collective-permute-start | bytes 786440 | tf_op jit(solution)/shard_map/ppermute | solution.py:266
  63.6 0.7 collective-permute-start.6
  64.3 6.1 %collective-permute-done.4.refs_1_ = bf16[8,128,128]{2,1,0:T(8,128)(2,1)S(1)} collective-permute-done((bf16[8,128,128]{2,1,0:T(8,128)(2,1)S(1)}, bf16[8,128,128]{2,1,0:T(8,128)(2,1)S(1)}, u32[]{:S(2)}, u32[]{:S(2)}) %collective-permute-start.4) | collective-permute-done | bytes 262176 | tf_op jit(solution)/shard_map/ppermute | solution.py:266
  70.5 6.5 %collective-permute-done.6.refs_3_ = bf16[8,128,128]{2,1,0:T(8,128)(2,1)S(1)} collective-permute-done((bf16[8,128,128]{2,1,0:T(8,128)(2,1)S(1)}, bf16[8,128,128]{2,1,0:T(8,128)(2,1)S(1)}, u32[]{:S(2)}, u32[]{:S(2)}) %collective-permute-start.6) | collective-permute-done | bytes 262176 | tf_op jit(solution)/shard_map/ppermute | solution.py:266
  76.9 0.9 %shard_map.34 = (bf16[32,128,128]{2,1,0:T(8,128)(2,1)S(1)}, bf16[32,128,128]{2,1,0:T(8,128)(2,1)S(1)}) custom-call(s32[2]{0:T(128)S(1)} %pad_add_fusion.place, bf16[32,128,128]{2,1,0:T(8,128)(2,1)S(1)} %get-tuple-element.42.first_ref, bf16[8,128,128]{2,1,0:T(8,128)(2,1)S(1)} %get-tuple-element.47.refs_0_, ...), custom_call_target="tpu_custom_call" | custom-call | bytes 4194304 | tf_op jit(solution)/shard_map/pallas_call | solution.py:267
  77.9 2.5 %collective-permute-start.7 = (bf16[32,128,128]{2,1,0:T(8,128)(2,1)S(1)}, bf16[32,128,128]{2,1,0:T(8,128)(2,1)S(1)}, u32[]{:S(2)}, u32[]{:S(2)}) collective-permute-start(bf16[32,128,128]{2,1,0:T(8,128)(2,1)S(1)} %get-tuple-element.51), channel_id=1, source_target_pairs={{0,1},{1,0},{2,3},{3,2},{4,5},{5,4},{6,7},{7,6},{8,9},{9,8},{10,11... | collective-permute-start | bytes 3145736 | tf_op jit(solution)/shard_map/ppermute | solution.py:275
  80.4 1.6 %shard_map.35 = (bf16[128,4096]{1,0:T(8,128)(2,1)S(1)}, f32[128,128]{1,0:T(8,128)S(1)}) custom-call(s32[2]{0:T(128)S(1)} %pad_add_fusion.place, bf16[3,128,8192]{2,1,0:T(8,128)(2,1)S(1)} %bitcast.9, bf16[128,8192]{1,0:T(8,128)(2,1)S(1)} %get-tuple-element.41.scores_ref, bf16[32,128,128]{2,1,0:T(8,128)(2,1)S(1)} %get-tuple-element.52.prior_ref), custom_call_target="tpu_custom_call" | custom-call | flops 268435456 | bytes 5242880 | tf_op jit(solution)/shard_map/pallas_call | solution.py:277
  82.0 0.7 collective-permute-done.7.prior_ref
  82.7 3.4 %shard_map.36 = bf16[128,8192]{1,0:T(8,128)(2,1)} custom-call(s32[2]{0:T(128)S(1)} %pad_add_fusion.place, bf16[3,128,8192]{2,1,0:T(8,128)(2,1)S(1)} %bitcast.10, bf16[128,8192]{1,0:T(8,128)(2,1)S(1)} %get-tuple-element.41.scores_ref, bf16[32,128,128]{2,1,0:T(8,128)(2,1)S(1)} %collective-permute-done.7.prior_ref, ...), custom_call_target="tpu_custom_call" | custom-call | flops 268435456 | bytes 7340032 | tf_op jit(solution)/shard_map/pallas_call | solution.py:285
  (9 shorter events, 0.2 us)
Async XLA Ops:
  0.1 6.3 %copy-start = (bf16[128,3,8192]{2,0,1:T(8,128)(2,1)S(1)}, bf16[128,3,8192]{2,0,1:T(8,128)(2,1)}, u32[]{:S(2)}) copy-start(bf16[128,3,8192]{2,0,1:T(8,128)(2,1)} %param.2) | copy-start | bytes 18874372
  3.0 5.6 %collective-permute-start = (bf16[32,128,128]{2,1,0:T(8,128)(2,1)S(1)}, bf16[32,128,128]{2,1,0:T(8,128)(2,1)S(1)}, u32[]{:S(2)}, u32[]{:S(2)}) collective-permute-start(bf16[32,128,128]{2,1,0:T(8,128)(2,1)S(1)} %shard_map.29), channel_id=1, source_target_pairs={{0,1},{1,0},{2,3},{3,2},{4,5},{5,4},{6,7},{7,6},{8,9},{9,8},{10,11... | collective-permute-start | bytes 3145736 | tf_op jit(solution)/shard_map/ppermute | solution.py:230
  9.4 9.5 %collective-permute-start.1 = (bf16[8,128,128]{2,1,0:T(8,128)(2,1)S(1)}, bf16[8,128,128]{2,1,0:T(8,128)(2,1)S(1)}, u32[]{:S(2)}, u32[]{:S(2)}) collective-permute-start(bf16[8,128,128]{2,1,0:T(8,128)(2,1)S(1)} %get-tuple-element.38), channel_id=1, source_target_pairs={{0,2},{1,3},{2,4},{3,5},{4,6},{5,7},{6,0},{7,1},{8,10},{9,11},{10,... | collective-permute-start | bytes 786440 | tf_op jit(solution)/shard_map/ppermute | solution.py:236
  9.5 13.6 %collective-permute-start.2 = (bf16[8,128,128]{2,1,0:T(8,128)(2,1)S(1)}, bf16[8,128,128]{2,1,0:T(8,128)(2,1)S(1)}, u32[]{:S(2)}, u32[]{:S(2)}) collective-permute-start(bf16[8,128,128]{2,1,0:T(8,128)(2,1)S(1)} %get-tuple-element.39), channel_id=1, source_target_pairs={{0,4},{1,5},{2,6},{3,7},{4,0},{5,1},{6,2},{7,3},{8,12},{9,13},{10,... | collective-permute-start | bytes 786440 | tf_op jit(solution)/shard_map/ppermute | solution.py:236
  11.4 12.7 %collective-permute-start.3 = (bf16[8,128,128]{2,1,0:T(8,128)(2,1)S(1)}, bf16[8,128,128]{2,1,0:T(8,128)(2,1)S(1)}, u32[]{:S(2)}, u32[]{:S(2)}) collective-permute-start(bf16[8,128,128]{2,1,0:T(8,128)(2,1)S(1)} %get-tuple-element.40), channel_id=1, source_target_pairs={{0,6},{1,7},{2,0},{3,1},{4,2},{5,3},{6,4},{7,5},{8,14},{9,15},{10,... | collective-permute-start | bytes 786440 | tf_op jit(solution)/shard_map/ppermute | solution.py:236
  60.6 9.8 %collective-permute-start.4 = (bf16[8,128,128]{2,1,0:T(8,128)(2,1)S(1)}, bf16[8,128,128]{2,1,0:T(8,128)(2,1)S(1)}, u32[]{:S(2)}, u32[]{:S(2)}) collective-permute-start(bf16[8,128,128]{2,1,0:T(8,128)(2,1)S(1)} %get-tuple-element.48), channel_id=1, source_target_pairs={{0,6},{1,7},{2,0},{3,1},{4,2},{5,3},{6,4},{7,5},{8,14},{9,15},{10,... | collective-permute-start | bytes 786440 | tf_op jit(solution)/shard_map/ppermute | solution.py:266
  63.6 6.8 %collective-permute-start.5 = (bf16[8,128,128]{2,1,0:T(8,128)(2,1)S(1)}, bf16[8,128,128]{2,1,0:T(8,128)(2,1)S(1)}, u32[]{:S(2)}, u32[]{:S(2)}) collective-permute-start(bf16[8,128,128]{2,1,0:T(8,128)(2,1)S(1)} %get-tuple-element.49), channel_id=1, source_target_pairs={{0,4},{1,5},{2,6},{3,7},{4,0},{5,1},{6,2},{7,3},{8,12},{9,13},{10,... | collective-permute-start | bytes 786440 | tf_op jit(solution)/shard_map/ppermute | solution.py:266
  63.6 13.3 %collective-permute-start.6 = (bf16[8,128,128]{2,1,0:T(8,128)(2,1)S(1)}, bf16[8,128,128]{2,1,0:T(8,128)(2,1)S(1)}, u32[]{:S(2)}, u32[]{:S(2)}) collective-permute-start(bf16[8,128,128]{2,1,0:T(8,128)(2,1)S(1)} %get-tuple-element.50), channel_id=1, source_target_pairs={{0,2},{1,3},{2,4},{3,5},{4,6},{5,7},{6,0},{7,1},{8,10},{9,11},{10,... | collective-permute-start | bytes 786440 | tf_op jit(solution)/shard_map/ppermute | solution.py:266
  77.9 4.8 %collective-permute-start.7 = (bf16[32,128,128]{2,1,0:T(8,128)(2,1)S(1)}, bf16[32,128,128]{2,1,0:T(8,128)(2,1)S(1)}, u32[]{:S(2)}, u32[]{:S(2)}) collective-permute-start(bf16[32,128,128]{2,1,0:T(8,128)(2,1)S(1)} %get-tuple-element.51), channel_id=1, source_target_pairs={{0,1},{1,0},{2,3},{3,2},{4,5},{5,4},{6,7},{7,6},{8,9},{9,8},{10,11... | collective-permute-start | bytes 3145736 | tf_op jit(solution)/shard_map/ppermute | solution.py:275
  80.4 2.3 %copy-start.1 = (f32[8192]{0:T(1024)S(1)}, f32[8192]{0:T(1024)}, u32[]{:S(2)}) copy-start(f32[8192]{0:T(1024)} %param.3) | copy-start | bytes 98308

commit v3 on v0

v3 whole, which is shorter than its diff:
```python
import functools

import jax
import jax.numpy as jnp
from jax import lax
from jax.experimental import pallas as pl
from jax.experimental.pallas import tpu as pltpu
from jax.sharding import PartitionSpec as P

DH = 128
F32 = jnp.float32
BF16 = jnp.bfloat16
VMEM = pl.BlockSpec(memory_space=pltpu.VMEM)
HBM = pl.BlockSpec(memory_space=pltpu.HBM)


ORDER = (2, 1, 3, 0)


def my_place():
    tp = lax.axis_index("tp")
    return tp // 2, lax.rem(tp, 2)


def group_of(place, d, n):
    return lax.rem(place[0] + d, n)


def columns(start, size):
    return pl.ds(pl.multiple_of(start, size), size)


def head_cols(h):
    return pl.ds(h * DH, DH)


def head_state(k_ref, v_ref, h):
    cols = head_cols(h)
    return lax.dot_general(
        k_ref[:, cols], v_ref[:, cols], (((0,), (0,)), ((), ())), preferred_element_type=F32
    )


def start_loads(qkv_ref, which, place, side, buf, sems):
    block = buf.shape[1] // len(ORDER)
    copies = []
    for i, d in enumerate(ORDER):
        start = (side * len(ORDER) + group_of(place, d, len(ORDER))) * block
        copy = pltpu.make_async_copy(
            qkv_ref.at[which, :, columns(start, block)],
            buf.at[:, pl.ds(i * block, block)],
            sems.at[i],
        )
        copy.start()
        copies.append(copy)
    return copies


def start_pairs(place, qkv_ref, side, k_ref, v_ref, sems):
    loads = [
        start_loads(qkv_ref, 1 + i, place, side, buf, sems.at[i])
        for i, buf in enumerate((k_ref, v_ref))
    ]
    return list(zip(*loads))


def first_body(qkv_ref, send_ref, k_ref, v_ref, own_k_ref, own_v_ref, sems):
    place = my_place()
    pairs = start_pairs(place, qkv_ref, 1 - place[1], k_ref, v_ref, sems.at[0])
    later = start_pairs(place, qkv_ref, place[1], own_k_ref, own_v_ref, sems.at[1])
    each = send_ref.shape[0] // len(pairs)
    for i, pair in enumerate(pairs):
        for copy in pair:
            copy.wait()
        for h in range(i * each, (i + 1) * each):
            send_ref[h] = head_state(k_ref, v_ref, h).astype(BF16)
    for pair in later:
        for copy in pair:
            copy.wait()


def own_body(k_ref, v_ref, own_ref, low_ref):
    for h in range(own_ref.shape[0]):
        state = head_state(k_ref, v_ref, h)
        own_ref[h] = state
        low_ref[h] = state.astype(BF16)


def chip_body(own_ref, got_ref, *chip_refs):
    each = chip_refs[0].shape[0]
    for i, chip_ref in enumerate(chip_refs):
        for h in range(each):
            at = i * each + h
            chip_ref[h] = (own_ref[at] + got_ref[at].astype(F32)).astype(BF16)


def inside_body(qkv_ref, *refs):
    place = my_place()
    kv_refs = refs[:4]
    got_ref, gain_ref, inside_ref, q_ref, order_ref, scores_ref, sems = refs[4:]
    rows, width = kv_refs[0].shape
    loads = [
        start_loads(qkv_ref, 0, place, side, q_ref.at[i], sems.at[i])
        for i, side in enumerate((place[1], 1 - place[1]))
    ]
    allowed = lax.broadcasted_iota(jnp.int32, (rows, rows), 1) <= lax.broadcasted_iota(
        jnp.int32, (rows, rows), 0
    )
    each = width // DH // len(ORDER)
    for side in range(2):
        for i in range(len(ORDER)):
            loads[side][i].wait()
            for h in range(i * each, (i + 1) * each):
                cols = head_cols(h)
                scores = lax.dot_general(
                    q_ref[side, :, cols],
                    kv_refs[2 * side][:, cols],
                    (((1,), (1,)), ((), ())),
                    preferred_element_type=F32,
                )
                scores_ref[side, :, cols] = jnp.where(allowed, scores, 0.0).astype(BF16)
    for i, side in enumerate((place[1], 1 - place[1])):
        block = each * DH
        for j, d in enumerate(ORDER):
            start = (side * len(ORDER) + group_of(place, d, len(ORDER))) * block
            order_ref[i, :, pl.ds(j * block, block)] = gain_ref[:, columns(start, block)]

    def plain(side):
        for h in range(width // DH):
            cols = head_cols(h)
            inside_ref[side, :, cols] = jnp.dot(
                scores_ref[side, :, cols],
                kv_refs[2 * side + 1][:, cols],
                preferred_element_type=F32,
            )

    plain(1)

    @pl.when(place[1] == 0)
    def _():
        plain(0)

    @pl.when(place[1] != 0)
    def _():
        for h in range(width // DH):
            cols = head_cols(h)
            inside_ref[0, :, cols] = jnp.dot(
                jnp.concatenate([scores_ref[0, :, cols], q_ref[0, :, cols]], axis=1),
                jnp.concatenate([kv_refs[1][:, cols], got_ref[h]], axis=0),
                preferred_element_type=F32,
            )


def running_sum_body(x_ref, out_ref):
    acc = jnp.zeros(x_ref.shape[1:], F32)
    for i in range(x_ref.shape[0]):
        out_ref[i] = acc.astype(BF16)
        acc = acc + x_ref[i].astype(F32)


def chip_priors_body(base_ref, *refs):
    place = my_place()
    n = len(refs) // 2
    chips, outs = refs[:n], refs[n:]
    for x in range(n):

        @pl.when(place[0] == x)
        def _():
            for h in range(base_ref.shape[0]):
                acc = base_ref[h].astype(F32)
                for chip in range(n):
                    i = ORDER.index((x - chip) % n)
                    outs[i][h] = acc.astype(BF16)
                    if chip < n - 1:
                        acc = acc + chips[i][h].astype(F32)


def give_body(first, prior_ref, low_ref, out_ref):
    place = my_place()

    @pl.when(place[1] == 0)
    def _():
        for h in range(out_ref.shape[0]):
            state = low_ref[first + h].astype(F32)
            out_ref[h] = (prior_ref[h].astype(F32) + state).astype(BF16)

    @pl.when(place[1] != 0)
    def _():
        out_ref[...] = prior_ref[...]


def attend(side, q_ref, inside_ref, gain_ref, priors, out_ref, total):
    each = priors[0].shape[0]
    for i, prior in enumerate(priors):
        for h in range(each):
            cols = head_cols(i * each + h)
            value = jnp.dot(q_ref[side, :, cols], prior[h], preferred_element_type=F32)
            value = (inside_ref[side, :, cols] + value).astype(BF16).astype(F32)
            out_ref[:, cols] = value * gain_ref[side, :, cols]
            total = total + value * value
    return total


def attend_body(q_ref, inside_ref, gain_ref, *refs):
    priors, out_ref, sq_ref = refs[:-2], refs[-2], refs[-1]
    zero = jnp.zeros(sq_ref.shape, F32)
    sq_ref[...] = attend(0, q_ref, inside_ref, gain_ref, priors, out_ref, zero)


def finish_body(q_ref, inside_ref, gain_ref, kept_ref, sq_ref, *refs):
    place = my_place()
    priors, (out_ref, other, done, sems) = refs[:-4], refs[-4:]
    n, each = len(priors), priors[0].shape[0]
    total = attend(1, q_ref, inside_ref, gain_ref, priors, other, sq_ref[...])
    meansq = jnp.sum(total, axis=-1, keepdims=True) / out_ref.shape[1]
    scale = jnp.broadcast_to(lax.rsqrt(meansq + 1e-06), total.shape)
    copies = []
    for source, side in ((kept_ref, place[1]), (other, 1 - place[1])):
        for i, d in enumerate(ORDER):
            slot = len(copies)
            for h in range(each):
                value = source[:, head_cols(i * each + h)]
                done[slot, :, head_cols(h)] = (value * scale).astype(BF16)
            first = (side * n + group_of(place, d, n)) * each
            copy = pltpu.make_async_copy(
                done.at[slot], out_ref.at[:, columns(first * DH, each * DH)], sems.at[slot]
            )
            copy.start()
            copies.append(copy)
    for copy in copies:
        copy.wait()


def per_device(nx, nctx, qkv, gain):
    rows, _, width = qkv.shape
    heads = width // DH
    half = heads // 2
    each = half // nx
    block = each * DH
    gain = gain.reshape(1, width)
    qkv = pltpu.with_memory_space_constraint(jnp.transpose(qkv, (1, 0, 2)), pltpu.HBM)
    swap = [(i, i ^ 1) for i in range(2 * nx)]

    def shift(d):
        return [(2 * x + c, 2 * ((x + d) % nx) + c) for x in range(nx) for c in range(2)]

    def states(n, dtype=BF16):
        return jax.ShapeDtypeStruct((n, DH, DH), dtype)

    def call(body, in_specs, out_specs, out_shape, products, nbytes, scratch=()):
        return pl.pallas_call(
            body,
            in_specs=in_specs,
            out_specs=out_specs,
            out_shape=out_shape,
            scratch_shapes=scratch,
            cost_estimate=pl.CostEstimate(
                flops=2 * products * rows * DH * DH, bytes_accessed=nbytes, transcendentals=0
            ),
            compiler_params=pltpu.CompilerParams(vmem_limit_bytes=16 * 2**20),
        )

    mib = 2**20
    matrix = jax.ShapeDtypeStruct((rows, width // 2), BF16)
    loads = pltpu.SemaphoreType.DMA((2, nx))
    send, keys, value_rows, own_keys, own_values = call(
        first_body,
        [HBM],
        [VMEM] * 5,
        [states(half)] + [matrix] * 4,
        half,
        5 * mib,
        scratch=[pltpu.SemaphoreType.DMA((2, 2, nx))],
    )(qkv)
    got = lax.ppermute(send, "tp", swap)
    own, low = call(
        own_body, [VMEM] * 2, [VMEM] * 2, [states(half, F32), states(half)], half, 5 * mib
    )(own_keys, own_values)
    chips = call(chip_body, [VMEM, VMEM], [VMEM] * nx, [states(each)] * nx, 0, 4 * mib)(own, got)
    chips = list(chips)
    gain, chips[-1] = lax.optimization_barrier((gain, chips[-1]))
    chips = [
        c if d == 0 else lax.ppermute(c, "tp", shift(d)) for d, c in zip(ORDER, chips)
    ]
    wide = (2, rows, width // 2)
    inside, queries, gains = call(
        inside_body,
        [HBM] + [VMEM] * 6,
        [VMEM] * 3,
        [
            jax.ShapeDtypeStruct(wide, F32),
            jax.ShapeDtypeStruct(wide, BF16),
            jax.ShapeDtypeStruct((2, 1, width // 2), F32),
        ],
        4 * half,
        12 * mib,
        scratch=[pltpu.VMEM(wide, BF16), loads],
    )(qkv, own_keys, own_values, keys, value_rows, got, gain)
    inside, queries, gains, *chips = lax.optimization_barrier((inside, queries, gains, *chips))

    total = sum(c.astype(F32) for c in chips).astype(BF16)
    piece = each * DH // nctx
    spread = lax.all_to_all(
        total.reshape(nctx, piece, DH), "ctx", split_axis=0, concat_axis=0, tiled=True
    )
    spread = call(
        running_sum_body, [VMEM], VMEM, jax.ShapeDtypeStruct(spread.shape, BF16), 0, mib
    )(spread)
    base = lax.all_to_all(spread, "ctx", split_axis=0, concat_axis=0, tiled=True)
    base = base.reshape(each, DH, DH)

    parts = call(
        chip_priors_body,
        [VMEM] * (nx + 1),
        [VMEM] * nx,
        [states(each)] * nx,
        0,
        2 * mib,
    )(base, *chips)
    parts = [
        p if d == 0 else lax.ppermute(p, "tp", shift(-d)) for d, p in zip(ORDER, parts)
    ]
    others = []
    for i, part in enumerate(parts):
        give = call(
            functools.partial(give_body, i * each),
            [VMEM, VMEM],
            VMEM,
            states(each),
            0,
            mib,
        )(part, low)
        others.append(lax.ppermute(give, "tp", swap))
    kept, sq = call(
        attend_body,
        [VMEM] * (3 + nx),
        [VMEM, VMEM],
        [jax.ShapeDtypeStruct((rows, width // 2), F32), jax.ShapeDtypeStruct((rows, DH), F32)],
        half,
        5 * mib,
    )(queries, inside, gains, *parts)
    return call(
        finish_body,
        [VMEM] * (5 + nx),
        HBM,
        jax.ShapeDtypeStruct((rows, width), BF16),
        half,
        7 * mib,
        scratch=[
            pltpu.VMEM((rows, width // 2), F32),
            pltpu.VMEM((2 * nx, rows, block), BF16),
            pltpu.SemaphoreType.DMA((2 * nx,)),
        ],
    )(queries, inside, gains, kept, sq, *others)


def solution(mesh):
    return jax.shard_map(
        functools.partial(per_device, mesh.shape["tp"] // 2, mesh.shape["ctx"]),
        mesh=mesh,
        in_specs=(P(("ctx", "tp"), None, None), P()),
        out_specs=P(("ctx", "tp"), None),
        check_vma=False,
    )
```

time: 332 us -> 79.4 us (0.24)
  the two profiles are of different devices: /device:TPU:248 before, /device:TPU:1 now
where the time goes in v3:
time: 79.4 us; the launch traced here: 79.2 us
  blocking collectives  34.7 us (44%)
  starting transfers between devices  23.6 us (30%)
  Pallas kernels  10.7 us (13%)
  waiting for transfers between devices  9.76 us (12%)
    all_to_all x1, blocking collectives, per_device(): lax.all_to_all(total.reshape(nctx, piece, DH), 'ctx', split_axis=0, conca...  18.9 us
    all_to_all x1, blocking collectives, per_device(): lax.all_to_all(spread, 'ctx', split_axis=0, concat_axis=0, tiled=True)  15.8 us
    ppermute x4, starting transfers between devices, per_device(): others.append(lax.ppermute(give, 'tp', swap))  12.8 us
    ppermute x3, waiting for transfers between devices, per_device(): lax.ppermute(c, 'tp', shift(d))  7.16 us
    pallas_call x1, Pallas kernels, per_device(): call(inside_body, [HBM] + [VMEM] * 6, [VMEM] * 3, [jax.ShapeDtypeStruct(w...  4.5 us
    ppermute x3, starting transfers between devices, per_device(): lax.ppermute(c, 'tp', shift(d))  3.77 us
    ppermute x3, starting transfers between devices, per_device(): lax.ppermute(p, 'tp', shift(-d))  3.69 us
    ppermute x1, starting transfers between devices, per_device(): got = lax.ppermute(send, 'tp', swap)  3.32 us
  transfers between devices with their start and end apart: 11, of which 5 were waited for; matrix products, arithmetic and copies ran while one was open for 0% of the time, Pallas kernels for 7%

profile of v3, /device:TPU:1, one launch (start us, length us, event | category | flops | bytes accessed | tf_op | source)
XLA Modules:
  0.0 79.2 jit_solution(9872991382778602870)
XLA Ops:
  0.0 2.5 %shard_map.28 = (bf16[32,128,128]{2,1,0:T(8,128)(2,1)S(1)}, bf16[128,4096]{1,0:T(8,128)(2,1)S(1)}, bf16[128,4096]{1,0:T(8,128)(2,1)S(1)}, bf16[128,4096]{1,0:T(8,128)(2,1)S(1)}, bf16[128,4096]{1,0:T(8,128)(2,1)S(1)}) custom-call(bf16[3,128,8192]{2,1,0:T(8,128)(2,1)} %bitcast.6), custom_call_target="tpu_custom_call" | custom-call | flops 134217728 | bytes 5242880 | tf_op jit(solution)/shard_map/pallas_call | solution.py:266
  2.5 3.3 %collective-permute-start = (bf16[32,128,128]{2,1,0:T(8,128)(2,1)S(1)}, bf16[32,128,128]{2,1,0:T(8,128)(2,1)S(1)}, u32[]{:S(2)}, u32[]{:S(2)}) collective-permute-start(bf16[32,128,128]{2,1,0:T(8,128)(2,1)S(1)} %get-tuple-element.38), channel_id=1, source_target_pairs={{0,1},{1,0},{2,3},{3,2},{4,5},{5,4},{6,7},{7,6},{8,9},{9,8},{10,11... | collective-permute-start | bytes 3145736 | tf_op jit(solution)/shard_map/ppermute | solution.py:275
  5.8 0.5 shard_map.29
  6.3 1.8 %collective-permute-done.got_ref.refs_4_ = bf16[32,128,128]{2,1,0:T(8,128)(2,1)S(1)} collective-permute-done((bf16[32,128,128]{2,1,0:T(8,128)(2,1)S(1)}, bf16[32,128,128]{2,1,0:T(8,128)(2,1)S(1)}, u32[]{:S(2)}, u32[]{:S(2)}) %collective-permute-start) | collective-permute-done | bytes 1048608 | tf_op jit(solution)/shard_map/ppermute | solution.py:275
  8.1 0.2 shard_map.30
  8.3 1.1 %collective-permute-start.1 = (bf16[8,128,128]{2,1,0:T(8,128)(2,1)S(1)}, bf16[8,128,128]{2,1,0:T(8,128)(2,1)S(1)}, u32[]{:S(2)}, u32[]{:S(2)}) collective-permute-start(bf16[8,128,128]{2,1,0:T(8,128)(2,1)S(1)} %get-tuple-element.45), channel_id=1, source_target_pairs={{0,4},{1,5},{2,6},{3,7},{4,0},{5,1},{6,2},{7,3},{8,12},{9,13},{10,... | collective-permute-start | bytes 786440 | tf_op jit(solution)/shard_map/ppermute | solution.py:283
  9.4 0.3 collective-permute-start.2
  9.7 2.4 %collective-permute-start.3 = (bf16[8,128,128]{2,1,0:T(8,128)(2,1)S(1)}, bf16[8,128,128]{2,1,0:T(8,128)(2,1)S(1)}, u32[]{:S(2)}, u32[]{:S(2)}) collective-permute-start(bf16[8,128,128]{2,1,0:T(8,128)(2,1)S(1)} %get-tuple-element.47), channel_id=1, source_target_pairs={{0,6},{1,7},{2,0},{3,1},{4,2},{5,3},{6,4},{7,5},{8,14},{9,15},{10,... | collective-permute-start | bytes 786440 | tf_op jit(solution)/shard_map/ppermute | solution.py:283
  12.1 4.5 %shard_map.31 = (f32[2,128,4096]{2,1,0:T(8,128)S(1)}, bf16[2,128,4096]{2,1,0:T(8,128)(2,1)S(1)}, f32[2,1,4096]{2,1,0:T(1,128)S(1)}) custom-call(bf16[3,128,8192]{2,1,0:T(8,128)(2,1)} %bitcast.7, bf16[128,4096]{1,0:T(8,128)(2,1)S(1)} %get-tuple-element.34.k_ref.refs_0_, bf16[128,4096]{1,0:T(8,128)(2,1)S(1)} %get-tuple-element.35.v_ref.refs_1_, ...), custom_call_target="tpu_custom_call" | custom-call | flops 536870912 | bytes 12582912 | tf_op jit(solution)/shard_map/pallas_call | solution.py:286
  16.6 0.9 %collective-permute-done.1.refs_0_ = bf16[8,128,128]{2,1,0:T(8,128)(2,1)S(1)} collective-permute-done((bf16[8,128,128]{2,1,0:T(8,128)(2,1)S(1)}, bf16[8,128,128]{2,1,0:T(8,128)(2,1)S(1)}, u32[]{:S(2)}, u32[]{:S(2)}) %collective-permute-start.1) | collective-permute-done | bytes 262176 | tf_op jit(solution)/shard_map/ppermute | solution.py:283
  17.4 6.3 %collective-permute-done.2.refs_1_ = bf16[8,128,128]{2,1,0:T(8,128)(2,1)S(1)} collective-permute-done((bf16[8,128,128]{2,1,0:T(8,128)(2,1)S(1)}, bf16[8,128,128]{2,1,0:T(8,128)(2,1)S(1)}, u32[]{:S(2)}, u32[]{:S(2)}) %collective-permute-start.2) | collective-permute-done | bytes 262176 | tf_op jit(solution)/shard_map/ppermute | solution.py:283
  23.9 18.9 %all_to_all.10.x_ref = bf16[32,32,128]{2,1,0:T(8,128)(2,1)S(1)} all-to-all(bf16[32,32,128]{2,1,0:T(8,128)(2,1)S(1)} %bitcast.8), channel_id=1, replica_groups=mesh['ctx'=32,'tp'=8] {'ctx'}, dimensions={0} | all-to-all | bytes 524288 | tf_op jit(solution)/shard_map/all_to_all | solution.py:303
  42.9 15.8 %all_to_all.11 = bf16[32,32,128]{2,1,0:T(8,128)(2,1)S(1)} all-to-all(bf16[32,32,128]{2,1,0:T(8,128)(2,1)S(1)} %shard_map.32), channel_id=1, replica_groups=mesh['ctx'=32,'tp'=8] {'ctx'}, dimensions={0} | all-to-all | bytes 524288 | tf_op jit(solution)/shard_map/all_to_all | solution.py:309
  58.6 0.2 shard_map.33
  58.8 1.1 %collective-permute-start.4 = (bf16[8,128,128]{2,1,0:T(8,128)(2,1)S(1)}, bf16[8,128,128]{2,1,0:T(8,128)(2,1)S(1)}, u32[]{:S(2)}, u32[]{:S(2)}) collective-permute-start(bf16[8,128,128]{2,1,0:T(8,128)(2,1)S(1)} %get-tuple-element.56), channel_id=1, source_target_pairs={{0,4},{1,5},{2,6},{3,7},{4,0},{5,1},{6,2},{7,3},{8,12},{9,13},{10,... | collective-permute-start | bytes 786440 | tf_op jit(solution)/shard_map/ppermute | solution.py:321
  59.9 2.6 %collective-permute-start.5 = (bf16[8,128,128]{2,1,0:T(8,128)(2,1)S(1)}, bf16[8,128,128]{2,1,0:T(8,128)(2,1)S(1)}, u32[]{:S(2)}, u32[]{:S(2)}) collective-permute-start(bf16[8,128,128]{2,1,0:T(8,128)(2,1)S(1)} %get-tuple-element.57), channel_id=1, source_target_pairs={{0,6},{1,7},{2,0},{3,1},{4,2},{5,3},{6,4},{7,5},{8,14},{9,15},{10,... | collective-permute-start | bytes 786440 | tf_op jit(solution)/shard_map/ppermute | solution.py:321
  62.5 4.3 %collective-permute-start.10 = (bf16[8,128,128]{2,1,0:T(8,128)(2,1)S(1)}, bf16[8,128,128]{2,1,0:T(8,128)(2,1)S(1)}, u32[]{:S(2)}, u32[]{:S(2)}) collective-permute-start(bf16[8,128,128]{2,1,0:T(8,128)(2,1)S(1)} %shard_map.38), channel_id=1, source_target_pairs={{0,1},{1,0},{2,3},{3,2},{4,5},{5,4},{6,7},{7,6},{8,9},{9,8},{10,11... | collective-permute-start | bytes 786440 | tf_op jit(solution)/shard_map/ppermute | solution.py:333
  66.9 5.3 %collective-permute-start.7 = (bf16[8,128,128]{2,1,0:T(8,128)(2,1)S(1)}, bf16[8,128,128]{2,1,0:T(8,128)(2,1)S(1)}, u32[]{:S(2)}, u32[]{:S(2)}) collective-permute-start(bf16[8,128,128]{2,1,0:T(8,128)(2,1)S(1)} %shard_map.35), channel_id=1, source_target_pairs={{0,1},{1,0},{2,3},{3,2},{4,5},{5,4},{6,7},{7,6},{8,9},{9,8},{10,11... | collective-permute-start | bytes 786440 | tf_op jit(solution)/shard_map/ppermute | solution.py:333
  72.2 2.9 %collective-permute-start.8 = (bf16[8,128,128]{2,1,0:T(8,128)(2,1)S(1)}, bf16[8,128,128]{2,1,0:T(8,128)(2,1)S(1)}, u32[]{:S(2)}, u32[]{:S(2)}) collective-permute-start(bf16[8,128,128]{2,1,0:T(8,128)(2,1)S(1)} %shard_map.36), channel_id=1, source_target_pairs={{0,1},{1,0},{2,3},{3,2},{4,5},{5,4},{6,7},{7,6},{8,9},{9,8},{10,11... | collective-permute-start | bytes 786440 | tf_op jit(solution)/shard_map/ppermute | solution.py:333
  75.2 0.3 collective-permute-start.9
  75.4 0.5 shard_map.34
  76.0 0.3 collective-permute-done.8.refs_1_
  76.3 0.5 collective-permute-done.9.refs_2_
  76.8 2.3 %shard_map.39 = bf16[128,8192]{1,0:T(8,128)(2,1)} custom-call(bf16[2,128,4096]{2,1,0:T(8,128)(2,1)S(1)} %get-tuple-element.49.q_ref, f32[2,128,4096]{2,1,0:T(8,128)S(1)} %get-tuple-element.50.inside_ref, f32[2,1,4096]{2,1,0:T(1,128)S(1)} %get-tuple-element.51.gain_ref, f32[128,4096]{1,0:T(8,128)S(1)} %get-tuple-element.60.kept_ref, ...), custom_call_target="tpu_custom_call" | custom-call | flops 134217728 | bytes 7340032 | tf_op jit(solution)/shard_map/pallas_call | solution.py:342
  (15 shorter events, 0.3 us)
Async XLA Ops:
  2.5 5.6 %collective-permute-start = (bf16[32,128,128]{2,1,0:T(8,128)(2,1)S(1)}, bf16[32,128,128]{2,1,0:T(8,128)(2,1)S(1)}, u32[]{:S(2)}, u32[]{:S(2)}) collective-permute-start(bf16[32,128,128]{2,1,0:T(8,128)(2,1)S(1)} %get-tuple-element.38), channel_id=1, source_target_pairs={{0,1},{1,0},{2,3},{3,2},{4,5},{5,4},{6,7},{7,6},{8,9},{9,8},{10,11... | collective-permute-start | bytes 3145736 | tf_op jit(solution)/shard_map/ppermute | solution.py:275
  6.3 5.7 %copy-start = (f32[8192]{0:T(1024)S(1)}, f32[8192]{0:T(1024)}, u32[]{:S(2)}) copy-start(f32[8192]{0:T(1024)} %param.3) | copy-start | bytes 98308
  8.3 9.2 %collective-permute-start.1 = (bf16[8,128,128]{2,1,0:T(8,128)(2,1)S(1)}, bf16[8,128,128]{2,1,0:T(8,128)(2,1)S(1)}, u32[]{:S(2)}, u32[]{:S(2)}) collective-permute-start(bf16[8,128,128]{2,1,0:T(8,128)(2,1)S(1)} %get-tuple-element.45), channel_id=1, source_target_pairs={{0,4},{1,5},{2,6},{3,7},{4,0},{5,1},{6,2},{7,3},{8,12},{9,13},{10,... | collective-permute-start | bytes 786440 | tf_op jit(solution)/shard_map/ppermute | solution.py:283
  9.4 14.3 %collective-permute-start.2 = (bf16[8,128,128]{2,1,0:T(8,128)(2,1)S(1)}, bf16[8,128,128]{2,1,0:T(8,128)(2,1)S(1)}, u32[]{:S(2)}, u32[]{:S(2)}) collective-permute-start(bf16[8,128,128]{2,1,0:T(8,128)(2,1)S(1)} %get-tuple-element.46), channel_id=1, source_target_pairs={{0,2},{1,3},{2,4},{3,5},{4,6},{5,7},{6,0},{7,1},{8,10},{9,11},{10,... | collective-permute-start | bytes 786440 | tf_op jit(solution)/shard_map/ppermute | solution.py:283
  9.7 14.0 %collective-permute-start.3 = (bf16[8,128,128]{2,1,0:T(8,128)(2,1)S(1)}, bf16[8,128,128]{2,1,0:T(8,128)(2,1)S(1)}, u32[]{:S(2)}, u32[]{:S(2)}) collective-permute-start(bf16[8,128,128]{2,1,0:T(8,128)(2,1)S(1)} %get-tuple-element.47), channel_id=1, source_target_pairs={{0,6},{1,7},{2,0},{3,1},{4,2},{5,3},{6,4},{7,5},{8,14},{9,15},{10,... | collective-permute-start | bytes 786440 | tf_op jit(solution)/shard_map/ppermute | solution.py:283
  58.8 8.0 %collective-permute-start.4 = (bf16[8,128,128]{2,1,0:T(8,128)(2,1)S(1)}, bf16[8,128,128]{2,1,0:T(8,128)(2,1)S(1)}, u32[]{:S(2)}, u32[]{:S(2)}) collective-permute-start(bf16[8,128,128]{2,1,0:T(8,128)(2,1)S(1)} %get-tuple-element.56), channel_id=1, source_target_pairs={{0,4},{1,5},{2,6},{3,7},{4,0},{5,1},{6,2},{7,3},{8,12},{9,13},{10,... | collective-permute-start | bytes 786440 | tf_op jit(solution)/shard_map/ppermute | solution.py:321
  59.9 12.3 %collective-permute-start.5 = (bf16[8,128,128]{2,1,0:T(8,128)(2,1)S(1)}, bf16[8,128,128]{2,1,0:T(8,128)(2,1)S(1)}, u32[]{:S(2)}, u32[]{:S(2)}) collective-permute-start(bf16[8,128,128]{2,1,0:T(8,128)(2,1)S(1)} %get-tuple-element.57), channel_id=1, source_target_pairs={{0,6},{1,7},{2,0},{3,1},{4,2},{5,3},{6,4},{7,5},{8,14},{9,15},{10,... | collective-permute-start | bytes 786440 | tf_op jit(solution)/shard_map/ppermute | solution.py:321
  62.5 12.6 %collective-permute-start.6 = (bf16[8,128,128]{2,1,0:T(8,128)(2,1)S(1)}, bf16[8,128,128]{2,1,0:T(8,128)(2,1)S(1)}, u32[]{:S(2)}, u32[]{:S(2)}) collective-permute-start(bf16[8,128,128]{2,1,0:T(8,128)(2,1)S(1)} %get-tuple-element.58), channel_id=1, source_target_pairs={{0,2},{1,3},{2,4},{3,5},{4,6},{5,7},{6,0},{7,1},{8,10},{9,11},{10,... | collective-permute-start | bytes 786440 | tf_op jit(solution)/shard_map/ppermute | solution.py:321
  62.5 13.4 %collective-permute-start.10 = (bf16[8,128,128]{2,1,0:T(8,128)(2,1)S(1)}, bf16[8,128,128]{2,1,0:T(8,128)(2,1)S(1)}, u32[]{:S(2)}, u32[]{:S(2)}) collective-permute-start(bf16[8,128,128]{2,1,0:T(8,128)(2,1)S(1)} %shard_map.38), channel_id=1, source_target_pairs={{0,1},{1,0},{2,3},{3,2},{4,5},{5,4},{6,7},{7,6},{8,9},{9,8},{10,11... | collective-permute-start | bytes 786440 | tf_op jit(solution)/shard_map/ppermute | solution.py:333
  66.9 9.1 %collective-permute-start.7 = (bf16[8,128,128]{2,1,0:T(8,128)(2,1)S(1)}, bf16[8,128,128]{2,1,0:T(8,128)(2,1)S(1)}, u32[]{:S(2)}, u32[]{:S(2)}) collective-permute-start(bf16[8,128,128]{2,1,0:T(8,128)(2,1)S(1)} %shard_map.35), channel_id=1, source_target_pairs={{0,1},{1,0},{2,3},{3,2},{4,5},{5,4},{6,7},{7,6},{8,9},{9,8},{10,11... | collective-permute-start | bytes 786440 | tf_op jit(solution)/shard_map/ppermute | solution.py:333
  72.2 4.1 %collective-permute-start.8 = (bf16[8,128,128]{2,1,0:T(8,128)(2,1)S(1)}, bf16[8,128,128]{2,1,0:T(8,128)(2,1)S(1)}, u32[]{:S(2)}, u32[]{:S(2)}) collective-permute-start(bf16[8,128,128]{2,1,0:T(8,128)(2,1)S(1)} %shard_map.36), channel_id=1, source_target_pairs={{0,1},{1,0},{2,3},{3,2},{4,5},{5,4},{6,7},{7,6},{8,9},{9,8},{10,11... | collective-permute-start | bytes 786440 | tf_op jit(solution)/shard_map/ppermute | solution.py:333
  75.2 1.6 %collective-permute-start.9 = (bf16[8,128,128]{2,1,0:T(8,128)(2,1)S(1)}, bf16[8,128,128]{2,1,0:T(8,128)(2,1)S(1)}, u32[]{:S(2)}, u32[]{:S(2)}) collective-permute-start(bf16[8,128,128]{2,1,0:T(8,128)(2,1)S(1)} %shard_map.37), channel_id=1, source_target_pairs={{0,1},{1,0},{2,3},{3,2},{4,5},{5,4},{6,7},{7,6},{8,9},{9,8},{10,11... | collective-permute-start | bytes 786440 | tf_op jit(solution)/shard_map/ppermute | solution.py:333

commit v4 on v3

--- a/solution.py
+++ b/solution.py
@@ -15,11 +15,25 @@
 
 
 ORDER = (2, 1, 3, 0)
+CHUNKS = 1
+NZ = 8
+LINE = NZ // 2
 
 
 def my_place():
     tp = lax.axis_index("tp")
     return tp // 2, lax.rem(tp, 2)
+
+
+def line_place():
+    ctx = lax.axis_index("ctx")
+    z = lax.rem(ctx, NZ)
+    late = z >= LINE
+    return ctx // NZ, late, jnp.where(late, NZ - 1 - z, z)
+
+
+def quarter_of(m, d):
+    return lax.rem(m + d, LINE)
 
 
 def group_of(place, d, n):
@@ -87,10 +101,10 @@
 
 
 def chip_body(own_ref, got_ref, *chip_refs):
-    each = chip_refs[0].shape[0]
+    few = chip_refs[0].shape[0]
     for i, chip_ref in enumerate(chip_refs):
-        for h in range(each):
-            at = i * each + h
+        for h in range(few):
+            at = i * few + h
             chip_ref[h] = (own_ref[at] + got_ref[at].astype(F32)).astype(BF16)
 
 
@@ -151,79 +165,133 @@
             )
 
 
-def running_sum_body(x_ref, out_ref):
-    acc = jnp.zeros(x_ref.shape[1:], F32)
-    for i in range(x_ref.shape[0]):
-        out_ref[i] = acc.astype(BF16)
-        acc = acc + x_ref[i].astype(F32)
-
-
-def chip_priors_body(base_ref, *refs):
+def totals_body(*refs):
+    chips, outs = refs[:-LINE], refs[-LINE:]
+    _, _, m = line_place()
+    few = outs[0].shape[0]
+    for d, out in enumerate(outs):
+        first = quarter_of(m, d) * few
+        for h in range(few):
+            out[h] = sum(c[first + h].astype(F32) for c in chips).astype(BF16)
+
+
+def line_sum_body(*refs):
+    out = refs[-1]
+    few = refs[0].shape[0]
+    for c in range(out.shape[0] // few):
+        terms = refs[c * LINE : (c + 1) * LINE]
+        for h in range(few):
+            out[c * few + h] = sum(t[h].astype(F32) for t in terms).astype(BF16)
+
+
+def line_priors_body(ny, mirror_ref, *refs):
+    y, late, m = line_place()
+    rows, refs = refs[: ny - 1], refs[ny - 1 :]
+    n = len(refs) // 2
+    terms, outs = refs[:n], refs[n:]
+    few = outs[0].shape[0]
+    seen = [jnp.where(y >= d, 1.0, 0.0) for d in range(1, ny)]
+    turn = jnp.where(late, 1.0, 0.0)
+    at = [jnp.where(late, -1, 1) * lax.rem(m - d + LINE, LINE) for d in range(LINE)]
+    weight = [[jnp.where(at[e] < at[d], 1.0, 0.0) for e in range(LINE)] for d in range(LINE)]
+    for c in range(n // LINE):
+        for h in range(few):
+            base = mirror_ref[c * few + h].astype(F32) * turn
+            for r, row in enumerate(rows):
+                base = base + row[c * few + h].astype(F32) * seen[r]
+            values = [t[h].astype(F32) for t in terms[c * LINE : (c + 1) * LINE]]
+            for d in range(LINE):
+                acc = base
+                for e in range(LINE):
+                    if e != d:
+                        acc = acc + values[e] * weight[d][e]
+                outs[c * LINE + d][h] = acc.astype(BF16)
+
+
+def chip_priors_body(*refs):
     place = my_place()
+    _, _, m = line_place()
+    bases, refs = refs[:LINE], refs[LINE:]
     n = len(refs) // 2
     chips, outs = refs[:n], refs[n:]
+    few = bases[0].shape[0]
     for x in range(n):
 
         @pl.when(place[0] == x)
         def _():
-            for h in range(base_ref.shape[0]):
-                acc = base_ref[h].astype(F32)
-                for chip in range(n):
-                    i = ORDER.index((x - chip) % n)
-                    outs[i][h] = acc.astype(BF16)
-                    if chip < n - 1:
-                        acc = acc + chips[i][h].astype(F32)
-
-
-def give_body(first, prior_ref, low_ref, out_ref):
+            for d in range(LINE):
+                first = quarter_of(m, d) * few
+                for h in range(few):
+                    acc = bases[d][h].astype(F32)
+                    for chip in range(n):
+                        i = ORDER.index((x - chip) % n)
+                        outs[i][first + h] = acc.astype(BF16)
+                        if chip < n - 1:
+                            acc = acc + chips[i][first + h].astype(F32)
+
+
+def give_body(starts, *refs):
     place = my_place()
+    priors, low_ref, out_ref = refs[:-2], refs[-2], refs[-1]
+    few = priors[0].shape[0]
 
     @pl.when(place[1] == 0)
     def _():
-        for h in range(out_ref.shape[0]):
-            state = low_ref[first + h].astype(F32)
-            out_ref[h] = (prior_ref[h].astype(F32) + state).astype(BF16)
+        for i, (prior_ref, start) in enumerate(zip(priors, starts)):
+            for h in range(few):
+                state = low_ref[start + h].astype(F32)
+                out_ref[i * few + h] = (prior_ref[h].astype(F32) + state).astype(BF16)
 
     @pl.when(place[1] != 0)
     def _():
-        out_ref[...] = prior_ref[...]
-
-
-def attend(side, q_ref, inside_ref, gain_ref, priors, out_ref, total):
-    each = priors[0].shape[0]
-    for i, prior in enumerate(priors):
-        for h in range(each):
-            cols = head_cols(i * each + h)
-            value = jnp.dot(q_ref[side, :, cols], prior[h], preferred_element_type=F32)
-            value = (inside_ref[side, :, cols] + value).astype(BF16).astype(F32)
-            out_ref[:, cols] = value * gain_ref[side, :, cols]
-            total = total + value * value
+        for i, prior_ref in enumerate(priors):
+            out_ref[i * few : (i + 1) * few] = prior_ref[...]
+
+
+def attend(side, q_ref, inside_ref, gain_ref, heads, priors, out_ref, total):
+    for at, (head, which, row) in enumerate(heads):
+        cols = head_cols(head)
+        value = jnp.dot(q_ref[side, :, cols], priors[which][row], preferred_element_type=F32)
+        value = (inside_ref[side, :, cols] + value).astype(BF16).astype(F32)
+        out_ref[:, head_cols(at)] = value * gain_ref[side, :, cols]
+        total = total + value * value
     return total
 
 
-def attend_body(q_ref, inside_ref, gain_ref, *refs):
-    priors, out_ref, sq_ref = refs[:-2], refs[-2], refs[-1]
-    zero = jnp.zeros(sq_ref.shape, F32)
-    sq_ref[...] = attend(0, q_ref, inside_ref, gain_ref, priors, out_ref, zero)
-
-
-def finish_body(q_ref, inside_ref, gain_ref, kept_ref, sq_ref, *refs):
+def attend_body(sides, q_ref, inside_ref, gain_ref, *refs):
+    n = len(sides)
+    outs, sq_ref = refs[-1 - n : -1], refs[-1]
+    total = jnp.zeros(sq_ref.shape, F32)
+    for (side, first, count, heads), out_ref in zip(sides, outs):
+        priors = refs[first : first + count]
+        total = attend(side, q_ref, inside_ref, gain_ref, heads, priors, out_ref, total)
+    sq_ref[...] = total
+
+
+def finish_body(heads, sources, few, q_ref, inside_ref, gain_ref, *refs):
     place = my_place()
-    priors, (out_ref, other, done, sems) = refs[:-4], refs[-4:]
-    n, each = len(priors), priors[0].shape[0]
-    total = attend(1, q_ref, inside_ref, gain_ref, priors, other, sq_ref[...])
+    n = len(ORDER)
+    each = q_ref.shape[2] // DH // n
+    out_ref, other, done, sems = refs[-4:]
+    count = len(sources) - 1
+    kept, sqs, priors = refs[:count], refs[count : count + CHUNKS], refs[count + CHUNKS : -4]
+    total = sqs[0][...]
+    for sq_ref in sqs[1:]:
+        total = total + sq_ref[...]
+    total = attend(1, q_ref, inside_ref, gain_ref, heads, priors, other, total)
     meansq = jnp.sum(total, axis=-1, keepdims=True) / out_ref.shape[1]
     scale = jnp.broadcast_to(lax.rsqrt(meansq + 1e-06), total.shape)
     copies = []
-    for source, side in ((kept_ref, place[1]), (other, 1 - place[1])):
+    for (side, chunk), source in zip(sources, (*kept, other)):
         for i, d in enumerate(ORDER):
             slot = len(copies)
-            for h in range(each):
-                value = source[:, head_cols(i * each + h)]
+            for h in range(few):
+                value = source[:, head_cols(i * few + h)]
                 done[slot, :, head_cols(h)] = (value * scale).astype(BF16)
-            first = (side * n + group_of(place, d, n)) * each
+            base = (place[1] if side == 0 else 1 - place[1]) * n
+            first = (base + group_of(place, d, n)) * each + chunk * few
             copy = pltpu.make_async_copy(
-                done.at[slot], out_ref.at[:, columns(first * DH, each * DH)], sems.at[slot]
+                done.at[slot], out_ref.at[:, columns(first * DH, few * DH)], sems.at[slot]
             )
             copy.start()
             copies.append(copy)
@@ -276,82 +344,162 @@
     own, low = call(
         own_body, [VMEM] * 2, [VMEM] * 2, [states(half, F32), states(half)], half, 5 * mib
     )(own_keys, own_values)
-    chips = call(chip_body, [VMEM, VMEM], [VMEM] * nx, [states(each)] * nx, 0, 4 * mib)(own, got)
-    chips = list(chips)
-    gain, chips[-1] = lax.optimization_barrier((gain, chips[-1]))
+    few = each // CHUNKS
+    ny = nctx // NZ
+    made = call(
+        chip_body,
+        [VMEM, VMEM],
+        [VMEM] * (nx * CHUNKS),
+        [states(few)] * (nx * CHUNKS),
+        0,
+        4 * mib,
+    )(own, got)
+    chips = [[made[i * CHUNKS + c] for i in range(nx)] for c in range(CHUNKS)]
+    if CHUNKS == 1:
+        gain, chips[-1][-1] = lax.optimization_barrier((gain, chips[-1][-1]))
     chips = [
-        c if d == 0 else lax.ppermute(c, "tp", shift(d)) for d, c in zip(ORDER, chips)
+        [t if d == 0 else lax.ppermute(t, "tp", shift(d)) for d, t in zip(ORDER, chunk)]
+        for chunk in chips
     ]
     wide = (2, rows, width // 2)
-    inside, queries, gains = call(
-        inside_body,
-        [HBM] + [VMEM] * 6,
-        [VMEM] * 3,
-        [
-            jax.ShapeDtypeStruct(wide, F32),
-            jax.ShapeDtypeStruct(wide, BF16),
-            jax.ShapeDtypeStruct((2, 1, width // 2), F32),
-        ],
-        4 * half,
-        12 * mib,
-        scratch=[pltpu.VMEM(wide, BF16), loads],
-    )(qkv, own_keys, own_values, keys, value_rows, got, gain)
-    inside, queries, gains, *chips = lax.optimization_barrier((inside, queries, gains, *chips))
-
-    total = sum(c.astype(F32) for c in chips).astype(BF16)
-    piece = each * DH // nctx
-    spread = lax.all_to_all(
-        total.reshape(nctx, piece, DH), "ctx", split_axis=0, concat_axis=0, tiled=True
-    )
-    spread = call(
-        running_sum_body, [VMEM], VMEM, jax.ShapeDtypeStruct(spread.shape, BF16), 0, mib
-    )(spread)
-    base = lax.all_to_all(spread, "ctx", split_axis=0, concat_axis=0, tiled=True)
-    base = base.reshape(each, DH, DH)
-
-    parts = call(
-        chip_priors_body,
-        [VMEM] * (nx + 1),
-        [VMEM] * nx,
-        [states(each)] * nx,
+
+    def local(gain):
+        return call(
+            inside_body,
+            [HBM] + [VMEM] * 6,
+            [VMEM] * 3,
+            [
+                jax.ShapeDtypeStruct(wide, F32),
+                jax.ShapeDtypeStruct(wide, BF16),
+                jax.ShapeDtypeStruct((2, 1, width // 2), F32),
+            ],
+            4 * half,
+            12 * mib,
+            scratch=[pltpu.VMEM(wide, BF16), loads],
+        )(qkv, own_keys, own_values, keys, value_rows, got, gain)
+
+    if CHUNKS == 1:
+        inside, queries, gains = local(gain)
+        inside, queries, gains, *chips[0] = lax.optimization_barrier(
+            (inside, queries, gains, *chips[0])
+        )
+
+    def pos(late, m):
+        return NZ - 1 - m if late else m
+
+    def line(d):
+        return [
+            (y * NZ + pos(late, m), y * NZ + pos(late, (m + d) % LINE))
+            for y in range(ny)
+            for late in range(2)
+            for m in range(LINE)
+        ]
+
+    mirror = [(y * NZ + z, y * NZ + NZ - 1 - z) for y in range(ny) for z in range(NZ)]
+
+    def row(d):
+        return [(y * NZ + z, (y + d) % ny * NZ + z) for y in range(ny) for z in range(NZ)]
+
+    small = few // LINE
+    terms = []
+    for chunk in chips:
+        totals = call(
+            totals_body, [VMEM] * nx, [VMEM] * LINE, [states(small)] * LINE, 0, mib
+        )(*chunk)
+        terms += [
+            t if d == 0 else lax.ppermute(t, "ctx", line(d)) for d, t in enumerate(totals)
+        ]
+    held = CHUNKS * small
+    mine = call(line_sum_body, [VMEM] * len(terms), VMEM, states(held), 0, mib)(*terms)
+    facing = lax.ppermute(mine, "ctx", mirror)
+    whole = (mine.astype(F32) + facing.astype(F32)).astype(BF16)
+    rows_before = [lax.ppermute(whole, "ctx", row(d)) for d in range(1, ny)]
+    bases = call(
+        functools.partial(line_priors_body, ny),
+        [VMEM] * (ny + len(terms)),
+        [VMEM] * len(terms),
+        [states(small)] * len(terms),
         0,
-        2 * mib,
-    )(base, *chips)
-    parts = [
-        p if d == 0 else lax.ppermute(p, "tp", shift(-d)) for d, p in zip(ORDER, parts)
+        mib,
+    )(facing, *rows_before, *terms)
+    bases = [
+        b if k % LINE == 0 else lax.ppermute(b, "ctx", line(-(k % LINE)))
+        for k, b in enumerate(bases)
     ]
-    others = []
-    for i, part in enumerate(parts):
-        give = call(
-            functools.partial(give_body, i * each),
-            [VMEM, VMEM],
+    parts = []
+    for c in range(CHUNKS):
+        made = call(
+            chip_priors_body,
+            [VMEM] * (LINE + nx),
+            [VMEM] * nx,
+            [states(few)] * nx,
+            0,
+            2 * mib,
+        )(*bases[c * LINE : (c + 1) * LINE], *chips[c])
+        if CHUNKS > 1 and c == CHUNKS - 1:
+            made = list(made)
+            gain, made[-1] = lax.optimization_barrier((gain, made[-1]))
+            inside, queries, gains = local(gain)
+        parts.append(
+            [p if d == 0 else lax.ppermute(p, "tp", shift(-d)) for d, p in zip(ORDER, made)]
+        )
+
+    def give(c, which):
+        given = call(
+            functools.partial(give_body, [(i * CHUNKS + c) * few for i in which]),
+            [VMEM] * (len(which) + 1),
             VMEM,
-            states(each),
+            states(few * len(which)),
             0,
             mib,
-        )(part, low)
-        others.append(lax.ppermute(give, "tp", swap))
-    kept, sq = call(
-        attend_body,
-        [VMEM] * (3 + nx),
-        [VMEM, VMEM],
-        [jax.ShapeDtypeStruct((rows, width // 2), F32), jax.ShapeDtypeStruct((rows, DH), F32)],
-        half,
-        5 * mib,
-    )(queries, inside, gains, *parts)
+        )(*[parts[c][i] for i in which], low)
+        return lax.ppermute(given, "tp", swap)
+
+    kept, sqs, sources = [], [], []
+    square = jax.ShapeDtypeStruct((rows, DH), F32)
+    for c in range(CHUNKS):
+        last = c == CHUNKS - 1
+        groups = [[i] for i in range(nx)] if last else [list(range(nx))]
+        others = [give(c, g) for g in groups]
+        own_heads = [
+            (i * each + c * few + h, i, h) for i in range(nx) for h in range(few)
+        ]
+        other_heads = [
+            (i * each + c * few + h, g, k * few + h)
+            for g, group in enumerate(groups)
+            for k, i in enumerate(group)
+            for h in range(few)
+        ]
+        sides = [(0, 0, nx, own_heads)]
+        if not last:
+            sides.append((1, nx, len(others), other_heads))
+        sources += [(side[0], c) for side in sides]
+        priors = parts[c] + ([] if last else others)
+        out = jax.ShapeDtypeStruct((rows, nx * few * DH), F32)
+        *outs, sq = call(
+            functools.partial(attend_body, sides),
+            [VMEM] * (3 + len(priors)),
+            [VMEM] * (len(sides) + 1),
+            [out] * len(sides) + [square],
+            half,
+            5 * mib,
+        )(queries, inside, gains, *priors)
+        kept += outs
+        sqs.append(sq)
+    sources.append((1, CHUNKS - 1))
     return call(
-        finish_body,
-        [VMEM] * (5 + nx),
+        functools.partial(finish_body, other_heads, sources, few),
+        [VMEM] * (3 + len(kept) + len(sqs) + len(others)),
         HBM,
         jax.ShapeDtypeStruct((rows, width), BF16),
         half,
         7 * mib,
         scratch=[
-            pltpu.VMEM((rows, width // 2), F32),
-            pltpu.VMEM((2 * nx, rows, block), BF16),
-            pltpu.SemaphoreType.DMA((2 * nx,)),
+            pltpu.VMEM((rows, nx * few * DH), F32),
+            pltpu.VMEM((2 * nx * CHUNKS, rows, few * DH), BF16),
+            pltpu.SemaphoreType.DMA((2 * nx * CHUNKS,)),
         ],
-    )(queries, inside, gains, kept, sq, *others)
+    )(queries, inside, gains, *kept, *sqs, *others)
 
 
 def solution(mesh):

time: 79.4 us -> 76.2 us (0.960)
  blocking collectives: 34.7 us -> 0 us
  starting transfers between devices: 23.6 us -> 40.1 us
  waiting for transfers between devices: 9.76 us -> 24.6 us
    all_to_all x2 -> x0, blocking collectives: 34.7 us -> none  [the longest x1 18.9 us: per_device(): lax.all_to_all(total.reshape(nctx, piece, DH), 'ctx', split_axis=0, conca...]
    ppermute x7 -> x17, starting transfers between devices: 16.6 us -> 33.1 us  [the longest x4 12.9 us: give(): return lax.ppermute(given, 'tp', swap)]
    ppermute x7 -> x17, waiting for transfers between devices: 7.96 us -> 22.8 us  [the longest x3 7.16 us: per_device(): lax.ppermute(t, 'tp', shift(d))]
    pallas_call x10 -> x12, Pallas kernels: 7.76 us -> 8.07 us  [the longest x1 4.5 us: local(): call(inside_body, [HBM] + [VMEM] * 6, [VMEM] * 3, [jax.ShapeDtypeStruct(w...]
  transfers between devices with their start and end apart: 11 -> 21, of which waited for: 5 -> 14; matrix products, arithmetic and copies ran while one was open for 0% -> 0% of each run, Pallas kernels for 7% -> 7%
where the time goes in v4:
time: 76.2 us; the launch traced here: 76.1 us
  starting transfers between devices  40.1 us (53%)
  waiting for transfers between devices  24.6 us (32%)
  Pallas kernels  11 us (14%)
    ppermute x4, starting transfers between devices, give(): return lax.ppermute(given, 'tp', swap)  12.9 us
    ppermute x3, waiting for transfers between devices, per_device(): lax.ppermute(t, 'tp', shift(d))  7.16 us
    ppermute x3, waiting for transfers between devices, per_device(): lax.ppermute(b, 'ctx', line(-(k % LINE)))  5.02 us
    ppermute x1, starting transfers between devices, per_device(): facing = lax.ppermute(mine, 'ctx', mirror)  4.75 us
    pallas_call x1, Pallas kernels, local(): call(inside_body, [HBM] + [VMEM] * 6, [VMEM] * 3, [jax.ShapeDtypeStruct(w...  4.5 us
    ppermute x3, waiting for transfers between devices, per_device(): rows_before = [lax.ppermute(whole, 'ctx', row(d)) for d in range(1, ny)]  4.28 us
    ppermute x3, starting transfers between devices, per_device(): lax.ppermute(b, 'ctx', line(-(k % LINE)))  4.13 us
    ppermute x3, starting transfers between devices, per_device(): rows_before = [lax.ppermute(whole, 'ctx', row(d)) for d in range(1, ny)]  3.85 us
  transfers between devices with their start and end apart: 21, of which 14 were waited for; matrix products, arithmetic and copies ran while one was open for 0% of the time, Pallas kernels for 7%

profile of v4, /device:TPU:1, one launch (start us, length us, event | category | flops | bytes accessed | tf_op | source)
XLA Modules:
  0.0 76.1 jit_solution(16128896932681189281)
XLA Ops:
  0.0 2.5 %shard_map.28 = (bf16[32,128,128]{2,1,0:T(8,128)(2,1)S(1)}, bf16[128,4096]{1,0:T(8,128)(2,1)S(1)}, bf16[128,4096]{1,0:T(8,128)(2,1)S(1)}, bf16[128,4096]{1,0:T(8,128)(2,1)S(1)}, bf16[128,4096]{1,0:T(8,128)(2,1)S(1)}) custom-call(bf16[3,128,8192]{2,1,0:T(8,128)(2,1)} %bitcast.3), custom_call_target="tpu_custom_call" | custom-call | flops 134217728 | bytes 5242880 | tf_op jit(solution)/shard_map/pallas_call | solution.py:334
  2.5 3.3 %collective-permute-start = (bf16[32,128,128]{2,1,0:T(8,128)(2,1)S(1)}, bf16[32,128,128]{2,1,0:T(8,128)(2,1)S(1)}, u32[]{:S(2)}, u32[]{:S(2)}) collective-permute-start(bf16[32,128,128]{2,1,0:T(8,128)(2,1)S(1)} %get-tuple-element.46), channel_id=1, source_target_pairs={{0,1},{1,0},{2,3},{3,2},{4,5},{5,4},{6,7},{7,6},{8,9},{9,8},{10,11... | collective-permute-start | bytes 3145736 | tf_op jit(solution)/shard_map/ppermute | solution.py:343
  6.3 1.8 %collective-permute-done.got_ref.refs_4_ = bf16[32,128,128]{2,1,0:T(8,128)(2,1)S(1)} collective-permute-done((bf16[32,128,128]{2,1,0:T(8,128)(2,1)S(1)}, bf16[32,128,128]{2,1,0:T(8,128)(2,1)S(1)}, u32[]{:S(2)}, u32[]{:S(2)}) %collective-permute-start) | collective-permute-done | bytes 1048608 | tf_op jit(solution)/shard_map/ppermute | solution.py:343
  8.3 1.1 %collective-permute-start.1 = (bf16[8,128,128]{2,1,0:T(8,128)(2,1)S(1)}, bf16[8,128,128]{2,1,0:T(8,128)(2,1)S(1)}, u32[]{:S(2)}, u32[]{:S(2)}) collective-permute-start(bf16[8,128,128]{2,1,0:T(8,128)(2,1)S(1)} %get-tuple-element.53), channel_id=1, source_target_pairs={{0,4},{1,5},{2,6},{3,7},{4,0},{5,1},{6,2},{7,3},{8,12},{9,13},{10,... | collective-permute-start | bytes 786440 | tf_op jit(solution)/shard_map/ppermute | solution.py:361
  9.7 2.4 %collective-permute-start.3 = (bf16[8,128,128]{2,1,0:T(8,128)(2,1)S(1)}, bf16[8,128,128]{2,1,0:T(8,128)(2,1)S(1)}, u32[]{:S(2)}, u32[]{:S(2)}) collective-permute-start(bf16[8,128,128]{2,1,0:T(8,128)(2,1)S(1)} %get-tuple-element.55), channel_id=1, source_target_pairs={{0,6},{1,7},{2,0},{3,1},{4,2},{5,3},{6,4},{7,5},{8,14},{9,15},{10,... | collective-permute-start | bytes 786440 | tf_op jit(solution)/shard_map/ppermute | solution.py:361
  12.1 4.5 %shard_map.31 = (f32[2,128,4096]{2,1,0:T(8,128)S(1)}, bf16[2,128,4096]{2,1,0:T(8,128)(2,1)S(1)}, f32[2,1,4096]{2,1,0:T(1,128)S(1)}) custom-call(bf16[3,128,8192]{2,1,0:T(8,128)(2,1)} %bitcast.4, bf16[128,4096]{1,0:T(8,128)(2,1)S(1)} %get-tuple-element.42.k_ref.refs_0_, bf16[128,4096]{1,0:T(8,128)(2,1)S(1)} %get-tuple-element.43.v_ref.refs_1_, ...), custom_call_target="tpu_custom_call" | custom-call | flops 536870912 | bytes 12582912 | tf_op jit(solution)/shard_map/pallas_call | solution.py:367
  16.6 0.9 %collective-permute-done.1.refs_0_.refs_4_ = bf16[8,128,128]{2,1,0:T(8,128)(2,1)S(1)} collective-permute-done((bf16[8,128,128]{2,1,0:T(8,128)(2,1)S(1)}, bf16[8,128,128]{2,1,0:T(8,128)(2,1)S(1)}, u32[]{:S(2)}, u32[]{:S(2)}) %collective-permute-start.1) | collective-permute-done | bytes 262176 | tf_op jit(solution)/shard_map/ppermute | solution.py:361
  17.4 6.3 %collective-permute-done.2.refs_1_.refs_5_ = bf16[8,128,128]{2,1,0:T(8,128)(2,1)S(1)} collective-permute-done((bf16[8,128,128]{2,1,0:T(8,128)(2,1)S(1)}, bf16[8,128,128]{2,1,0:T(8,128)(2,1)S(1)}, u32[]{:S(2)}, u32[]{:S(2)}) %collective-permute-start.2) | collective-permute-done | bytes 262176 | tf_op jit(solution)/shard_map/ppermute | solution.py:361
  23.9 2.9 %collective-permute-start.5 = (bf16[2,128,128]{2,1,0:T(8,128)(2,1)S(1)}, bf16[2,128,128]{2,1,0:T(8,128)(2,1)S(1)}, u32[]{:S(2)}, u32[]{:S(2)}) collective-permute-start(bf16[2,128,128]{2,1,0:T(8,128)(2,1)S(1)} %get-tuple-element.66), channel_id=1, source_target_pairs={{0,16},{8,24},{16,0},{24,8},{56,40},{48,32},{40,56},{32,48},{64,80... | collective-permute-start | bytes 196616 | tf_op jit(solution)/shard_map/ppermute | solution.py:410
  27.6 1.4 %collective-permute-done.4.refs_1_.refs_4_ = bf16[2,128,128]{2,1,0:T(8,128)(2,1)S(1)} collective-permute-done((bf16[2,128,128]{2,1,0:T(8,128)(2,1)S(1)}, bf16[2,128,128]{2,1,0:T(8,128)(2,1)S(1)}, u32[]{:S(2)}, u32[]{:S(2)}) %collective-permute-start.4) | collective-permute-done | bytes 65568 | tf_op jit(solution)/shard_map/ppermute | solution.py:410
  29.0 2.4 %collective-permute-done.5.refs_2_.refs_5_ = bf16[2,128,128]{2,1,0:T(8,128)(2,1)S(1)} collective-permute-done((bf16[2,128,128]{2,1,0:T(8,128)(2,1)S(1)}, bf16[2,128,128]{2,1,0:T(8,128)(2,1)S(1)}, u32[]{:S(2)}, u32[]{:S(2)}) %collective-permute-start.5) | collective-permute-done | bytes 65568 | tf_op jit(solution)/shard_map/ppermute | solution.py:410
  31.4 4.7 %collective-permute-start.7 = (bf16[2,128,128]{2,1,0:T(8,128)(2,1)S(1)}, bf16[2,128,128]{2,1,0:T(8,128)(2,1)S(1)}, u32[]{:S(2)}, u32[]{:S(2)}) collective-permute-start(bf16[2,128,128]{2,1,0:T(8,128)(2,1)S(1)} %shard_map.33), channel_id=1, source_target_pairs={{0,56},{8,48},{16,40},{24,32},{32,24},{40,16},{48,8},{56,0},{64,12... | collective-permute-start | bytes 196616 | tf_op jit(solution)/shard_map/ppermute | solution.py:414
  36.2 1.7 %collective-permute-done.7.mirror_ref = bf16[2,128,128]{2,1,0:T(8,128)(2,1)S(1)} collective-permute-done((bf16[2,128,128]{2,1,0:T(8,128)(2,1)S(1)}, bf16[2,128,128]{2,1,0:T(8,128)(2,1)S(1)}, u32[]{:S(2)}, u32[]{:S(2)}) %collective-permute-start.7) | collective-permute-done | bytes 65568 | tf_op jit(solution)/shard_map/ppermute | solution.py:414
  37.9 2.8 %collective-permute-start.10 = (bf16[2,128,128]{2,1,0:T(8,128)(2,1)S(1)}, bf16[2,128,128]{2,1,0:T(8,128)(2,1)S(1)}, u32[]{:S(2)}, u32[]{:S(2)}) collective-permute-start(bf16[2,128,128]{2,1,0:T(8,128)(2,1)S(1)} %add_convert_fusion), channel_id=1, source_target_pairs={{0,192},{8,200},{16,208},{24,216},{32,224},{40,232},{48,240},{56,2... | collective-permute-start | bytes 196616 | tf_op jit(solution)/shard_map/ppermute | solution.py:416
  42.0 3.4 %collective-permute-done.9.refs_1_ = bf16[2,128,128]{2,1,0:T(8,128)(2,1)S(1)} collective-permute-done((bf16[2,128,128]{2,1,0:T(8,128)(2,1)S(1)}, bf16[2,128,128]{2,1,0:T(8,128)(2,1)S(1)}, u32[]{:S(2)}, u32[]{:S(2)}) %collective-permute-start.9) | collective-permute-done | bytes 65568 | tf_op jit(solution)/shard_map/ppermute | solution.py:416
  46.2 3.5 %collective-permute-start.11 = (bf16[2,128,128]{2,1,0:T(8,128)(2,1)S(1)}, bf16[2,128,128]{2,1,0:T(8,128)(2,1)S(1)}, u32[]{:S(2)}, u32[]{:S(2)}) collective-permute-start(bf16[2,128,128]{2,1,0:T(8,128)(2,1)S(1)} %get-tuple-element.69), channel_id=1, source_target_pairs={{0,24},{8,0},{16,8},{24,16},{56,32},{48,56},{40,48},{32,40},{64,88... | collective-permute-start | bytes 196616 | tf_op jit(solution)/shard_map/ppermute | solution.py:426
  51.1 2.7 %collective-permute-done.12.refs_2_ = bf16[2,128,128]{2,1,0:T(8,128)(2,1)S(1)} collective-permute-done((bf16[2,128,128]{2,1,0:T(8,128)(2,1)S(1)}, bf16[2,128,128]{2,1,0:T(8,128)(2,1)S(1)}, u32[]{:S(2)}, u32[]{:S(2)}) %collective-permute-start.12) | collective-permute-done | bytes 65568 | tf_op jit(solution)/shard_map/ppermute | solution.py:426
  53.7 1.6 %collective-permute-done.13.refs_3_ = bf16[2,128,128]{2,1,0:T(8,128)(2,1)S(1)} collective-permute-done((bf16[2,128,128]{2,1,0:T(8,128)(2,1)S(1)}, bf16[2,128,128]{2,1,0:T(8,128)(2,1)S(1)}, u32[]{:S(2)}, u32[]{:S(2)}) %collective-permute-start.13) | collective-permute-done | bytes 65568 | tf_op jit(solution)/shard_map/ppermute | solution.py:426
  55.5 1.0 %collective-permute-start.14 = (bf16[8,128,128]{2,1,0:T(8,128)(2,1)S(1)}, bf16[8,128,128]{2,1,0:T(8,128)(2,1)S(1)}, u32[]{:S(2)}, u32[]{:S(2)}) collective-permute-start(bf16[8,128,128]{2,1,0:T(8,128)(2,1)S(1)} %get-tuple-element.72), channel_id=1, source_target_pairs={{0,4},{1,5},{2,6},{3,7},{4,0},{5,1},{6,2},{7,3},{8,12},{9,13},{10,... | collective-permute-start | bytes 786440 | tf_op jit(solution)/shard_map/ppermute | solution.py:444
  56.5 2.7 %collective-permute-start.15 = (bf16[8,128,128]{2,1,0:T(8,128)(2,1)S(1)}, bf16[8,128,128]{2,1,0:T(8,128)(2,1)S(1)}, u32[]{:S(2)}, u32[]{:S(2)}) collective-permute-start(bf16[8,128,128]{2,1,0:T(8,128)(2,1)S(1)} %get-tuple-element.73), channel_id=1, source_target_pairs={{0,6},{1,7},{2,0},{3,1},{4,2},{5,3},{6,4},{7,5},{8,14},{9,15},{10,... | collective-permute-start | bytes 786440 | tf_op jit(solution)/shard_map/ppermute | solution.py:444
  59.2 5.2 %collective-permute-start.20 = (bf16[8,128,128]{2,1,0:T(8,128)(2,1)S(1)}, bf16[8,128,128]{2,1,0:T(8,128)(2,1)S(1)}, u32[]{:S(2)}, u32[]{:S(2)}) collective-permute-start(bf16[8,128,128]{2,1,0:T(8,128)(2,1)S(1)} %shard_map.40), channel_id=1, source_target_pairs={{0,1},{1,0},{2,3},{3,2},{4,5},{5,4},{6,7},{7,6},{8,9},{9,8},{10,11... | collective-permute-start | bytes 786440 | tf_op jit(solution)/shard_map/ppermute | solution.py:456
  64.5 4.4 %collective-permute-start.17 = (bf16[8,128,128]{2,1,0:T(8,128)(2,1)S(1)}, bf16[8,128,128]{2,1,0:T(8,128)(2,1)S(1)}, u32[]{:S(2)}, u32[]{:S(2)}) collective-permute-start(bf16[8,128,128]{2,1,0:T(8,128)(2,1)S(1)} %shard_map.37), channel_id=1, source_target_pairs={{0,1},{1,0},{2,3},{3,2},{4,5},{5,4},{6,7},{7,6},{8,9},{9,8},{10,11... | collective-permute-start | bytes 786440 | tf_op jit(solution)/shard_map/ppermute | solution.py:456
  69.0 3.1 %collective-permute-start.18 = (bf16[8,128,128]{2,1,0:T(8,128)(2,1)S(1)}, bf16[8,128,128]{2,1,0:T(8,128)(2,1)S(1)}, u32[]{:S(2)}, u32[]{:S(2)}) collective-permute-start(bf16[8,128,128]{2,1,0:T(8,128)(2,1)S(1)} %shard_map.38), channel_id=1, source_target_pairs={{0,1},{1,0},{2,3},{3,2},{4,5},{5,4},{6,7},{7,6},{8,9},{9,8},{10,11... | collective-permute-start | bytes 786440 | tf_op jit(solution)/shard_map/ppermute | solution.py:456
  73.7 2.3 %shard_map.41 = bf16[128,8192]{1,0:T(8,128)(2,1)} custom-call(bf16[2,128,4096]{2,1,0:T(8,128)(2,1)S(1)} %get-tuple-element.57.q_ref, f32[2,128,4096]{2,1,0:T(8,128)S(1)} %get-tuple-element.58.inside_ref, f32[2,1,4096]{2,1,0:T(1,128)S(1)} %get-tuple-element.59.gain_ref, f32[128,4096]{1,0:T(8,128)S(1)} %get-tuple-element.76.refs_0_, ...), custom_call_target="tpu_custom_call" | custom-call | flops 134217728 | bytes 7340032 | tf_op jit(solution)/shard_map/pallas_call | solution.py:490
  (35 shorter events, 7.4 us)
Async XLA Ops:
  2.5 5.6 %collective-permute-start = (bf16[32,128,128]{2,1,0:T(8,128)(2,1)S(1)}, bf16[32,128,128]{2,1,0:T(8,128)(2,1)S(1)}, u32[]{:S(2)}, u32[]{:S(2)}) collective-permute-start(bf16[32,128,128]{2,1,0:T(8,128)(2,1)S(1)} %get-tuple-element.46), channel_id=1, source_target_pairs={{0,1},{1,0},{2,3},{3,2},{4,5},{5,4},{6,7},{7,6},{8,9},{9,8},{10,11... | collective-permute-start | bytes 3145736 | tf_op jit(solution)/shard_map/ppermute | solution.py:343
  6.3 5.7 %copy-start = (f32[8192]{0:T(1024)S(1)}, f32[8192]{0:T(1024)}, u32[]{:S(2)}) copy-start(f32[8192]{0:T(1024)} %param.3) | copy-start | bytes 98308
  8.3 9.2 %collective-permute-start.1 = (bf16[8,128,128]{2,1,0:T(8,128)(2,1)S(1)}, bf16[8,128,128]{2,1,0:T(8,128)(2,1)S(1)}, u32[]{:S(2)}, u32[]{:S(2)}) collective-permute-start(bf16[8,128,128]{2,1,0:T(8,128)(2,1)S(1)} %get-tuple-element.53), channel_id=1, source_target_pairs={{0,4},{1,5},{2,6},{3,7},{4,0},{5,1},{6,2},{7,3},{8,12},{9,13},{10,... | collective-permute-start | bytes 786440 | tf_op jit(solution)/shard_map/ppermute | solution.py:361
  9.4 14.3 %collective-permute-start.2 = (bf16[8,128,128]{2,1,0:T(8,128)(2,1)S(1)}, bf16[8,128,128]{2,1,0:T(8,128)(2,1)S(1)}, u32[]{:S(2)}, u32[]{:S(2)}) collective-permute-start(bf16[8,128,128]{2,1,0:T(8,128)(2,1)S(1)} %get-tuple-element.54), channel_id=1, source_target_pairs={{0,2},{1,3},{2,4},{3,5},{4,6},{5,7},{6,0},{7,1},{8,10},{9,11},{10,... | collective-permute-start | bytes 786440 | tf_op jit(solution)/shard_map/ppermute | solution.py:361
  9.7 14.0 %collective-permute-start.3 = (bf16[8,128,128]{2,1,0:T(8,128)(2,1)S(1)}, bf16[8,128,128]{2,1,0:T(8,128)(2,1)S(1)}, u32[]{:S(2)}, u32[]{:S(2)}) collective-permute-start(bf16[8,128,128]{2,1,0:T(8,128)(2,1)S(1)} %get-tuple-element.55), channel_id=1, source_target_pairs={{0,6},{1,7},{2,0},{3,1},{4,2},{5,3},{6,4},{7,5},{8,14},{9,15},{10,... | collective-permute-start | bytes 786440 | tf_op jit(solution)/shard_map/ppermute | solution.py:361
  23.9 5.1 %collective-permute-start.4 = (bf16[2,128,128]{2,1,0:T(8,128)(2,1)S(1)}, bf16[2,128,128]{2,1,0:T(8,128)(2,1)S(1)}, u32[]{:S(2)}, u32[]{:S(2)}) collective-permute-start(bf16[2,128,128]{2,1,0:T(8,128)(2,1)S(1)} %get-tuple-element.65), channel_id=1, source_target_pairs={{0,8},{8,16},{16,24},{24,0},{56,48},{48,40},{40,32},{32,56},{64,72... | collective-permute-start | bytes 196616 | tf_op jit(solution)/shard_map/ppermute | solution.py:410
  23.9 7.4 %collective-permute-start.5 = (bf16[2,128,128]{2,1,0:T(8,128)(2,1)S(1)}, bf16[2,128,128]{2,1,0:T(8,128)(2,1)S(1)}, u32[]{:S(2)}, u32[]{:S(2)}) collective-permute-start(bf16[2,128,128]{2,1,0:T(8,128)(2,1)S(1)} %get-tuple-element.66), channel_id=1, source_target_pairs={{0,16},{8,24},{16,0},{24,8},{56,40},{48,32},{40,56},{32,48},{64,80... | collective-permute-start | bytes 196616 | tf_op jit(solution)/shard_map/ppermute | solution.py:410
  26.8 4.6 %collective-permute-start.6 = (bf16[2,128,128]{2,1,0:T(8,128)(2,1)S(1)}, bf16[2,128,128]{2,1,0:T(8,128)(2,1)S(1)}, u32[]{:S(2)}, u32[]{:S(2)}) collective-permute-start(bf16[2,128,128]{2,1,0:T(8,128)(2,1)S(1)} %get-tuple-element.67), channel_id=1, source_target_pairs={{0,24},{8,0},{16,8},{24,16},{56,32},{48,56},{40,48},{32,40},{64,88... | collective-permute-start | bytes 196616 | tf_op jit(solution)/shard_map/ppermute | solution.py:410
  31.4 6.4 %collective-permute-start.7 = (bf16[2,128,128]{2,1,0:T(8,128)(2,1)S(1)}, bf16[2,128,128]{2,1,0:T(8,128)(2,1)S(1)}, u32[]{:S(2)}, u32[]{:S(2)}) collective-permute-start(bf16[2,128,128]{2,1,0:T(8,128)(2,1)S(1)} %shard_map.33), channel_id=1, source_target_pairs={{0,56},{8,48},{16,40},{24,32},{32,24},{40,16},{48,8},{56,0},{64,12... | collective-permute-start | bytes 196616 | tf_op jit(solution)/shard_map/ppermute | solution.py:414
  37.9 4.1 %collective-permute-start.10 = (bf16[2,128,128]{2,1,0:T(8,128)(2,1)S(1)}, bf16[2,128,128]{2,1,0:T(8,128)(2,1)S(1)}, u32[]{:S(2)}, u32[]{:S(2)}) collective-permute-start(bf16[2,128,128]{2,1,0:T(8,128)(2,1)S(1)} %add_convert_fusion), channel_id=1, source_target_pairs={{0,192},{8,200},{16,208},{24,216},{32,224},{40,232},{48,240},{56,2... | collective-permute-start | bytes 196616 | tf_op jit(solution)/shard_map/ppermute | solution.py:416
  40.7 4.7 %collective-permute-start.9 = (bf16[2,128,128]{2,1,0:T(8,128)(2,1)S(1)}, bf16[2,128,128]{2,1,0:T(8,128)(2,1)S(1)}, u32[]{:S(2)}, u32[]{:S(2)}) collective-permute-start(bf16[2,128,128]{2,1,0:T(8,128)(2,1)S(1)} %add_convert_fusion), channel_id=1, source_target_pairs={{0,128},{8,136},{16,144},{24,152},{32,160},{40,168},{48,176},{56,1... | collective-permute-start | bytes 196616 | tf_op jit(solution)/shard_map/ppermute | solution.py:416
  41.0 5.0 %collective-permute-start.8 = (bf16[2,128,128]{2,1,0:T(8,128)(2,1)S(1)}, bf16[2,128,128]{2,1,0:T(8,128)(2,1)S(1)}, u32[]{:S(2)}, u32[]{:S(2)}) collective-permute-start(bf16[2,128,128]{2,1,0:T(8,128)(2,1)S(1)} %add_convert_fusion), channel_id=1, source_target_pairs={{0,64},{8,72},{16,80},{24,88},{32,96},{40,104},{48,112},{56,120},{... | collective-permute-start | bytes 196616 | tf_op jit(solution)/shard_map/ppermute | solution.py:416
  46.2 4.9 %collective-permute-start.11 = (bf16[2,128,128]{2,1,0:T(8,128)(2,1)S(1)}, bf16[2,128,128]{2,1,0:T(8,128)(2,1)S(1)}, u32[]{:S(2)}, u32[]{:S(2)}) collective-permute-start(bf16[2,128,128]{2,1,0:T(8,128)(2,1)S(1)} %get-tuple-element.69), channel_id=1, source_target_pairs={{0,24},{8,0},{16,8},{24,16},{56,32},{48,56},{40,48},{32,40},{64,88... | collective-permute-start | bytes 196616 | tf_op jit(solution)/shard_map/ppermute | solution.py:426
  49.7 4.0 %collective-permute-start.12 = (bf16[2,128,128]{2,1,0:T(8,128)(2,1)S(1)}, bf16[2,128,128]{2,1,0:T(8,128)(2,1)S(1)}, u32[]{:S(2)}, u32[]{:S(2)}) collective-permute-start(bf16[2,128,128]{2,1,0:T(8,128)(2,1)S(1)} %get-tuple-element.70), channel_id=1, source_target_pairs={{0,16},{8,24},{16,0},{24,8},{56,40},{48,32},{40,56},{32,48},{64,80... | collective-permute-start | bytes 196616 | tf_op jit(solution)/shard_map/ppermute | solution.py:426
  50.3 5.0 %collective-permute-start.13 = (bf16[2,128,128]{2,1,0:T(8,128)(2,1)S(1)}, bf16[2,128,128]{2,1,0:T(8,128)(2,1)S(1)}, u32[]{:S(2)}, u32[]{:S(2)}) collective-permute-start(bf16[2,128,128]{2,1,0:T(8,128)(2,1)S(1)} %get-tuple-element.71), channel_id=1, source_target_pairs={{0,8},{8,16},{16,24},{24,0},{56,48},{48,40},{40,32},{32,56},{64,72... | collective-permute-start | bytes 196616 | tf_op jit(solution)/shard_map/ppermute | solution.py:426
  55.5 8.9 %collective-permute-start.14 = (bf16[8,128,128]{2,1,0:T(8,128)(2,1)S(1)}, bf16[8,128,128]{2,1,0:T(8,128)(2,1)S(1)}, u32[]{:S(2)}, u32[]{:S(2)}) collective-permute-start(bf16[8,128,128]{2,1,0:T(8,128)(2,1)S(1)} %get-tuple-element.72), channel_id=1, source_target_pairs={{0,4},{1,5},{2,6},{3,7},{4,0},{5,1},{6,2},{7,3},{8,12},{9,13},{10,... | collective-permute-start | bytes 786440 | tf_op jit(solution)/shard_map/ppermute | solution.py:444
  56.5 12.4 %collective-permute-start.15 = (bf16[8,128,128]{2,1,0:T(8,128)(2,1)S(1)}, bf16[8,128,128]{2,1,0:T(8,128)(2,1)S(1)}, u32[]{:S(2)}, u32[]{:S(2)}) collective-permute-start(bf16[8,128,128]{2,1,0:T(8,128)(2,1)S(1)} %get-tuple-element.73), channel_id=1, source_target_pairs={{0,6},{1,7},{2,0},{3,1},{4,2},{5,3},{6,4},{7,5},{8,14},{9,15},{10,... | collective-permute-start | bytes 786440 | tf_op jit(solution)/shard_map/ppermute | solution.py:444
  59.2 12.8 %collective-permute-start.16 = (bf16[8,128,128]{2,1,0:T(8,128)(2,1)S(1)}, bf16[8,128,128]{2,1,0:T(8,128)(2,1)S(1)}, u32[]{:S(2)}, u32[]{:S(2)}) collective-permute-start(bf16[8,128,128]{2,1,0:T(8,128)(2,1)S(1)} %get-tuple-element.74), channel_id=1, source_target_pairs={{0,2},{1,3},{2,4},{3,5},{4,6},{5,7},{6,0},{7,1},{8,10},{9,11},{10,... | collective-permute-start | bytes 786440 | tf_op jit(solution)/shard_map/ppermute | solution.py:444
  59.2 13.5 %collective-permute-start.20 = (bf16[8,128,128]{2,1,0:T(8,128)(2,1)S(1)}, bf16[8,128,128]{2,1,0:T(8,128)(2,1)S(1)}, u32[]{:S(2)}, u32[]{:S(2)}) collective-permute-start(bf16[8,128,128]{2,1,0:T(8,128)(2,1)S(1)} %shard_map.40), channel_id=1, source_target_pairs={{0,1},{1,0},{2,3},{3,2},{4,5},{5,4},{6,7},{7,6},{8,9},{9,8},{10,11... | collective-permute-start | bytes 786440 | tf_op jit(solution)/shard_map/ppermute | solution.py:456
  64.5 8.3 %collective-permute-start.17 = (bf16[8,128,128]{2,1,0:T(8,128)(2,1)S(1)}, bf16[8,128,128]{2,1,0:T(8,128)(2,1)S(1)}, u32[]{:S(2)}, u32[]{:S(2)}) collective-permute-start(bf16[8,128,128]{2,1,0:T(8,128)(2,1)S(1)} %shard_map.37), channel_id=1, source_target_pairs={{0,1},{1,0},{2,3},{3,2},{4,5},{5,4},{6,7},{7,6},{8,9},{9,8},{10,11... | collective-permute-start | bytes 786440 | tf_op jit(solution)/shard_map/ppermute | solution.py:456
  69.0 4.3 %collective-permute-start.18 = (bf16[8,128,128]{2,1,0:T(8,128)(2,1)S(1)}, bf16[8,128,128]{2,1,0:T(8,128)(2,1)S(1)}, u32[]{:S(2)}, u32[]{:S(2)}) collective-permute-start(bf16[8,128,128]{2,1,0:T(8,128)(2,1)S(1)} %shard_map.38), channel_id=1, source_target_pairs={{0,1},{1,0},{2,3},{3,2},{4,5},{5,4},{6,7},{7,6},{8,9},{9,8},{10,11... | collective-permute-start | bytes 786440 | tf_op jit(solution)/shard_map/ppermute | solution.py:456
  72.1 1.6 %collective-permute-start.19 = (bf16[8,128,128]{2,1,0:T(8,128)(2,1)S(1)}, bf16[8,128,128]{2,1,0:T(8,128)(2,1)S(1)}, u32[]{:S(2)}, u32[]{:S(2)}) collective-permute-start(bf16[8,128,128]{2,1,0:T(8,128)(2,1)S(1)} %shard_map.39), channel_id=1, source_target_pairs={{0,1},{1,0},{2,3},{3,2},{4,5},{5,4},{6,7},{7,6},{8,9},{9,8},{10,11... | collective-permute-start | bytes 786440 | tf_op jit(solution)/shard_map/ppermute | solution.py:456

commit v5 on v4

--- a/solution.py
+++ b/solution.py
@@ -18,6 +18,7 @@
 CHUNKS = 1
 NZ = 8
 LINE = NZ // 2
+FACING = 6
 
 
 def my_place():
@@ -29,15 +30,15 @@
     ctx = lax.axis_index("ctx")
     z = lax.rem(ctx, NZ)
     late = z >= LINE
-    return ctx // NZ, late, jnp.where(late, NZ - 1 - z, z)
+    return ctx // NZ, late, jnp.where(late, z ^ FACING, z)
 
 
 def quarter_of(m, d):
-    return lax.rem(m + d, LINE)
+    return m ^ d
 
 
 def group_of(place, d, n):
-    return lax.rem(place[0] + d, n)
+    return place[0] ^ d
 
 
 def columns(start, size):
@@ -190,9 +191,10 @@
     n = len(refs) // 2
     terms, outs = refs[:n], refs[n:]
     few = outs[0].shape[0]
-    seen = [jnp.where(y >= d, 1.0, 0.0) for d in range(1, ny)]
+    seen = [jnp.where(y > y ^ d, 1.0, 0.0) for d in range(1, ny)]
     turn = jnp.where(late, 1.0, 0.0)
-    at = [jnp.where(late, -1, 1) * lax.rem(m - d + LINE, LINE) for d in range(LINE)]
+    turned = jnp.where(late, FACING % LINE, 0)
+    at = [m ^ d ^ turned for d in range(LINE)]
     weight = [[jnp.where(at[e] < at[d], 1.0, 0.0) for e in range(LINE)] for d in range(LINE)]
     for c in range(n // LINE):
         for h in range(few):
@@ -224,7 +226,7 @@
                 for h in range(few):
                     acc = bases[d][h].astype(F32)
                     for chip in range(n):
-                        i = ORDER.index((x - chip) % n)
+                        i = ORDER.index(x ^ chip)
                         outs[i][first + h] = acc.astype(BF16)
                         if chip < n - 1:
                             acc = acc + chips[i][first + h].astype(F32)
@@ -310,7 +312,7 @@
     swap = [(i, i ^ 1) for i in range(2 * nx)]
 
     def shift(d):
-        return [(2 * x + c, 2 * ((x + d) % nx) + c) for x in range(nx) for c in range(2)]
+        return [(2 * x + c, 2 * (x ^ d) + c) for x in range(nx) for c in range(2)]
 
     def states(n, dtype=BF16):
         return jax.ShapeDtypeStruct((n, DH, DH), dtype)
@@ -385,20 +387,20 @@
         )
 
     def pos(late, m):
-        return NZ - 1 - m if late else m
+        return m ^ FACING if late else m
 
     def line(d):
         return [
-            (y * NZ + pos(late, m), y * NZ + pos(late, (m + d) % LINE))
+            (y * NZ + pos(late, m), y * NZ + pos(late, m ^ d))
             for y in range(ny)
             for late in range(2)
             for m in range(LINE)
         ]
 
-    mirror = [(y * NZ + z, y * NZ + NZ - 1 - z) for y in range(ny) for z in range(NZ)]
+    mirror = [(y * NZ + z, y * NZ + (z ^ FACING)) for y in range(ny) for z in range(NZ)]
 
     def row(d):
-        return [(y * NZ + z, (y + d) % ny * NZ + z) for y in range(ny) for z in range(NZ)]
+        return [(y * NZ + z, (y ^ d) * NZ + z) for y in range(ny) for z in range(NZ)]
 
     small = few // LINE
     terms = []
@@ -423,7 +425,7 @@
         mib,
     )(facing, *rows_before, *terms)
     bases = [
-        b if k % LINE == 0 else lax.ppermute(b, "ctx", line(-(k % LINE)))
+        b if k % LINE == 0 else lax.ppermute(b, "ctx", line(k % LINE))
         for k, b in enumerate(bases)
     ]
     parts = []
@@ -441,7 +443,7 @@
             gain, made[-1] = lax.optimization_barrier((gain, made[-1]))
             inside, queries, gains = local(gain)
         parts.append(
-            [p if d == 0 else lax.ppermute(p, "tp", shift(-d)) for d, p in zip(ORDER, made)]
+            [p if d == 0 else lax.ppermute(p, "tp", shift(d)) for d, p in zip(ORDER, made)]
         )
 
     def give(c, which):

time: 76.2 us -> 74.1 us (0.972)
  waiting for transfers between devices: 24.6 us -> 23.2 us
    ppermute x6, waiting for transfers between devices: 5.03 us -> 3.28 us  [the longest x3 3.27 us: per_device(): lax.ppermute(b, 'ctx', line(k % LINE))]
  transfers between devices with their start and end apart: 21 -> 21, of which waited for: 14 -> 13; matrix products, arithmetic and copies ran while one was open for 0% -> 0% of each run, Pallas kernels for 7% -> 8%
where the time goes in v5:
time: 74.1 us; the launch traced here: 74 us
  starting transfers between devices  39.4 us (53%)
  waiting for transfers between devices  23.2 us (31%)
  Pallas kernels  11 us (15%)
    ppermute x4, starting transfers between devices, give(): return lax.ppermute(given, 'tp', swap)  13.5 us
    ppermute x3, waiting for transfers between devices, per_device(): lax.ppermute(t, 'tp', shift(d))  7.59 us
    ppermute x1, starting transfers between devices, per_device(): facing = lax.ppermute(mine, 'ctx', mirror)  4.82 us
    pallas_call x1, Pallas kernels, local(): call(inside_body, [HBM] + [VMEM] * 6, [VMEM] * 3, [jax.ShapeDtypeStruct(w...  4.49 us
    ppermute x3, waiting for transfers between devices, per_device(): lax.ppermute(t, 'ctx', line(d))  4.26 us
    ppermute x3, waiting for transfers between devices, per_device(): rows_before = [lax.ppermute(whole, 'ctx', row(d)) for d in range(1, ny)]  3.99 us
    ppermute x3, starting transfers between devices, per_device(): lax.ppermute(p, 'tp', shift(d))  3.73 us
    ppermute x3, starting transfers between devices, per_device(): lax.ppermute(b, 'ctx', line(k % LINE))  3.63 us
  transfers between devices with their start and end apart: 21, of which 13 were waited for; matrix products, arithmetic and copies ran while one was open for 0% of the time, Pallas kernels for 8%

profile of v5, /device:TPU:1, one launch (start us, length us, event | category | flops | bytes accessed | tf_op | source)
XLA Modules:
  0.0 74.0 jit_solution(6686250654509365263)
XLA Ops:
  0.0 2.5 %shard_map.28 = (bf16[32,128,128]{2,1,0:T(8,128)(2,1)S(1)}, bf16[128,4096]{1,0:T(8,128)(2,1)S(1)}, bf16[128,4096]{1,0:T(8,128)(2,1)S(1)}, bf16[128,4096]{1,0:T(8,128)(2,1)S(1)}, bf16[128,4096]{1,0:T(8,128)(2,1)S(1)}) custom-call(bf16[3,128,8192]{2,1,0:T(8,128)(2,1)} %bitcast.3), custom_call_target="tpu_custom_call" | custom-call | flops 134217728 | bytes 5242880 | tf_op jit(solution)/shard_map/pallas_call | solution.py:336
  2.5 3.3 %collective-permute-start = (bf16[32,128,128]{2,1,0:T(8,128)(2,1)S(1)}, bf16[32,128,128]{2,1,0:T(8,128)(2,1)S(1)}, u32[]{:S(2)}, u32[]{:S(2)}) collective-permute-start(bf16[32,128,128]{2,1,0:T(8,128)(2,1)S(1)} %get-tuple-element.46), channel_id=1, source_target_pairs={{0,1},{1,0},{2,3},{3,2},{4,5},{5,4},{6,7},{7,6},{8,9},{9,8},{10,11... | collective-permute-start | bytes 3145736 | tf_op jit(solution)/shard_map/ppermute | solution.py:345
  6.3 1.8 %collective-permute-done.got_ref.refs_4_ = bf16[32,128,128]{2,1,0:T(8,128)(2,1)S(1)} collective-permute-done((bf16[32,128,128]{2,1,0:T(8,128)(2,1)S(1)}, bf16[32,128,128]{2,1,0:T(8,128)(2,1)S(1)}, u32[]{:S(2)}, u32[]{:S(2)}) %collective-permute-start) | collective-permute-done | bytes 1048608 | tf_op jit(solution)/shard_map/ppermute | solution.py:345
  8.3 1.1 %collective-permute-start.1 = (bf16[8,128,128]{2,1,0:T(8,128)(2,1)S(1)}, bf16[8,128,128]{2,1,0:T(8,128)(2,1)S(1)}, u32[]{:S(2)}, u32[]{:S(2)}) collective-permute-start(bf16[8,128,128]{2,1,0:T(8,128)(2,1)S(1)} %get-tuple-element.53), channel_id=1, source_target_pairs={{0,4},{1,5},{2,6},{3,7},{4,0},{5,1},{6,2},{7,3},{8,12},{9,13},{10,... | collective-permute-start | bytes 786440 | tf_op jit(solution)/shard_map/ppermute | solution.py:363
  9.7 1.9 %collective-permute-start.3 = (bf16[8,128,128]{2,1,0:T(8,128)(2,1)S(1)}, bf16[8,128,128]{2,1,0:T(8,128)(2,1)S(1)}, u32[]{:S(2)}, u32[]{:S(2)}) collective-permute-start(bf16[8,128,128]{2,1,0:T(8,128)(2,1)S(1)} %get-tuple-element.55), channel_id=1, source_target_pairs={{0,6},{1,7},{2,4},{3,5},{4,2},{5,3},{6,0},{7,1},{8,14},{9,15},{10,... | collective-permute-start | bytes 786440 | tf_op jit(solution)/shard_map/ppermute | solution.py:363
  11.6 4.5 %shard_map.31 = (f32[2,128,4096]{2,1,0:T(8,128)S(1)}, bf16[2,128,4096]{2,1,0:T(8,128)(2,1)S(1)}, f32[2,1,4096]{2,1,0:T(1,128)S(1)}) custom-call(bf16[3,128,8192]{2,1,0:T(8,128)(2,1)} %bitcast.4, bf16[128,4096]{1,0:T(8,128)(2,1)S(1)} %get-tuple-element.42.k_ref.refs_0_, bf16[128,4096]{1,0:T(8,128)(2,1)S(1)} %get-tuple-element.43.v_ref.refs_1_, ...), custom_call_target="tpu_custom_call" | custom-call | flops 536870912 | bytes 12582912 | tf_op jit(solution)/shard_map/pallas_call | solution.py:369
  16.1 1.3 %collective-permute-done.1.refs_0_.refs_4_ = bf16[8,128,128]{2,1,0:T(8,128)(2,1)S(1)} collective-permute-done((bf16[8,128,128]{2,1,0:T(8,128)(2,1)S(1)}, bf16[8,128,128]{2,1,0:T(8,128)(2,1)S(1)}, u32[]{:S(2)}, u32[]{:S(2)}) %collective-permute-start.1) | collective-permute-done | bytes 262176 | tf_op jit(solution)/shard_map/ppermute | solution.py:363
  17.4 4.0 %collective-permute-done.2.refs_1_.refs_5_ = bf16[8,128,128]{2,1,0:T(8,128)(2,1)S(1)} collective-permute-done((bf16[8,128,128]{2,1,0:T(8,128)(2,1)S(1)}, bf16[8,128,128]{2,1,0:T(8,128)(2,1)S(1)}, u32[]{:S(2)}, u32[]{:S(2)}) %collective-permute-start.2) | collective-permute-done | bytes 262176 | tf_op jit(solution)/shard_map/ppermute | solution.py:363
  21.4 2.3 %collective-permute-done.3.refs_2_.refs_6_ = bf16[8,128,128]{2,1,0:T(8,128)(2,1)S(1)} collective-permute-done((bf16[8,128,128]{2,1,0:T(8,128)(2,1)S(1)}, bf16[8,128,128]{2,1,0:T(8,128)(2,1)S(1)}, u32[]{:S(2)}, u32[]{:S(2)}) %collective-permute-start.3) | collective-permute-done | bytes 262176 | tf_op jit(solution)/shard_map/ppermute | solution.py:363
  24.0 2.9 %collective-permute-start.5 = (bf16[2,128,128]{2,1,0:T(8,128)(2,1)S(1)}, bf16[2,128,128]{2,1,0:T(8,128)(2,1)S(1)}, u32[]{:S(2)}, u32[]{:S(2)}) collective-permute-start(bf16[2,128,128]{2,1,0:T(8,128)(2,1)S(1)} %get-tuple-element.66), channel_id=1, source_target_pairs={{0,16},{8,24},{16,0},{24,8},{48,32},{56,40},{32,48},{40,56},{64,80... | collective-permute-start | bytes 196616 | tf_op jit(solution)/shard_map/ppermute | solution.py:412
  27.5 1.1 %collective-permute-done.5.refs_2_.refs_5_ = bf16[2,128,128]{2,1,0:T(8,128)(2,1)S(1)} collective-permute-done((bf16[2,128,128]{2,1,0:T(8,128)(2,1)S(1)}, bf16[2,128,128]{2,1,0:T(8,128)(2,1)S(1)}, u32[]{:S(2)}, u32[]{:S(2)}) %collective-permute-start.5) | collective-permute-done | bytes 65568 | tf_op jit(solution)/shard_map/ppermute | solution.py:412
  28.6 3.2 %collective-permute-done.6.refs_3_.refs_6_ = bf16[2,128,128]{2,1,0:T(8,128)(2,1)S(1)} collective-permute-done((bf16[2,128,128]{2,1,0:T(8,128)(2,1)S(1)}, bf16[2,128,128]{2,1,0:T(8,128)(2,1)S(1)}, u32[]{:S(2)}, u32[]{:S(2)}) %collective-permute-start.6) | collective-permute-done | bytes 65568 | tf_op jit(solution)/shard_map/ppermute | solution.py:412
  31.8 4.8 %collective-permute-start.7 = (bf16[2,128,128]{2,1,0:T(8,128)(2,1)S(1)}, bf16[2,128,128]{2,1,0:T(8,128)(2,1)S(1)}, u32[]{:S(2)}, u32[]{:S(2)}) collective-permute-start(bf16[2,128,128]{2,1,0:T(8,128)(2,1)S(1)} %shard_map.33), channel_id=1, source_target_pairs={{0,48},{8,56},{16,32},{24,40},{32,16},{40,24},{48,0},{56,8},{64,11... | collective-permute-start | bytes 196616 | tf_op jit(solution)/shard_map/ppermute | solution.py:416
  36.6 1.7 %collective-permute-done.7.mirror_ref = bf16[2,128,128]{2,1,0:T(8,128)(2,1)S(1)} collective-permute-done((bf16[2,128,128]{2,1,0:T(8,128)(2,1)S(1)}, bf16[2,128,128]{2,1,0:T(8,128)(2,1)S(1)}, u32[]{:S(2)}, u32[]{:S(2)}) %collective-permute-start.7) | collective-permute-done | bytes 65568 | tf_op jit(solution)/shard_map/ppermute | solution.py:416
  38.3 2.8 %collective-permute-start.10 = (bf16[2,128,128]{2,1,0:T(8,128)(2,1)S(1)}, bf16[2,128,128]{2,1,0:T(8,128)(2,1)S(1)}, u32[]{:S(2)}, u32[]{:S(2)}) collective-permute-start(bf16[2,128,128]{2,1,0:T(8,128)(2,1)S(1)} %add_convert_fusion), channel_id=1, source_target_pairs={{0,192},{8,200},{16,208},{24,216},{32,224},{40,232},{48,240},{56,2... | collective-permute-start | bytes 196616 | tf_op jit(solution)/shard_map/ppermute | solution.py:418
  42.8 3.0 %collective-permute-done.9.refs_1_ = bf16[2,128,128]{2,1,0:T(8,128)(2,1)S(1)} collective-permute-done((bf16[2,128,128]{2,1,0:T(8,128)(2,1)S(1)}, bf16[2,128,128]{2,1,0:T(8,128)(2,1)S(1)}, u32[]{:S(2)}, u32[]{:S(2)}) %collective-permute-start.9) | collective-permute-done | bytes 65568 | tf_op jit(solution)/shard_map/ppermute | solution.py:418
  46.1 1.9 %collective-permute-start.12 = (bf16[2,128,128]{2,1,0:T(8,128)(2,1)S(1)}, bf16[2,128,128]{2,1,0:T(8,128)(2,1)S(1)}, u32[]{:S(2)}, u32[]{:S(2)}) collective-permute-start(bf16[2,128,128]{2,1,0:T(8,128)(2,1)S(1)} %get-tuple-element.70), channel_id=1, source_target_pairs={{0,16},{8,24},{16,0},{24,8},{48,32},{56,40},{32,48},{40,56},{64,80... | collective-permute-start | bytes 196616 | tf_op jit(solution)/shard_map/ppermute | solution.py:428
  48.0 1.6 %collective-permute-start.13 = (bf16[2,128,128]{2,1,0:T(8,128)(2,1)S(1)}, bf16[2,128,128]{2,1,0:T(8,128)(2,1)S(1)}, u32[]{:S(2)}, u32[]{:S(2)}) collective-permute-start(bf16[2,128,128]{2,1,0:T(8,128)(2,1)S(1)} %get-tuple-element.71), channel_id=1, source_target_pairs={{0,24},{8,16},{16,8},{24,0},{48,40},{56,32},{32,56},{40,48},{64,88... | collective-permute-start | bytes 196616 | tf_op jit(solution)/shard_map/ppermute | solution.py:428
  50.2 2.7 %collective-permute-done.13.refs_3_ = bf16[2,128,128]{2,1,0:T(8,128)(2,1)S(1)} collective-permute-done((bf16[2,128,128]{2,1,0:T(8,128)(2,1)S(1)}, bf16[2,128,128]{2,1,0:T(8,128)(2,1)S(1)}, u32[]{:S(2)}, u32[]{:S(2)}) %collective-permute-start.13) | collective-permute-done | bytes 65568 | tf_op jit(solution)/shard_map/ppermute | solution.py:428
  53.1 2.9 %collective-permute-start.14 = (bf16[8,128,128]{2,1,0:T(8,128)(2,1)S(1)}, bf16[8,128,128]{2,1,0:T(8,128)(2,1)S(1)}, u32[]{:S(2)}, u32[]{:S(2)}) collective-permute-start(bf16[8,128,128]{2,1,0:T(8,128)(2,1)S(1)} %get-tuple-element.72), channel_id=1, source_target_pairs={{0,4},{1,5},{2,6},{3,7},{4,0},{5,1},{6,2},{7,3},{8,12},{9,13},{10,... | collective-permute-start | bytes 786440 | tf_op jit(solution)/shard_map/ppermute | solution.py:446
  56.8 6.5 %collective-permute-start.20 = (bf16[8,128,128]{2,1,0:T(8,128)(2,1)S(1)}, bf16[8,128,128]{2,1,0:T(8,128)(2,1)S(1)}, u32[]{:S(2)}, u32[]{:S(2)}) collective-permute-start(bf16[8,128,128]{2,1,0:T(8,128)(2,1)S(1)} %shard_map.40), channel_id=1, source_target_pairs={{0,1},{1,0},{2,3},{3,2},{4,5},{5,4},{6,7},{7,6},{8,9},{9,8},{10,11... | collective-permute-start | bytes 786440 | tf_op jit(solution)/shard_map/ppermute | solution.py:458
  63.4 3.7 %collective-permute-start.17 = (bf16[8,128,128]{2,1,0:T(8,128)(2,1)S(1)}, bf16[8,128,128]{2,1,0:T(8,128)(2,1)S(1)}, u32[]{:S(2)}, u32[]{:S(2)}) collective-permute-start(bf16[8,128,128]{2,1,0:T(8,128)(2,1)S(1)} %shard_map.37), channel_id=1, source_target_pairs={{0,1},{1,0},{2,3},{3,2},{4,5},{5,4},{6,7},{7,6},{8,9},{9,8},{10,11... | collective-permute-start | bytes 786440 | tf_op jit(solution)/shard_map/ppermute | solution.py:458
  67.1 2.9 %collective-permute-start.18 = (bf16[8,128,128]{2,1,0:T(8,128)(2,1)S(1)}, bf16[8,128,128]{2,1,0:T(8,128)(2,1)S(1)}, u32[]{:S(2)}, u32[]{:S(2)}) collective-permute-start(bf16[8,128,128]{2,1,0:T(8,128)(2,1)S(1)} %shard_map.38), channel_id=1, source_target_pairs={{0,1},{1,0},{2,3},{3,2},{4,5},{5,4},{6,7},{7,6},{8,9},{9,8},{10,11... | collective-permute-start | bytes 786440 | tf_op jit(solution)/shard_map/ppermute | solution.py:458
  71.6 2.3 %shard_map.41 = bf16[128,8192]{1,0:T(8,128)(2,1)} custom-call(bf16[2,128,4096]{2,1,0:T(8,128)(2,1)S(1)} %get-tuple-element.57.q_ref, f32[2,128,4096]{2,1,0:T(8,128)S(1)} %get-tuple-element.58.inside_ref, f32[2,1,4096]{2,1,0:T(1,128)S(1)} %get-tuple-element.59.gain_ref, f32[128,4096]{1,0:T(8,128)S(1)} %get-tuple-element.76.refs_0_, ...), custom_call_target="tpu_custom_call" | custom-call | flops 134217728 | bytes 7340032 | tf_op jit(solution)/shard_map/pallas_call | solution.py:492
  (35 shorter events, 7.1 us)
Async XLA Ops:
  2.5 5.6 %collective-permute-start = (bf16[32,128,128]{2,1,0:T(8,128)(2,1)S(1)}, bf16[32,128,128]{2,1,0:T(8,128)(2,1)S(1)}, u32[]{:S(2)}, u32[]{:S(2)}) collective-permute-start(bf16[32,128,128]{2,1,0:T(8,128)(2,1)S(1)} %get-tuple-element.46), channel_id=1, source_target_pairs={{0,1},{1,0},{2,3},{3,2},{4,5},{5,4},{6,7},{7,6},{8,9},{9,8},{10,11... | collective-permute-start | bytes 3145736 | tf_op jit(solution)/shard_map/ppermute | solution.py:345
  6.3 5.3 %copy-start = (f32[8192]{0:T(1024)S(1)}, f32[8192]{0:T(1024)}, u32[]{:S(2)}) copy-start(f32[8192]{0:T(1024)} %param.3) | copy-start | bytes 98308
  8.3 9.2 %collective-permute-start.1 = (bf16[8,128,128]{2,1,0:T(8,128)(2,1)S(1)}, bf16[8,128,128]{2,1,0:T(8,128)(2,1)S(1)}, u32[]{:S(2)}, u32[]{:S(2)}) collective-permute-start(bf16[8,128,128]{2,1,0:T(8,128)(2,1)S(1)} %get-tuple-element.53), channel_id=1, source_target_pairs={{0,4},{1,5},{2,6},{3,7},{4,0},{5,1},{6,2},{7,3},{8,12},{9,13},{10,... | collective-permute-start | bytes 786440 | tf_op jit(solution)/shard_map/ppermute | solution.py:363
  9.4 12.0 %collective-permute-start.2 = (bf16[8,128,128]{2,1,0:T(8,128)(2,1)S(1)}, bf16[8,128,128]{2,1,0:T(8,128)(2,1)S(1)}, u32[]{:S(2)}, u32[]{:S(2)}) collective-permute-start(bf16[8,128,128]{2,1,0:T(8,128)(2,1)S(1)} %get-tuple-element.54), channel_id=1, source_target_pairs={{0,2},{1,3},{2,0},{3,1},{4,6},{5,7},{6,4},{7,5},{8,10},{9,11},{10,... | collective-permute-start | bytes 786440 | tf_op jit(solution)/shard_map/ppermute | solution.py:363
  9.7 14.0 %collective-permute-start.3 = (bf16[8,128,128]{2,1,0:T(8,128)(2,1)S(1)}, bf16[8,128,128]{2,1,0:T(8,128)(2,1)S(1)}, u32[]{:S(2)}, u32[]{:S(2)}) collective-permute-start(bf16[8,128,128]{2,1,0:T(8,128)(2,1)S(1)} %get-tuple-element.55), channel_id=1, source_target_pairs={{0,6},{1,7},{2,4},{3,5},{4,2},{5,3},{6,0},{7,1},{8,14},{9,15},{10,... | collective-permute-start | bytes 786440 | tf_op jit(solution)/shard_map/ppermute | solution.py:363
  23.9 3.6 %collective-permute-start.4 = (bf16[2,128,128]{2,1,0:T(8,128)(2,1)S(1)}, bf16[2,128,128]{2,1,0:T(8,128)(2,1)S(1)}, u32[]{:S(2)}, u32[]{:S(2)}) collective-permute-start(bf16[2,128,128]{2,1,0:T(8,128)(2,1)S(1)} %get-tuple-element.65), channel_id=1, source_target_pairs={{0,8},{8,0},{16,24},{24,16},{48,56},{56,48},{32,40},{40,32},{64,72... | collective-permute-start | bytes 196616 | tf_op jit(solution)/shard_map/ppermute | solution.py:412
  24.0 4.6 %collective-permute-start.5 = (bf16[2,128,128]{2,1,0:T(8,128)(2,1)S(1)}, bf16[2,128,128]{2,1,0:T(8,128)(2,1)S(1)}, u32[]{:S(2)}, u32[]{:S(2)}) collective-permute-start(bf16[2,128,128]{2,1,0:T(8,128)(2,1)S(1)} %get-tuple-element.66), channel_id=1, source_target_pairs={{0,16},{8,24},{16,0},{24,8},{48,32},{56,40},{32,48},{40,56},{64,80... | collective-permute-start | bytes 196616 | tf_op jit(solution)/shard_map/ppermute | solution.py:412
  26.8 4.9 %collective-permute-start.6 = (bf16[2,128,128]{2,1,0:T(8,128)(2,1)S(1)}, bf16[2,128,128]{2,1,0:T(8,128)(2,1)S(1)}, u32[]{:S(2)}, u32[]{:S(2)}) collective-permute-start(bf16[2,128,128]{2,1,0:T(8,128)(2,1)S(1)} %get-tuple-element.67), channel_id=1, source_target_pairs={{0,24},{8,16},{16,8},{24,0},{48,40},{56,32},{32,56},{40,48},{64,88... | collective-permute-start | bytes 196616 | tf_op jit(solution)/shard_map/ppermute | solution.py:412
  31.8 6.5 %collective-permute-start.7 = (bf16[2,128,128]{2,1,0:T(8,128)(2,1)S(1)}, bf16[2,128,128]{2,1,0:T(8,128)(2,1)S(1)}, u32[]{:S(2)}, u32[]{:S(2)}) collective-permute-start(bf16[2,128,128]{2,1,0:T(8,128)(2,1)S(1)} %shard_map.33), channel_id=1, source_target_pairs={{0,48},{8,56},{16,32},{24,40},{32,16},{40,24},{48,0},{56,8},{64,11... | collective-permute-start | bytes 196616 | tf_op jit(solution)/shard_map/ppermute | solution.py:416
  38.3 4.5 %collective-permute-start.10 = (bf16[2,128,128]{2,1,0:T(8,128)(2,1)S(1)}, bf16[2,128,128]{2,1,0:T(8,128)(2,1)S(1)}, u32[]{:S(2)}, u32[]{:S(2)}) collective-permute-start(bf16[2,128,128]{2,1,0:T(8,128)(2,1)S(1)} %add_convert_fusion), channel_id=1, source_target_pairs={{0,192},{8,200},{16,208},{24,216},{32,224},{40,232},{48,240},{56,2... | collective-permute-start | bytes 196616 | tf_op jit(solution)/shard_map/ppermute | solution.py:418
  41.1 4.7 %collective-permute-start.9 = (bf16[2,128,128]{2,1,0:T(8,128)(2,1)S(1)}, bf16[2,128,128]{2,1,0:T(8,128)(2,1)S(1)}, u32[]{:S(2)}, u32[]{:S(2)}) collective-permute-start(bf16[2,128,128]{2,1,0:T(8,128)(2,1)S(1)} %add_convert_fusion), channel_id=1, source_target_pairs={{0,128},{8,136},{16,144},{24,152},{32,160},{40,168},{48,176},{56,1... | collective-permute-start | bytes 196616 | tf_op jit(solution)/shard_map/ppermute | solution.py:418
  41.5 4.3 %collective-permute-start.8 = (bf16[2,128,128]{2,1,0:T(8,128)(2,1)S(1)}, bf16[2,128,128]{2,1,0:T(8,128)(2,1)S(1)}, u32[]{:S(2)}, u32[]{:S(2)}) collective-permute-start(bf16[2,128,128]{2,1,0:T(8,128)(2,1)S(1)} %add_convert_fusion), channel_id=1, source_target_pairs={{0,64},{8,72},{16,80},{24,88},{32,96},{40,104},{48,112},{56,120},{... | collective-permute-start | bytes 196616 | tf_op jit(solution)/shard_map/ppermute | solution.py:418
  46.0 3.6 %collective-permute-start.11 = (bf16[2,128,128]{2,1,0:T(8,128)(2,1)S(1)}, bf16[2,128,128]{2,1,0:T(8,128)(2,1)S(1)}, u32[]{:S(2)}, u32[]{:S(2)}) collective-permute-start(bf16[2,128,128]{2,1,0:T(8,128)(2,1)S(1)} %get-tuple-element.69), channel_id=1, source_target_pairs={{0,8},{8,0},{16,24},{24,16},{48,56},{56,48},{32,40},{40,32},{64,72... | collective-permute-start | bytes 196616 | tf_op jit(solution)/shard_map/ppermute | solution.py:428
  46.1 4.1 %collective-permute-start.12 = (bf16[2,128,128]{2,1,0:T(8,128)(2,1)S(1)}, bf16[2,128,128]{2,1,0:T(8,128)(2,1)S(1)}, u32[]{:S(2)}, u32[]{:S(2)}) collective-permute-start(bf16[2,128,128]{2,1,0:T(8,128)(2,1)S(1)} %get-tuple-element.70), channel_id=1, source_target_pairs={{0,16},{8,24},{16,0},{24,8},{48,32},{56,40},{32,48},{40,56},{64,80... | collective-permute-start | bytes 196616 | tf_op jit(solution)/shard_map/ppermute | solution.py:428
  48.0 4.9 %collective-permute-start.13 = (bf16[2,128,128]{2,1,0:T(8,128)(2,1)S(1)}, bf16[2,128,128]{2,1,0:T(8,128)(2,1)S(1)}, u32[]{:S(2)}, u32[]{:S(2)}) collective-permute-start(bf16[2,128,128]{2,1,0:T(8,128)(2,1)S(1)} %get-tuple-element.71), channel_id=1, source_target_pairs={{0,24},{8,16},{16,8},{24,0},{48,40},{56,32},{32,56},{40,48},{64,88... | collective-permute-start | bytes 196616 | tf_op jit(solution)/shard_map/ppermute | solution.py:428
  53.1 10.3 %collective-permute-start.14 = (bf16[8,128,128]{2,1,0:T(8,128)(2,1)S(1)}, bf16[8,128,128]{2,1,0:T(8,128)(2,1)S(1)}, u32[]{:S(2)}, u32[]{:S(2)}) collective-permute-start(bf16[8,128,128]{2,1,0:T(8,128)(2,1)S(1)} %get-tuple-element.72), channel_id=1, source_target_pairs={{0,4},{1,5},{2,6},{3,7},{4,0},{5,1},{6,2},{7,3},{8,12},{9,13},{10,... | collective-permute-start | bytes 786440 | tf_op jit(solution)/shard_map/ppermute | solution.py:446
  56.0 11.1 %collective-permute-start.15 = (bf16[8,128,128]{2,1,0:T(8,128)(2,1)S(1)}, bf16[8,128,128]{2,1,0:T(8,128)(2,1)S(1)}, u32[]{:S(2)}, u32[]{:S(2)}) collective-permute-start(bf16[8,128,128]{2,1,0:T(8,128)(2,1)S(1)} %get-tuple-element.73), channel_id=1, source_target_pairs={{0,2},{1,3},{2,0},{3,1},{4,6},{5,7},{6,4},{7,5},{8,10},{9,11},{10,... | collective-permute-start | bytes 786440 | tf_op jit(solution)/shard_map/ppermute | solution.py:446
  56.3 13.7 %collective-permute-start.16 = (bf16[8,128,128]{2,1,0:T(8,128)(2,1)S(1)}, bf16[8,128,128]{2,1,0:T(8,128)(2,1)S(1)}, u32[]{:S(2)}, u32[]{:S(2)}) collective-permute-start(bf16[8,128,128]{2,1,0:T(8,128)(2,1)S(1)} %get-tuple-element.74), channel_id=1, source_target_pairs={{0,6},{1,7},{2,4},{3,5},{4,2},{5,3},{6,0},{7,1},{8,14},{9,15},{10,... | collective-permute-start | bytes 786440 | tf_op jit(solution)/shard_map/ppermute | solution.py:446
  56.8 14.1 %collective-permute-start.20 = (bf16[8,128,128]{2,1,0:T(8,128)(2,1)S(1)}, bf16[8,128,128]{2,1,0:T(8,128)(2,1)S(1)}, u32[]{:S(2)}, u32[]{:S(2)}) collective-permute-start(bf16[8,128,128]{2,1,0:T(8,128)(2,1)S(1)} %shard_map.40), channel_id=1, source_target_pairs={{0,1},{1,0},{2,3},{3,2},{4,5},{5,4},{6,7},{7,6},{8,9},{9,8},{10,11... | collective-permute-start | bytes 786440 | tf_op jit(solution)/shard_map/ppermute | solution.py:458
  63.4 7.6 %collective-permute-start.17 = (bf16[8,128,128]{2,1,0:T(8,128)(2,1)S(1)}, bf16[8,128,128]{2,1,0:T(8,128)(2,1)S(1)}, u32[]{:S(2)}, u32[]{:S(2)}) collective-permute-start(bf16[8,128,128]{2,1,0:T(8,128)(2,1)S(1)} %shard_map.37), channel_id=1, source_target_pairs={{0,1},{1,0},{2,3},{3,2},{4,5},{5,4},{6,7},{7,6},{8,9},{9,8},{10,11... | collective-permute-start | bytes 786440 | tf_op jit(solution)/shard_map/ppermute | solution.py:458
  67.1 4.0 %collective-permute-start.18 = (bf16[8,128,128]{2,1,0:T(8,128)(2,1)S(1)}, bf16[8,128,128]{2,1,0:T(8,128)(2,1)S(1)}, u32[]{:S(2)}, u32[]{:S(2)}) collective-permute-start(bf16[8,128,128]{2,1,0:T(8,128)(2,1)S(1)} %shard_map.38), channel_id=1, source_target_pairs={{0,1},{1,0},{2,3},{3,2},{4,5},{5,4},{6,7},{7,6},{8,9},{9,8},{10,11... | collective-permute-start | bytes 786440 | tf_op jit(solution)/shard_map/ppermute | solution.py:458
  70.0 1.6 %collective-permute-start.19 = (bf16[8,128,128]{2,1,0:T(8,128)(2,1)S(1)}, bf16[8,128,128]{2,1,0:T(8,128)(2,1)S(1)}, u32[]{:S(2)}, u32[]{:S(2)}) collective-permute-start(bf16[8,128,128]{2,1,0:T(8,128)(2,1)S(1)} %shard_map.39), channel_id=1, source_target_pairs={{0,1},{1,0},{2,3},{3,2},{4,5},{5,4},{6,7},{7,6},{8,9},{9,8},{10,11... | collective-permute-start | bytes 786440 | tf_op jit(solution)/shard_map/ppermute | solution.py:458

commit v6 on v5

--- a/solution.py
+++ b/solution.py
@@ -14,7 +14,7 @@
 HBM = pl.BlockSpec(memory_space=pltpu.HBM)
 
 
-ORDER = (2, 1, 3, 0)
+ORDER = (1, 3, 2, 0)
 CHUNKS = 1
 NZ = 8
 LINE = NZ // 2
@@ -79,16 +79,18 @@
     return list(zip(*loads))
 
 
-def first_body(qkv_ref, send_ref, k_ref, v_ref, own_k_ref, own_v_ref, sems):
+def first_body(qkv_ref, send0_ref, send1_ref, k_ref, v_ref, own_k_ref, own_v_ref, sems):
     place = my_place()
     pairs = start_pairs(place, qkv_ref, 1 - place[1], k_ref, v_ref, sems.at[0])
     later = start_pairs(place, qkv_ref, place[1], own_k_ref, own_v_ref, sems.at[1])
-    each = send_ref.shape[0] // len(pairs)
+    few = send0_ref.shape[0]
+    each = 2 * few // len(pairs)
     for i, pair in enumerate(pairs):
         for copy in pair:
             copy.wait()
         for h in range(i * each, (i + 1) * each):
-            send_ref[h] = head_state(k_ref, v_ref, h).astype(BF16)
+            send_ref = send0_ref if h < few else send1_ref
+            send_ref[h % few] = head_state(k_ref, v_ref, h).astype(BF16)
     for pair in later:
         for copy in pair:
             copy.wait()
@@ -101,18 +103,20 @@
         low_ref[h] = state.astype(BF16)
 
 
-def chip_body(own_ref, got_ref, *chip_refs):
+def chip_body(before, own_ref, got_ref, *chip_refs):
     few = chip_refs[0].shape[0]
     for i, chip_ref in enumerate(chip_refs):
         for h in range(few):
             at = i * few + h
-            chip_ref[h] = (own_ref[at] + got_ref[at].astype(F32)).astype(BF16)
+            chip_ref[h] = (own_ref[before + at] + got_ref[at].astype(F32)).astype(BF16)
 
 
 def inside_body(qkv_ref, *refs):
     place = my_place()
     kv_refs = refs[:4]
-    got_ref, gain_ref, inside_ref, q_ref, order_ref, scores_ref, sems = refs[4:]
+    got_refs = refs[4:6]
+    gain_ref, inside_ref, q_ref, order_ref, scores_ref, sems = refs[6:]
+    few = got_refs[0].shape[0]
     rows, width = kv_refs[0].shape
     loads = [
         start_loads(qkv_ref, 0, place, side, q_ref.at[i], sems.at[i])
@@ -161,7 +165,7 @@
             cols = head_cols(h)
             inside_ref[0, :, cols] = jnp.dot(
                 jnp.concatenate([scores_ref[0, :, cols], q_ref[0, :, cols]], axis=1),
-                jnp.concatenate([kv_refs[1][:, cols], got_ref[h]], axis=0),
+                jnp.concatenate([kv_refs[1][:, cols], got_refs[h // few][h % few]], axis=0),
                 preferred_element_type=F32,
             )
 
@@ -333,29 +337,31 @@
     mib = 2**20
     matrix = jax.ShapeDtypeStruct((rows, width // 2), BF16)
     loads = pltpu.SemaphoreType.DMA((2, nx))
-    send, keys, value_rows, own_keys, own_values = call(
+    send0, send1, keys, value_rows, own_keys, own_values = call(
         first_body,
         [HBM],
-        [VMEM] * 5,
-        [states(half)] + [matrix] * 4,
+        [VMEM] * 6,
+        [states(half // 2)] * 2 + [matrix] * 4,
         half,
         5 * mib,
         scratch=[pltpu.SemaphoreType.DMA((2, 2, nx))],
     )(qkv)
-    got = lax.ppermute(send, "tp", swap)
+    got = [lax.ppermute(send, "tp", swap) for send in (send0, send1)]
     own, low = call(
         own_body, [VMEM] * 2, [VMEM] * 2, [states(half, F32), states(half)], half, 5 * mib
     )(own_keys, own_values)
     few = each // CHUNKS
     ny = nctx // NZ
-    made = call(
-        chip_body,
-        [VMEM, VMEM],
-        [VMEM] * (nx * CHUNKS),
-        [states(few)] * (nx * CHUNKS),
-        0,
-        4 * mib,
-    )(own, got)
+    made = []
+    for i in range(2):
+        made += call(
+            functools.partial(chip_body, i * half // 2),
+            [VMEM, VMEM],
+            [VMEM] * (nx * CHUNKS // 2),
+            [states(few)] * (nx * CHUNKS // 2),
+            0,
+            2 * mib,
+        )(own, got[i])
     chips = [[made[i * CHUNKS + c] for i in range(nx)] for c in range(CHUNKS)]
     if CHUNKS == 1:
         gain, chips[-1][-1] = lax.optimization_barrier((gain, chips[-1][-1]))
@@ -368,7 +374,7 @@
     def local(gain):
         return call(
             inside_body,
-            [HBM] + [VMEM] * 6,
+            [HBM] + [VMEM] * 7,
             [VMEM] * 3,
             [
                 jax.ShapeDtypeStruct(wide, F32),
@@ -378,7 +384,7 @@
             4 * half,
             12 * mib,
             scratch=[pltpu.VMEM(wide, BF16), loads],
-        )(qkv, own_keys, own_values, keys, value_rows, got, gain)
+        )(qkv, own_keys, own_values, keys, value_rows, *got, gain)
 
     if CHUNKS == 1:
         inside, queries, gains = local(gain)

time: 74.1 us -> 72.7 us (0.981)
    ppermute x1, starting transfers between devices: 4.82 us -> 2.28 us  [per_device(): facing = lax.ppermute(mine, 'ctx', mirror)]
    ppermute x3, waiting for transfers between devices: 7.59 us -> 5.69 us  [per_device(): lax.ppermute(t, 'tp', shift(d))]
    ppermute x1, waiting for transfers between devices: 1.66 us -> 3.46 us  [per_device(): facing = lax.ppermute(mine, 'ctx', mirror)]
    ppermute x3, starting transfers between devices: 3.63 us -> 4.71 us  [per_device(): lax.ppermute(t, 'ctx', line(d))]
    ppermute x4, starting transfers between devices: 13.5 us -> 14.3 us  [give(): return lax.ppermute(given, 'tp', swap)]
    ppermute x1 -> x2, waiting for transfers between devices: 1.79 us -> 0.95 us  [per_device(): got = [lax.ppermute(send, 'tp', swap) for send in (send0, send1)]]
    ppermute x1 -> x2, starting transfers between devices: 3.32 us -> 3.42 us  [per_device(): got = [lax.ppermute(send, 'tp', swap) for send in (send0, send1)]]
    pallas_call x3 -> x4, Pallas kernels: 7.15 us -> 7.17 us  [the longest x1 4.5 us: local(): call(inside_body, [HBM] + [VMEM] * 7, [VMEM] * 3, [jax.ShapeDtypeStruct(w...]
  transfers between devices with their start and end apart: 21 -> 22, of which waited for: 13 -> 11; matrix products, arithmetic and copies ran while one was open for 0% -> 0% of each run, Pallas kernels for 8% -> 8%
where the time goes in v6:
time: 72.7 us; the launch traced here: 72.6 us
  starting transfers between devices  38.7 us (53%)
  waiting for transfers between devices  22.6 us (31%)
  Pallas kernels  11 us (15%)
    ppermute x4, starting transfers between devices, give(): return lax.ppermute(given, 'tp', swap)  14.3 us
    ppermute x3, waiting for transfers between devices, per_device(): lax.ppermute(t, 'tp', shift(d))  5.69 us
    ppermute x3, waiting for transfers between devices, per_device(): lax.ppermute(t, 'ctx', line(d))  4.91 us
    ppermute x3, starting transfers between devices, per_device(): lax.ppermute(t, 'ctx', line(d))  4.71 us
    pallas_call x1, Pallas kernels, local(): call(inside_body, [HBM] + [VMEM] * 7, [VMEM] * 3, [jax.ShapeDtypeStruct(w...  4.5 us
    ppermute x3, waiting for transfers between devices, per_device(): rows_before = [lax.ppermute(whole, 'ctx', row(d)) for d in range(1, ny)]  3.94 us
    ppermute x3, starting transfers between devices, per_device(): lax.ppermute(b, 'ctx', line(k % LINE))  3.63 us
    ppermute x3, starting transfers between devices, per_device(): rows_before = [lax.ppermute(whole, 'ctx', row(d)) for d in range(1, ny)]  3.5 us
  transfers between devices with their start and end apart: 22, of which 11 were waited for; matrix products, arithmetic and copies ran while one was open for 0% of the time, Pallas kernels for 8%

profile of v6, /device:TPU:1, one launch (start us, length us, event | category | flops | bytes accessed | tf_op | source)
XLA Modules:
  0.0 72.6 jit_solution(13578393181340510932)
XLA Ops:
  0.0 2.5 %shard_map.28 = (bf16[16,128,128]{2,1,0:T(8,128)(2,1)S(1)}, bf16[16,128,128]{2,1,0:T(8,128)(2,1)S(1)}, bf16[128,4096]{1,0:T(8,128)(2,1)S(1)}, bf16[128,4096]{1,0...) custom-call(bf16[3,128,8192]{2,1,0:T(8,128)(2,1)} %bitcast.3), custom_call_target="tpu_custom_call" | custom-call | flops 134217728 | bytes 5242880 | tf_op jit(solution)/shard_map/pallas_call | solution.py:340
  2.5 3.3 %collective-permute-start = (bf16[16,128,128]{2,1,0:T(8,128)(2,1)S(1)}, bf16[16,128,128]{2,1,0:T(8,128)(2,1)S(1)}, u32[]{:S(2)}, u32[]{:S(2)}) collective-permute-start(bf16[16,128,128]{2,1,0:T(8,128)(2,1)S(1)} %get-tuple-element.47), channel_id=1, source_target_pairs={{0,1},{1,0},{2,3},{3,2},{4,5},{5,4},{6,7},{7,6},{8,9},{9,8},{10,11... | collective-permute-start | bytes 1572872 | tf_op jit(solution)/shard_map/ppermute | solution.py:349
  7.6 1.3 %collective-permute-start.3 = (bf16[8,128,128]{2,1,0:T(8,128)(2,1)S(1)}, bf16[8,128,128]{2,1,0:T(8,128)(2,1)S(1)}, u32[]{:S(2)}, u32[]{:S(2)}) collective-permute-start(bf16[8,128,128]{2,1,0:T(8,128)(2,1)S(1)} %get-tuple-element.56), channel_id=1, source_target_pairs={{0,6},{1,7},{2,4},{3,5},{4,2},{5,3},{6,0},{7,1},{8,14},{9,15},{10,... | collective-permute-start | bytes 786440 | tf_op jit(solution)/shard_map/ppermute | solution.py:369
  8.9 2.0 %collective-permute-start.4 = (bf16[8,128,128]{2,1,0:T(8,128)(2,1)S(1)}, bf16[8,128,128]{2,1,0:T(8,128)(2,1)S(1)}, u32[]{:S(2)}, u32[]{:S(2)}) collective-permute-start(bf16[8,128,128]{2,1,0:T(8,128)(2,1)S(1)} %get-tuple-element.57), channel_id=1, source_target_pairs={{0,4},{1,5},{2,6},{3,7},{4,0},{5,1},{6,2},{7,3},{8,12},{9,13},{10,... | collective-permute-start | bytes 786440 | tf_op jit(solution)/shard_map/ppermute | solution.py:369
  11.0 4.5 %shard_map.31 = (f32[2,128,4096]{2,1,0:T(8,128)S(1)}, bf16[2,128,4096]{2,1,0:T(8,128)(2,1)S(1)}, f32[2,1,4096]{2,1,0:T(1,128)S(1)}) custom-call(bf16[3,128,8192]{2,1,0:T(8,128)(2,1)} %bitcast.4, bf16[128,4096]{1,0:T(8,128)(2,1)S(1)} %get-tuple-element.43.k_ref.refs_0_, bf16[128,4096]{1,0:T(8,128)(2,1)S(1)} %get-tuple-element.44.v_ref.refs_1_, ...), custom_call_target="tpu_custom_call" | custom-call | flops 536870912 | bytes 12582912 | tf_op jit(solution)/shard_map/pallas_call | solution.py:375
  15.5 1.7 %collective-permute-done.3.refs_1_.refs_5_ = bf16[8,128,128]{2,1,0:T(8,128)(2,1)S(1)} collective-permute-done((bf16[8,128,128]{2,1,0:T(8,128)(2,1)S(1)}, bf16[8,128,128]{2,1,0:T(8,128)(2,1)S(1)}, u32[]{:S(2)}, u32[]{:S(2)}) %collective-permute-start.3) | collective-permute-done | bytes 262176 | tf_op jit(solution)/shard_map/ppermute | solution.py:369
  17.2 4.0 %collective-permute-done.4.refs_2_.refs_6_ = bf16[8,128,128]{2,1,0:T(8,128)(2,1)S(1)} collective-permute-done((bf16[8,128,128]{2,1,0:T(8,128)(2,1)S(1)}, bf16[8,128,128]{2,1,0:T(8,128)(2,1)S(1)}, u32[]{:S(2)}, u32[]{:S(2)}) %collective-permute-start.4) | collective-permute-done | bytes 262176 | tf_op jit(solution)/shard_map/ppermute | solution.py:369
  21.3 1.7 %collective-permute-start.5 = (bf16[2,128,128]{2,1,0:T(8,128)(2,1)S(1)}, bf16[2,128,128]{2,1,0:T(8,128)(2,1)S(1)}, u32[]{:S(2)}, u32[]{:S(2)}) collective-permute-start(bf16[2,128,128]{2,1,0:T(8,128)(2,1)S(1)} %get-tuple-element.67), channel_id=1, source_target_pairs={{0,8},{8,0},{16,24},{24,16},{48,56},{56,48},{32,40},{40,32},{64,72... | collective-permute-start | bytes 196616 | tf_op jit(solution)/shard_map/ppermute | solution.py:418
  23.0 3.0 %collective-permute-start.6 = (bf16[2,128,128]{2,1,0:T(8,128)(2,1)S(1)}, bf16[2,128,128]{2,1,0:T(8,128)(2,1)S(1)}, u32[]{:S(2)}, u32[]{:S(2)}) collective-permute-start(bf16[2,128,128]{2,1,0:T(8,128)(2,1)S(1)} %get-tuple-element.68), channel_id=1, source_target_pairs={{0,16},{8,24},{16,0},{24,8},{48,32},{56,40},{32,48},{40,56},{64,80... | collective-permute-start | bytes 196616 | tf_op jit(solution)/shard_map/ppermute | solution.py:418
  26.0 2.3 %collective-permute-done.6.refs_2_.refs_5_ = bf16[2,128,128]{2,1,0:T(8,128)(2,1)S(1)} collective-permute-done((bf16[2,128,128]{2,1,0:T(8,128)(2,1)S(1)}, bf16[2,128,128]{2,1,0:T(8,128)(2,1)S(1)}, u32[]{:S(2)}, u32[]{:S(2)}) %collective-permute-start.6) | collective-permute-done | bytes 65568 | tf_op jit(solution)/shard_map/ppermute | solution.py:418
  28.4 2.6 %collective-permute-done.7.refs_3_.refs_6_ = bf16[2,128,128]{2,1,0:T(8,128)(2,1)S(1)} collective-permute-done((bf16[2,128,128]{2,1,0:T(8,128)(2,1)S(1)}, bf16[2,128,128]{2,1,0:T(8,128)(2,1)S(1)}, u32[]{:S(2)}, u32[]{:S(2)}) %collective-permute-start.7) | collective-permute-done | bytes 65568 | tf_op jit(solution)/shard_map/ppermute | solution.py:418
  31.0 2.3 %collective-permute-start.8 = (bf16[2,128,128]{2,1,0:T(8,128)(2,1)S(1)}, bf16[2,128,128]{2,1,0:T(8,128)(2,1)S(1)}, u32[]{:S(2)}, u32[]{:S(2)}) collective-permute-start(bf16[2,128,128]{2,1,0:T(8,128)(2,1)S(1)} %shard_map.34), channel_id=1, source_target_pairs={{0,48},{8,56},{16,32},{24,40},{32,16},{40,24},{48,0},{56,8},{64,11... | collective-permute-start | bytes 196616 | tf_op jit(solution)/shard_map/ppermute | solution.py:422
  33.3 3.5 %collective-permute-done.8.mirror_ref = bf16[2,128,128]{2,1,0:T(8,128)(2,1)S(1)} collective-permute-done((bf16[2,128,128]{2,1,0:T(8,128)(2,1)S(1)}, bf16[2,128,128]{2,1,0:T(8,128)(2,1)S(1)}, u32[]{:S(2)}, u32[]{:S(2)}) %collective-permute-start.8) | collective-permute-done | bytes 65568 | tf_op jit(solution)/shard_map/ppermute | solution.py:422
  36.7 2.8 %collective-permute-start.11 = (bf16[2,128,128]{2,1,0:T(8,128)(2,1)S(1)}, bf16[2,128,128]{2,1,0:T(8,128)(2,1)S(1)}, u32[]{:S(2)}, u32[]{:S(2)}) collective-permute-start(bf16[2,128,128]{2,1,0:T(8,128)(2,1)S(1)} %add_convert_fusion), channel_id=1, source_target_pairs={{0,192},{8,200},{16,208},{24,216},{32,224},{40,232},{48,240},{56,2... | collective-permute-start | bytes 196616 | tf_op jit(solution)/shard_map/ppermute | solution.py:424
  41.2 3.0 %collective-permute-done.10.refs_1_ = bf16[2,128,128]{2,1,0:T(8,128)(2,1)S(1)} collective-permute-done((bf16[2,128,128]{2,1,0:T(8,128)(2,1)S(1)}, bf16[2,128,128]{2,1,0:T(8,128)(2,1)S(1)}, u32[]{:S(2)}, u32[]{:S(2)}) %collective-permute-start.10) | collective-permute-done | bytes 65568 | tf_op jit(solution)/shard_map/ppermute | solution.py:424
  46.0 2.0 %collective-permute-start.14 = (bf16[2,128,128]{2,1,0:T(8,128)(2,1)S(1)}, bf16[2,128,128]{2,1,0:T(8,128)(2,1)S(1)}, u32[]{:S(2)}, u32[]{:S(2)}) collective-permute-start(bf16[2,128,128]{2,1,0:T(8,128)(2,1)S(1)} %get-tuple-element.73), channel_id=1, source_target_pairs={{0,24},{8,16},{16,8},{24,0},{48,40},{56,32},{32,56},{40,48},{64,88... | collective-permute-start | bytes 196616 | tf_op jit(solution)/shard_map/ppermute | solution.py:434
  49.0 2.0 %collective-permute-done.14.refs_3_ = bf16[2,128,128]{2,1,0:T(8,128)(2,1)S(1)} collective-permute-done((bf16[2,128,128]{2,1,0:T(8,128)(2,1)S(1)}, bf16[2,128,128]{2,1,0:T(8,128)(2,1)S(1)}, u32[]{:S(2)}, u32[]{:S(2)}) %collective-permute-start.14) | collective-permute-done | bytes 65568 | tf_op jit(solution)/shard_map/ppermute | solution.py:434
  51.7 1.3 %collective-permute-start.16 = (bf16[8,128,128]{2,1,0:T(8,128)(2,1)S(1)}, bf16[8,128,128]{2,1,0:T(8,128)(2,1)S(1)}, u32[]{:S(2)}, u32[]{:S(2)}) collective-permute-start(bf16[8,128,128]{2,1,0:T(8,128)(2,1)S(1)} %get-tuple-element.75), channel_id=1, source_target_pairs={{0,6},{1,7},{2,4},{3,5},{4,2},{5,3},{6,0},{7,1},{8,14},{9,15},{10,... | collective-permute-start | bytes 786440 | tf_op jit(solution)/shard_map/ppermute | solution.py:452
  53.0 1.6 %collective-permute-start.17 = (bf16[8,128,128]{2,1,0:T(8,128)(2,1)S(1)}, bf16[8,128,128]{2,1,0:T(8,128)(2,1)S(1)}, u32[]{:S(2)}, u32[]{:S(2)}) collective-permute-start(bf16[8,128,128]{2,1,0:T(8,128)(2,1)S(1)} %get-tuple-element.76), channel_id=1, source_target_pairs={{0,4},{1,5},{2,6},{3,7},{4,0},{5,1},{6,2},{7,3},{8,12},{9,13},{10,... | collective-permute-start | bytes 786440 | tf_op jit(solution)/shard_map/ppermute | solution.py:452
  54.6 7.8 %collective-permute-start.21 = (bf16[8,128,128]{2,1,0:T(8,128)(2,1)S(1)}, bf16[8,128,128]{2,1,0:T(8,128)(2,1)S(1)}, u32[]{:S(2)}, u32[]{:S(2)}) collective-permute-start(bf16[8,128,128]{2,1,0:T(8,128)(2,1)S(1)} %shard_map.41), channel_id=1, source_target_pairs={{0,1},{1,0},{2,3},{3,2},{4,5},{5,4},{6,7},{7,6},{8,9},{9,8},{10,11... | collective-permute-start | bytes 786440 | tf_op jit(solution)/shard_map/ppermute | solution.py:464
  62.4 2.3 %collective-permute-start.18 = (bf16[8,128,128]{2,1,0:T(8,128)(2,1)S(1)}, bf16[8,128,128]{2,1,0:T(8,128)(2,1)S(1)}, u32[]{:S(2)}, u32[]{:S(2)}) collective-permute-start(bf16[8,128,128]{2,1,0:T(8,128)(2,1)S(1)} %shard_map.38), channel_id=1, source_target_pairs={{0,1},{1,0},{2,3},{3,2},{4,5},{5,4},{6,7},{7,6},{8,9},{9,8},{10,11... | collective-permute-start | bytes 786440 | tf_op jit(solution)/shard_map/ppermute | solution.py:464
  64.7 2.5 %collective-permute-start.19 = (bf16[8,128,128]{2,1,0:T(8,128)(2,1)S(1)}, bf16[8,128,128]{2,1,0:T(8,128)(2,1)S(1)}, u32[]{:S(2)}, u32[]{:S(2)}) collective-permute-start(bf16[8,128,128]{2,1,0:T(8,128)(2,1)S(1)} %shard_map.39), channel_id=1, source_target_pairs={{0,1},{1,0},{2,3},{3,2},{4,5},{5,4},{6,7},{7,6},{8,9},{9,8},{10,11... | collective-permute-start | bytes 786440 | tf_op jit(solution)/shard_map/ppermute | solution.py:464
  67.3 1.8 %collective-permute-start.20 = (bf16[8,128,128]{2,1,0:T(8,128)(2,1)S(1)}, bf16[8,128,128]{2,1,0:T(8,128)(2,1)S(1)}, u32[]{:S(2)}, u32[]{:S(2)}) collective-permute-start(bf16[8,128,128]{2,1,0:T(8,128)(2,1)S(1)} %shard_map.40), channel_id=1, source_target_pairs={{0,1},{1,0},{2,3},{3,2},{4,5},{5,4},{6,7},{7,6},{8,9},{9,8},{10,11... | collective-permute-start | bytes 786440 | tf_op jit(solution)/shard_map/ppermute | solution.py:464
  70.2 2.3 %shard_map.42 = bf16[128,8192]{1,0:T(8,128)(2,1)} custom-call(bf16[2,128,4096]{2,1,0:T(8,128)(2,1)S(1)} %get-tuple-element.59.q_ref, f32[2,128,4096]{2,1,0:T(8,128)S(1)} %get-tuple-element.60.inside_ref, f32[2,1,4096]{2,1,0:T(1,128)S(1)} %get-tuple-element.61.gain_ref, f32[128,4096]{1,0:T(8,128)S(1)} %get-tuple-element.78.refs_0_, ...), custom_call_target="tpu_custom_call" | custom-call | flops 134217728 | bytes 7340032 | tf_op jit(solution)/shard_map/pallas_call | solution.py:498
  (38 shorter events, 8.4 us)
Async XLA Ops:
  2.5 4.9 %collective-permute-start = (bf16[16,128,128]{2,1,0:T(8,128)(2,1)S(1)}, bf16[16,128,128]{2,1,0:T(8,128)(2,1)S(1)}, u32[]{:S(2)}, u32[]{:S(2)}) collective-permute-start(bf16[16,128,128]{2,1,0:T(8,128)(2,1)S(1)} %get-tuple-element.47), channel_id=1, source_target_pairs={{0,1},{1,0},{2,3},{3,2},{4,5},{5,4},{6,7},{7,6},{8,9},{9,8},{10,11... | collective-permute-start | bytes 1572872 | tf_op jit(solution)/shard_map/ppermute | solution.py:349
  5.8 3.0 %collective-permute-start.1 = (bf16[16,128,128]{2,1,0:T(8,128)(2,1)S(1)}, bf16[16,128,128]{2,1,0:T(8,128)(2,1)S(1)}, u32[]{:S(2)}, u32[]{:S(2)}) collective-permute-start(bf16[16,128,128]{2,1,0:T(8,128)(2,1)S(1)} %get-tuple-element.48), channel_id=1, source_target_pairs={{0,1},{1,0},{2,3},{3,2},{4,5},{5,4},{6,7},{7,6},{8,9},{9,8},{10,11... | collective-permute-start | bytes 1572872 | tf_op jit(solution)/shard_map/ppermute | solution.py:349
  7.4 3.6 %copy-start = (f32[8192]{0:T(1024)S(1)}, f32[8192]{0:T(1024)}, u32[]{:S(2)}) copy-start(f32[8192]{0:T(1024)} %param.3) | copy-start | bytes 98308
  7.5 8.0 %collective-permute-start.2 = (bf16[8,128,128]{2,1,0:T(8,128)(2,1)S(1)}, bf16[8,128,128]{2,1,0:T(8,128)(2,1)S(1)}, u32[]{:S(2)}, u32[]{:S(2)}) collective-permute-start(bf16[8,128,128]{2,1,0:T(8,128)(2,1)S(1)} %get-tuple-element.55), channel_id=1, source_target_pairs={{0,2},{1,3},{2,0},{3,1},{4,6},{5,7},{6,4},{7,5},{8,10},{9,11},{10,... | collective-permute-start | bytes 786440 | tf_op jit(solution)/shard_map/ppermute | solution.py:369
  7.6 9.6 %collective-permute-start.3 = (bf16[8,128,128]{2,1,0:T(8,128)(2,1)S(1)}, bf16[8,128,128]{2,1,0:T(8,128)(2,1)S(1)}, u32[]{:S(2)}, u32[]{:S(2)}) collective-permute-start(bf16[8,128,128]{2,1,0:T(8,128)(2,1)S(1)} %get-tuple-element.56), channel_id=1, source_target_pairs={{0,6},{1,7},{2,4},{3,5},{4,2},{5,3},{6,0},{7,1},{8,14},{9,15},{10,... | collective-permute-start | bytes 786440 | tf_op jit(solution)/shard_map/ppermute | solution.py:369
  8.9 12.3 %collective-permute-start.4 = (bf16[8,128,128]{2,1,0:T(8,128)(2,1)S(1)}, bf16[8,128,128]{2,1,0:T(8,128)(2,1)S(1)}, u32[]{:S(2)}, u32[]{:S(2)}) collective-permute-start(bf16[8,128,128]{2,1,0:T(8,128)(2,1)S(1)} %get-tuple-element.57), channel_id=1, source_target_pairs={{0,4},{1,5},{2,6},{3,7},{4,0},{5,1},{6,2},{7,3},{8,12},{9,13},{10,... | collective-permute-start | bytes 786440 | tf_op jit(solution)/shard_map/ppermute | solution.py:369
  21.3 4.7 %collective-permute-start.5 = (bf16[2,128,128]{2,1,0:T(8,128)(2,1)S(1)}, bf16[2,128,128]{2,1,0:T(8,128)(2,1)S(1)}, u32[]{:S(2)}, u32[]{:S(2)}) collective-permute-start(bf16[2,128,128]{2,1,0:T(8,128)(2,1)S(1)} %get-tuple-element.67), channel_id=1, source_target_pairs={{0,8},{8,0},{16,24},{24,16},{48,56},{56,48},{32,40},{40,32},{64,72... | collective-permute-start | bytes 196616 | tf_op jit(solution)/shard_map/ppermute | solution.py:418
  23.0 5.3 %collective-permute-start.6 = (bf16[2,128,128]{2,1,0:T(8,128)(2,1)S(1)}, bf16[2,128,128]{2,1,0:T(8,128)(2,1)S(1)}, u32[]{:S(2)}, u32[]{:S(2)}) collective-permute-start(bf16[2,128,128]{2,1,0:T(8,128)(2,1)S(1)} %get-tuple-element.68), channel_id=1, source_target_pairs={{0,16},{8,24},{16,0},{24,8},{48,32},{56,40},{32,48},{40,56},{64,80... | collective-permute-start | bytes 196616 | tf_op jit(solution)/shard_map/ppermute | solution.py:418
  26.0 4.9 %collective-permute-start.7 = (bf16[2,128,128]{2,1,0:T(8,128)(2,1)S(1)}, bf16[2,128,128]{2,1,0:T(8,128)(2,1)S(1)}, u32[]{:S(2)}, u32[]{:S(2)}) collective-permute-start(bf16[2,128,128]{2,1,0:T(8,128)(2,1)S(1)} %get-tuple-element.69), channel_id=1, source_target_pairs={{0,24},{8,16},{16,8},{24,0},{48,40},{56,32},{32,56},{40,48},{64,88... | collective-permute-start | bytes 196616 | tf_op jit(solution)/shard_map/ppermute | solution.py:418
  31.0 5.7 %collective-permute-start.8 = (bf16[2,128,128]{2,1,0:T(8,128)(2,1)S(1)}, bf16[2,128,128]{2,1,0:T(8,128)(2,1)S(1)}, u32[]{:S(2)}, u32[]{:S(2)}) collective-permute-start(bf16[2,128,128]{2,1,0:T(8,128)(2,1)S(1)} %shard_map.34), channel_id=1, source_target_pairs={{0,48},{8,56},{16,32},{24,40},{32,16},{40,24},{48,0},{56,8},{64,11... | collective-permute-start | bytes 196616 | tf_op jit(solution)/shard_map/ppermute | solution.py:422
  36.7 4.5 %collective-permute-start.11 = (bf16[2,128,128]{2,1,0:T(8,128)(2,1)S(1)}, bf16[2,128,128]{2,1,0:T(8,128)(2,1)S(1)}, u32[]{:S(2)}, u32[]{:S(2)}) collective-permute-start(bf16[2,128,128]{2,1,0:T(8,128)(2,1)S(1)} %add_convert_fusion), channel_id=1, source_target_pairs={{0,192},{8,200},{16,208},{24,216},{32,224},{40,232},{48,240},{56,2... | collective-permute-start | bytes 196616 | tf_op jit(solution)/shard_map/ppermute | solution.py:424
  39.6 4.6 %collective-permute-start.10 = (bf16[2,128,128]{2,1,0:T(8,128)(2,1)S(1)}, bf16[2,128,128]{2,1,0:T(8,128)(2,1)S(1)}, u32[]{:S(2)}, u32[]{:S(2)}) collective-permute-start(bf16[2,128,128]{2,1,0:T(8,128)(2,1)S(1)} %add_convert_fusion), channel_id=1, source_target_pairs={{0,128},{8,136},{16,144},{24,152},{32,160},{40,168},{48,176},{56,1... | collective-permute-start | bytes 196616 | tf_op jit(solution)/shard_map/ppermute | solution.py:424
  39.9 4.3 %collective-permute-start.9 = (bf16[2,128,128]{2,1,0:T(8,128)(2,1)S(1)}, bf16[2,128,128]{2,1,0:T(8,128)(2,1)S(1)}, u32[]{:S(2)}, u32[]{:S(2)}) collective-permute-start(bf16[2,128,128]{2,1,0:T(8,128)(2,1)S(1)} %add_convert_fusion), channel_id=1, source_target_pairs={{0,64},{8,72},{16,80},{24,88},{32,96},{40,104},{48,112},{56,120},{... | collective-permute-start | bytes 196616 | tf_op jit(solution)/shard_map/ppermute | solution.py:424
  44.4 3.6 %collective-permute-start.12 = (bf16[2,128,128]{2,1,0:T(8,128)(2,1)S(1)}, bf16[2,128,128]{2,1,0:T(8,128)(2,1)S(1)}, u32[]{:S(2)}, u32[]{:S(2)}) collective-permute-start(bf16[2,128,128]{2,1,0:T(8,128)(2,1)S(1)} %get-tuple-element.71), channel_id=1, source_target_pairs={{0,8},{8,0},{16,24},{24,16},{48,56},{56,48},{32,40},{40,32},{64,72... | collective-permute-start | bytes 196616 | tf_op jit(solution)/shard_map/ppermute | solution.py:434
  44.9 4.1 %collective-permute-start.13 = (bf16[2,128,128]{2,1,0:T(8,128)(2,1)S(1)}, bf16[2,128,128]{2,1,0:T(8,128)(2,1)S(1)}, u32[]{:S(2)}, u32[]{:S(2)}) collective-permute-start(bf16[2,128,128]{2,1,0:T(8,128)(2,1)S(1)} %get-tuple-element.72), channel_id=1, source_target_pairs={{0,16},{8,24},{16,0},{24,8},{48,32},{56,40},{32,48},{40,56},{64,80... | collective-permute-start | bytes 196616 | tf_op jit(solution)/shard_map/ppermute | solution.py:434
  46.0 5.0 %collective-permute-start.14 = (bf16[2,128,128]{2,1,0:T(8,128)(2,1)S(1)}, bf16[2,128,128]{2,1,0:T(8,128)(2,1)S(1)}, u32[]{:S(2)}, u32[]{:S(2)}) collective-permute-start(bf16[2,128,128]{2,1,0:T(8,128)(2,1)S(1)} %get-tuple-element.73), channel_id=1, source_target_pairs={{0,24},{8,16},{16,8},{24,0},{48,40},{56,32},{32,56},{40,48},{64,88... | collective-permute-start | bytes 196616 | tf_op jit(solution)/shard_map/ppermute | solution.py:434
  51.2 11.2 %collective-permute-start.15 = (bf16[8,128,128]{2,1,0:T(8,128)(2,1)S(1)}, bf16[8,128,128]{2,1,0:T(8,128)(2,1)S(1)}, u32[]{:S(2)}, u32[]{:S(2)}) collective-permute-start(bf16[8,128,128]{2,1,0:T(8,128)(2,1)S(1)} %get-tuple-element.74), channel_id=1, source_target_pairs={{0,2},{1,3},{2,0},{3,1},{4,6},{5,7},{6,4},{7,5},{8,10},{9,11},{10,... | collective-permute-start | bytes 786440 | tf_op jit(solution)/shard_map/ppermute | solution.py:452
  51.7 12.9 %collective-permute-start.16 = (bf16[8,128,128]{2,1,0:T(8,128)(2,1)S(1)}, bf16[8,128,128]{2,1,0:T(8,128)(2,1)S(1)}, u32[]{:S(2)}, u32[]{:S(2)}) collective-permute-start(bf16[8,128,128]{2,1,0:T(8,128)(2,1)S(1)} %get-tuple-element.75), channel_id=1, source_target_pairs={{0,6},{1,7},{2,4},{3,5},{4,2},{5,3},{6,0},{7,1},{8,14},{9,15},{10,... | collective-permute-start | bytes 786440 | tf_op jit(solution)/shard_map/ppermute | solution.py:452
  53.0 14.2 %collective-permute-start.17 = (bf16[8,128,128]{2,1,0:T(8,128)(2,1)S(1)}, bf16[8,128,128]{2,1,0:T(8,128)(2,1)S(1)}, u32[]{:S(2)}, u32[]{:S(2)}) collective-permute-start(bf16[8,128,128]{2,1,0:T(8,128)(2,1)S(1)} %get-tuple-element.76), channel_id=1, source_target_pairs={{0,4},{1,5},{2,6},{3,7},{4,0},{5,1},{6,2},{7,3},{8,12},{9,13},{10,... | collective-permute-start | bytes 786440 | tf_op jit(solution)/shard_map/ppermute | solution.py:452
  54.6 15.0 %collective-permute-start.21 = (bf16[8,128,128]{2,1,0:T(8,128)(2,1)S(1)}, bf16[8,128,128]{2,1,0:T(8,128)(2,1)S(1)}, u32[]{:S(2)}, u32[]{:S(2)}) collective-permute-start(bf16[8,128,128]{2,1,0:T(8,128)(2,1)S(1)} %shard_map.41), channel_id=1, source_target_pairs={{0,1},{1,0},{2,3},{3,2},{4,5},{5,4},{6,7},{7,6},{8,9},{9,8},{10,11... | collective-permute-start | bytes 786440 | tf_op jit(solution)/shard_map/ppermute | solution.py:464
  62.4 7.1 %collective-permute-start.18 = (bf16[8,128,128]{2,1,0:T(8,128)(2,1)S(1)}, bf16[8,128,128]{2,1,0:T(8,128)(2,1)S(1)}, u32[]{:S(2)}, u32[]{:S(2)}) collective-permute-start(bf16[8,128,128]{2,1,0:T(8,128)(2,1)S(1)} %shard_map.38), channel_id=1, source_target_pairs={{0,1},{1,0},{2,3},{3,2},{4,5},{5,4},{6,7},{7,6},{8,9},{9,8},{10,11... | collective-permute-start | bytes 786440 | tf_op jit(solution)/shard_map/ppermute | solution.py:464
  64.7 4.9 %collective-permute-start.19 = (bf16[8,128,128]{2,1,0:T(8,128)(2,1)S(1)}, bf16[8,128,128]{2,1,0:T(8,128)(2,1)S(1)}, u32[]{:S(2)}, u32[]{:S(2)}) collective-permute-start(bf16[8,128,128]{2,1,0:T(8,128)(2,1)S(1)} %shard_map.39), channel_id=1, source_target_pairs={{0,1},{1,0},{2,3},{3,2},{4,5},{5,4},{6,7},{7,6},{8,9},{9,8},{10,11... | collective-permute-start | bytes 786440 | tf_op jit(solution)/shard_map/ppermute | solution.py:464
  67.3 2.9 %collective-permute-start.20 = (bf16[8,128,128]{2,1,0:T(8,128)(2,1)S(1)}, bf16[8,128,128]{2,1,0:T(8,128)(2,1)S(1)}, u32[]{:S(2)}, u32[]{:S(2)}) collective-permute-start(bf16[8,128,128]{2,1,0:T(8,128)(2,1)S(1)} %shard_map.40), channel_id=1, source_target_pairs={{0,1},{1,0},{2,3},{3,2},{4,5},{5,4},{6,7},{7,6},{8,9},{9,8},{10,11... | collective-permute-start | bytes 786440 | tf_op jit(solution)/shard_map/ppermute | solution.py:464

commit v7 on v6

--- a/solution.py
+++ b/solution.py
@@ -16,6 +16,7 @@
 
 ORDER = (1, 3, 2, 0)
 CHUNKS = 1
+BATCHES = 4
 NZ = 8
 LINE = NZ // 2
 FACING = 6
@@ -79,18 +80,18 @@
     return list(zip(*loads))
 
 
-def first_body(qkv_ref, send0_ref, send1_ref, k_ref, v_ref, own_k_ref, own_v_ref, sems):
+def first_body(qkv_ref, *refs):
+    send_refs, (k_ref, v_ref, own_k_ref, own_v_ref, sems) = refs[:-5], refs[-5:]
     place = my_place()
     pairs = start_pairs(place, qkv_ref, 1 - place[1], k_ref, v_ref, sems.at[0])
     later = start_pairs(place, qkv_ref, place[1], own_k_ref, own_v_ref, sems.at[1])
-    few = send0_ref.shape[0]
-    each = 2 * few // len(pairs)
+    few = send_refs[0].shape[0]
+    each = len(send_refs) * few // len(pairs)
     for i, pair in enumerate(pairs):
         for copy in pair:
             copy.wait()
         for h in range(i * each, (i + 1) * each):
-            send_ref = send0_ref if h < few else send1_ref
-            send_ref[h % few] = head_state(k_ref, v_ref, h).astype(BF16)
+            send_refs[h // few][h % few] = head_state(k_ref, v_ref, h).astype(BF16)
     for pair in later:
         for copy in pair:
             copy.wait()
@@ -114,8 +115,8 @@
 def inside_body(qkv_ref, *refs):
     place = my_place()
     kv_refs = refs[:4]
-    got_refs = refs[4:6]
-    gain_ref, inside_ref, q_ref, order_ref, scores_ref, sems = refs[6:]
+    got_refs = refs[4:-6]
+    gain_ref, inside_ref, q_ref, order_ref, scores_ref, sems = refs[-6:]
     few = got_refs[0].shape[0]
     rows, width = kv_refs[0].shape
     loads = [
@@ -337,28 +338,28 @@
     mib = 2**20
     matrix = jax.ShapeDtypeStruct((rows, width // 2), BF16)
     loads = pltpu.SemaphoreType.DMA((2, nx))
-    send0, send1, keys, value_rows, own_keys, own_values = call(
+    *sends, keys, value_rows, own_keys, own_values = call(
         first_body,
         [HBM],
-        [VMEM] * 6,
-        [states(half // 2)] * 2 + [matrix] * 4,
+        [VMEM] * (BATCHES + 4),
+        [states(half // BATCHES)] * BATCHES + [matrix] * 4,
         half,
         5 * mib,
         scratch=[pltpu.SemaphoreType.DMA((2, 2, nx))],
     )(qkv)
-    got = [lax.ppermute(send, "tp", swap) for send in (send0, send1)]
+    got = [lax.ppermute(send, "tp", swap) for send in sends]
     own, low = call(
         own_body, [VMEM] * 2, [VMEM] * 2, [states(half, F32), states(half)], half, 5 * mib
     )(own_keys, own_values)
     few = each // CHUNKS
     ny = nctx // NZ
     made = []
-    for i in range(2):
+    for i in range(BATCHES):
         made += call(
-            functools.partial(chip_body, i * half // 2),
+            functools.partial(chip_body, i * half // BATCHES),
             [VMEM, VMEM],
-            [VMEM] * (nx * CHUNKS // 2),
-            [states(few)] * (nx * CHUNKS // 2),
+            [VMEM] * (nx * CHUNKS // BATCHES),
+            [states(few)] * (nx * CHUNKS // BATCHES),
             0,
             2 * mib,
         )(own, got[i])
@@ -374,7 +375,7 @@
     def local(gain):
         return call(
             inside_body,
-            [HBM] + [VMEM] * 7,
+            [HBM] + [VMEM] * (5 + BATCHES),
             [VMEM] * 3,
             [
                 jax.ShapeDtypeStruct(wide, F32),

time: 72.7 us -> 72.3 us (level)
    ppermute x3, starting transfers between devices: 4.71 us -> 3.63 us  [per_device(): lax.ppermute(t, 'ctx', line(d))]
    ppermute x3, waiting for transfers between devices: 5.69 us -> 6.6 us  [per_device(): lax.ppermute(t, 'tp', shift(d))]
    ppermute x2 -> x4, starting transfers between devices: 3.42 us -> 3.93 us  [per_device(): got = [lax.ppermute(send, 'tp', swap) for send in sends]]
    pallas_call x4 -> x6, Pallas kernels: 7.17 us -> 7.19 us  [the longest x1 4.51 us: local(): call(inside_body, [HBM] + [VMEM] * (5 + BATCHES), [VMEM] * 3, [jax.ShapeD...]
  transfers between devices with their start and end apart: 22 -> 24, of which waited for: 11 -> 11; matrix products, arithmetic and copies ran while one was open for 0% -> 0% of each run, Pallas kernels for 8% -> 8%
where the time goes in v7:
time: 72.3 us; the launch traced here: 72.2 us
  starting transfers between devices  38 us (53%)
  waiting for transfers between devices  22.8 us (32%)
  Pallas kernels  11.1 us (15%)
    ppermute x4, starting transfers between devices, give(): return lax.ppermute(given, 'tp', swap)  14.4 us
    ppermute x3, waiting for transfers between devices, per_device(): lax.ppermute(t, 'tp', shift(d))  6.6 us
    ppermute x3, waiting for transfers between devices, per_device(): lax.ppermute(t, 'ctx', line(d))  4.9 us
    pallas_call x1, Pallas kernels, local(): call(inside_body, [HBM] + [VMEM] * (5 + BATCHES), [VMEM] * 3, [jax.ShapeD...  4.51 us
    ppermute x3, waiting for transfers between devices, per_device(): rows_before = [lax.ppermute(whole, 'ctx', row(d)) for d in range(1, ny)]  3.94 us
    ppermute x4, starting transfers between devices, per_device(): got = [lax.ppermute(send, 'tp', swap) for send in sends]  3.93 us
    ppermute x3, starting transfers between devices, per_device(): lax.ppermute(b, 'ctx', line(k % LINE))  3.63 us
    ppermute x3, starting transfers between devices, per_device(): lax.ppermute(t, 'ctx', line(d))  3.63 us
  transfers between devices with their start and end apart: 24, of which 11 were waited for; matrix products, arithmetic and copies ran while one was open for 0% of the time, Pallas kernels for 8%

profile of v7, /device:TPU:1, one launch (start us, length us, event | category | flops | bytes accessed | tf_op | source)
XLA Modules:
  0.0 72.2 jit_solution(2629816287155904705)
XLA Ops:
  0.0 2.5 %shard_map.28 = (bf16[8,128,128]{2,1,0:T(8,128)(2,1)S(1)}, bf16[8,128,128]{2,1,0:T(8,128)(2,1)S(1)}, bf16[8,128,128]{2,1,0:T(8,128)(2,1)S(1)}, bf16[8,128,128]{2...) custom-call(bf16[3,128,8192]{2,1,0:T(8,128)(2,1)} %bitcast.3), custom_call_target="tpu_custom_call" | custom-call | flops 134217728 | bytes 5242880 | tf_op jit(solution)/shard_map/pallas_call | solution.py:341
  2.5 3.3 %collective-permute-start = (bf16[8,128,128]{2,1,0:T(8,128)(2,1)S(1)}, bf16[8,128,128]{2,1,0:T(8,128)(2,1)S(1)}, u32[]{:S(2)}, u32[]{:S(2)}) collective-permute-start(bf16[8,128,128]{2,1,0:T(8,128)(2,1)S(1)} %get-tuple-element.45), channel_id=1, source_target_pairs={{0,1},{1,0},{2,3},{3,2},{4,5},{5,4},{6,7},{7,6},{8,9},{9,8},{10,11... | collective-permute-start | bytes 786440 | tf_op jit(solution)/shard_map/ppermute | solution.py:350
  7.4 1.1 %collective-permute-start.5 = (bf16[8,128,128]{2,1,0:T(8,128)(2,1)S(1)}, bf16[8,128,128]{2,1,0:T(8,128)(2,1)S(1)}, u32[]{:S(2)}, u32[]{:S(2)}) collective-permute-start(bf16[8,128,128]{2,1,0:T(8,128)(2,1)S(1)} %shard_map.33), channel_id=1, source_target_pairs={{0,6},{1,7},{2,4},{3,5},{4,2},{5,3},{6,0},{7,1},{8,14},{9,15},{10,... | collective-permute-start | bytes 786440 | tf_op jit(solution)/shard_map/ppermute | solution.py:370
  8.6 2.0 %collective-permute-start.6 = (bf16[8,128,128]{2,1,0:T(8,128)(2,1)S(1)}, bf16[8,128,128]{2,1,0:T(8,128)(2,1)S(1)}, u32[]{:S(2)}, u32[]{:S(2)}) collective-permute-start(bf16[8,128,128]{2,1,0:T(8,128)(2,1)S(1)} %shard_map.34), channel_id=1, source_target_pairs={{0,4},{1,5},{2,6},{3,7},{4,0},{5,1},{6,2},{7,3},{8,12},{9,13},{10,... | collective-permute-start | bytes 786440 | tf_op jit(solution)/shard_map/ppermute | solution.py:370
  10.7 4.5 %shard_map.31 = (f32[2,128,4096]{2,1,0:T(8,128)S(1)}, bf16[2,128,4096]{2,1,0:T(8,128)(2,1)S(1)}, f32[2,1,4096]{2,1,0:T(1,128)S(1)}) custom-call(bf16[3,128,8192]{2,1,0:T(8,128)(2,1)} %bitcast.4, bf16[128,4096]{1,0:T(8,128)(2,1)S(1)} %get-tuple-element.41.k_ref.refs_0_, bf16[128,4096]{1,0:T(8,128)(2,1)S(1)} %get-tuple-element.42.v_ref.refs_1_, ...), custom_call_target="tpu_custom_call" | custom-call | flops 536870912 | bytes 12582912 | tf_op jit(solution)/shard_map/pallas_call | solution.py:376
  15.3 6.6 %collective-permute-done.5.refs_1_.refs_5_ = bf16[8,128,128]{2,1,0:T(8,128)(2,1)S(1)} collective-permute-done((bf16[8,128,128]{2,1,0:T(8,128)(2,1)S(1)}, bf16[8,128,128]{2,1,0:T(8,128)(2,1)S(1)}, u32[]{:S(2)}, u32[]{:S(2)}) %collective-permute-start.5) | collective-permute-done | bytes 262176 | tf_op jit(solution)/shard_map/ppermute | solution.py:370
  22.6 3.0 %collective-permute-start.8 = (bf16[2,128,128]{2,1,0:T(8,128)(2,1)S(1)}, bf16[2,128,128]{2,1,0:T(8,128)(2,1)S(1)}, u32[]{:S(2)}, u32[]{:S(2)}) collective-permute-start(bf16[2,128,128]{2,1,0:T(8,128)(2,1)S(1)} %get-tuple-element.64), channel_id=1, source_target_pairs={{0,16},{8,24},{16,0},{24,8},{48,32},{56,40},{32,48},{40,56},{64,80... | collective-permute-start | bytes 196616 | tf_op jit(solution)/shard_map/ppermute | solution.py:419
  25.6 2.3 %collective-permute-done.8.refs_2_.refs_5_ = bf16[2,128,128]{2,1,0:T(8,128)(2,1)S(1)} collective-permute-done((bf16[2,128,128]{2,1,0:T(8,128)(2,1)S(1)}, bf16[2,128,128]{2,1,0:T(8,128)(2,1)S(1)}, u32[]{:S(2)}, u32[]{:S(2)}) %collective-permute-start.8) | collective-permute-done | bytes 65568 | tf_op jit(solution)/shard_map/ppermute | solution.py:419
  28.0 2.6 %collective-permute-done.9.refs_3_.refs_6_ = bf16[2,128,128]{2,1,0:T(8,128)(2,1)S(1)} collective-permute-done((bf16[2,128,128]{2,1,0:T(8,128)(2,1)S(1)}, bf16[2,128,128]{2,1,0:T(8,128)(2,1)S(1)}, u32[]{:S(2)}, u32[]{:S(2)}) %collective-permute-start.9) | collective-permute-done | bytes 65568 | tf_op jit(solution)/shard_map/ppermute | solution.py:419
  30.6 2.3 %collective-permute-start.10 = (bf16[2,128,128]{2,1,0:T(8,128)(2,1)S(1)}, bf16[2,128,128]{2,1,0:T(8,128)(2,1)S(1)}, u32[]{:S(2)}, u32[]{:S(2)}) collective-permute-start(bf16[2,128,128]{2,1,0:T(8,128)(2,1)S(1)} %shard_map.36), channel_id=1, source_target_pairs={{0,48},{8,56},{16,32},{24,40},{32,16},{40,24},{48,0},{56,8},{64,11... | collective-permute-start | bytes 196616 | tf_op jit(solution)/shard_map/ppermute | solution.py:423
  32.8 3.6 %collective-permute-done.10.mirror_ref = bf16[2,128,128]{2,1,0:T(8,128)(2,1)S(1)} collective-permute-done((bf16[2,128,128]{2,1,0:T(8,128)(2,1)S(1)}, bf16[2,128,128]{2,1,0:T(8,128)(2,1)S(1)}, u32[]{:S(2)}, u32[]{:S(2)}) %collective-permute-start.10) | collective-permute-done | bytes 65568 | tf_op jit(solution)/shard_map/ppermute | solution.py:423
  36.5 2.8 %collective-permute-start.13 = (bf16[2,128,128]{2,1,0:T(8,128)(2,1)S(1)}, bf16[2,128,128]{2,1,0:T(8,128)(2,1)S(1)}, u32[]{:S(2)}, u32[]{:S(2)}) collective-permute-start(bf16[2,128,128]{2,1,0:T(8,128)(2,1)S(1)} %add_convert_fusion), channel_id=1, source_target_pairs={{0,192},{8,200},{16,208},{24,216},{32,224},{40,232},{48,240},{56,2... | collective-permute-start | bytes 196616 | tf_op jit(solution)/shard_map/ppermute | solution.py:425
  40.0 1.0 %collective-permute-done.13.refs_2_ = bf16[2,128,128]{2,1,0:T(8,128)(2,1)S(1)} collective-permute-done((bf16[2,128,128]{2,1,0:T(8,128)(2,1)S(1)}, bf16[2,128,128]{2,1,0:T(8,128)(2,1)S(1)}, u32[]{:S(2)}, u32[]{:S(2)}) %collective-permute-start.13) | collective-permute-done | bytes 65568 | tf_op jit(solution)/shard_map/ppermute | solution.py:425
  41.0 3.0 %collective-permute-done.12.refs_1_ = bf16[2,128,128]{2,1,0:T(8,128)(2,1)S(1)} collective-permute-done((bf16[2,128,128]{2,1,0:T(8,128)(2,1)S(1)}, bf16[2,128,128]{2,1,0:T(8,128)(2,1)S(1)}, u32[]{:S(2)}, u32[]{:S(2)}) %collective-permute-start.12) | collective-permute-done | bytes 65568 | tf_op jit(solution)/shard_map/ppermute | solution.py:425
  44.3 1.3 %collective-permute-start.15 = (bf16[2,128,128]{2,1,0:T(8,128)(2,1)S(1)}, bf16[2,128,128]{2,1,0:T(8,128)(2,1)S(1)}, u32[]{:S(2)}, u32[]{:S(2)}) collective-permute-start(bf16[2,128,128]{2,1,0:T(8,128)(2,1)S(1)} %get-tuple-element.68), channel_id=1, source_target_pairs={{0,16},{8,24},{16,0},{24,8},{48,32},{56,40},{32,48},{40,56},{64,80... | collective-permute-start | bytes 196616 | tf_op jit(solution)/shard_map/ppermute | solution.py:435
  45.6 2.2 %collective-permute-start.16 = (bf16[2,128,128]{2,1,0:T(8,128)(2,1)S(1)}, bf16[2,128,128]{2,1,0:T(8,128)(2,1)S(1)}, u32[]{:S(2)}, u32[]{:S(2)}) collective-permute-start(bf16[2,128,128]{2,1,0:T(8,128)(2,1)S(1)} %get-tuple-element.69), channel_id=1, source_target_pairs={{0,24},{8,16},{16,8},{24,0},{48,40},{56,32},{32,56},{40,48},{64,88... | collective-permute-start | bytes 196616 | tf_op jit(solution)/shard_map/ppermute | solution.py:435
  48.6 2.0 %collective-permute-done.16.refs_3_ = bf16[2,128,128]{2,1,0:T(8,128)(2,1)S(1)} collective-permute-done((bf16[2,128,128]{2,1,0:T(8,128)(2,1)S(1)}, bf16[2,128,128]{2,1,0:T(8,128)(2,1)S(1)}, u32[]{:S(2)}, u32[]{:S(2)}) %collective-permute-start.16) | collective-permute-done | bytes 65568 | tf_op jit(solution)/shard_map/ppermute | solution.py:435
  51.3 1.4 %collective-permute-start.18 = (bf16[8,128,128]{2,1,0:T(8,128)(2,1)S(1)}, bf16[8,128,128]{2,1,0:T(8,128)(2,1)S(1)}, u32[]{:S(2)}, u32[]{:S(2)}) collective-permute-start(bf16[8,128,128]{2,1,0:T(8,128)(2,1)S(1)} %get-tuple-element.71), channel_id=1, source_target_pairs={{0,6},{1,7},{2,4},{3,5},{4,2},{5,3},{6,0},{7,1},{8,14},{9,15},{10,... | collective-permute-start | bytes 786440 | tf_op jit(solution)/shard_map/ppermute | solution.py:453
  52.8 1.3 %collective-permute-start.19 = (bf16[8,128,128]{2,1,0:T(8,128)(2,1)S(1)}, bf16[8,128,128]{2,1,0:T(8,128)(2,1)S(1)}, u32[]{:S(2)}, u32[]{:S(2)}) collective-permute-start(bf16[8,128,128]{2,1,0:T(8,128)(2,1)S(1)} %get-tuple-element.72), channel_id=1, source_target_pairs={{0,4},{1,5},{2,6},{3,7},{4,0},{5,1},{6,2},{7,3},{8,12},{9,13},{10,... | collective-permute-start | bytes 786440 | tf_op jit(solution)/shard_map/ppermute | solution.py:453
  54.1 7.9 %collective-permute-start.23 = (bf16[8,128,128]{2,1,0:T(8,128)(2,1)S(1)}, bf16[8,128,128]{2,1,0:T(8,128)(2,1)S(1)}, u32[]{:S(2)}, u32[]{:S(2)}) collective-permute-start(bf16[8,128,128]{2,1,0:T(8,128)(2,1)S(1)} %shard_map.43), channel_id=1, source_target_pairs={{0,1},{1,0},{2,3},{3,2},{4,5},{5,4},{6,7},{7,6},{8,9},{9,8},{10,11... | collective-permute-start | bytes 786440 | tf_op jit(solution)/shard_map/ppermute | solution.py:465
  62.0 2.3 %collective-permute-start.20 = (bf16[8,128,128]{2,1,0:T(8,128)(2,1)S(1)}, bf16[8,128,128]{2,1,0:T(8,128)(2,1)S(1)}, u32[]{:S(2)}, u32[]{:S(2)}) collective-permute-start(bf16[8,128,128]{2,1,0:T(8,128)(2,1)S(1)} %shard_map.40), channel_id=1, source_target_pairs={{0,1},{1,0},{2,3},{3,2},{4,5},{5,4},{6,7},{7,6},{8,9},{9,8},{10,11... | collective-permute-start | bytes 786440 | tf_op jit(solution)/shard_map/ppermute | solution.py:465
  64.3 2.5 %collective-permute-start.21 = (bf16[8,128,128]{2,1,0:T(8,128)(2,1)S(1)}, bf16[8,128,128]{2,1,0:T(8,128)(2,1)S(1)}, u32[]{:S(2)}, u32[]{:S(2)}) collective-permute-start(bf16[8,128,128]{2,1,0:T(8,128)(2,1)S(1)} %shard_map.41), channel_id=1, source_target_pairs={{0,1},{1,0},{2,3},{3,2},{4,5},{5,4},{6,7},{7,6},{8,9},{9,8},{10,11... | collective-permute-start | bytes 786440 | tf_op jit(solution)/shard_map/ppermute | solution.py:465
  66.9 1.8 %collective-permute-start.22 = (bf16[8,128,128]{2,1,0:T(8,128)(2,1)S(1)}, bf16[8,128,128]{2,1,0:T(8,128)(2,1)S(1)}, u32[]{:S(2)}, u32[]{:S(2)}) collective-permute-start(bf16[8,128,128]{2,1,0:T(8,128)(2,1)S(1)} %shard_map.42), channel_id=1, source_target_pairs={{0,1},{1,0},{2,3},{3,2},{4,5},{5,4},{6,7},{7,6},{8,9},{9,8},{10,11... | collective-permute-start | bytes 786440 | tf_op jit(solution)/shard_map/ppermute | solution.py:465
  69.8 2.3 %shard_map.44 = bf16[128,8192]{1,0:T(8,128)(2,1)} custom-call(bf16[2,128,4096]{2,1,0:T(8,128)(2,1)S(1)} %get-tuple-element.55.q_ref, f32[2,128,4096]{2,1,0:T(8,128)S(1)} %get-tuple-element.56.inside_ref, f32[2,1,4096]{2,1,0:T(1,128)S(1)} %get-tuple-element.57.gain_ref, f32[128,4096]{1,0:T(8,128)S(1)} %get-tuple-element.74.refs_0_, ...), custom_call_target="tpu_custom_call" | custom-call | flops 134217728 | bytes 7340032 | tf_op jit(solution)/shard_map/pallas_call | solution.py:499
  (44 shorter events, 6.4 us)
Async XLA Ops:
  2.5 4.5 %collective-permute-start = (bf16[8,128,128]{2,1,0:T(8,128)(2,1)S(1)}, bf16[8,128,128]{2,1,0:T(8,128)(2,1)S(1)}, u32[]{:S(2)}, u32[]{:S(2)}) collective-permute-start(bf16[8,128,128]{2,1,0:T(8,128)(2,1)S(1)} %get-tuple-element.45), channel_id=1, source_target_pairs={{0,1},{1,0},{2,3},{3,2},{4,5},{5,4},{6,7},{7,6},{8,9},{9,8},{10,11... | collective-permute-start | bytes 786440 | tf_op jit(solution)/shard_map/ppermute | solution.py:350
  5.8 1.5 %collective-permute-start.1 = (bf16[8,128,128]{2,1,0:T(8,128)(2,1)S(1)}, bf16[8,128,128]{2,1,0:T(8,128)(2,1)S(1)}, u32[]{:S(2)}, u32[]{:S(2)}) collective-permute-start(bf16[8,128,128]{2,1,0:T(8,128)(2,1)S(1)} %get-tuple-element.46), channel_id=1, source_target_pairs={{0,1},{1,0},{2,3},{3,2},{4,5},{5,4},{6,7},{7,6},{8,9},{9,8},{10,11... | collective-permute-start | bytes 786440 | tf_op jit(solution)/shard_map/ppermute | solution.py:350
  5.9 2.6 %collective-permute-start.2 = (bf16[8,128,128]{2,1,0:T(8,128)(2,1)S(1)}, bf16[8,128,128]{2,1,0:T(8,128)(2,1)S(1)}, u32[]{:S(2)}, u32[]{:S(2)}) collective-permute-start(bf16[8,128,128]{2,1,0:T(8,128)(2,1)S(1)} %get-tuple-element.47), channel_id=1, source_target_pairs={{0,1},{1,0},{2,3},{3,2},{4,5},{5,4},{6,7},{7,6},{8,9},{9,8},{10,11... | collective-permute-start | bytes 786440 | tf_op jit(solution)/shard_map/ppermute | solution.py:350
  6.3 4.3 %collective-permute-start.3 = (bf16[8,128,128]{2,1,0:T(8,128)(2,1)S(1)}, bf16[8,128,128]{2,1,0:T(8,128)(2,1)S(1)}, u32[]{:S(2)}, u32[]{:S(2)}) collective-permute-start(bf16[8,128,128]{2,1,0:T(8,128)(2,1)S(1)} %get-tuple-element.48), channel_id=1, source_target_pairs={{0,1},{1,0},{2,3},{3,2},{4,5},{5,4},{6,7},{7,6},{8,9},{9,8},{10,11... | collective-permute-start | bytes 786440 | tf_op jit(solution)/shard_map/ppermute | solution.py:350
  7.0 8.2 %collective-permute-start.4 = (bf16[8,128,128]{2,1,0:T(8,128)(2,1)S(1)}, bf16[8,128,128]{2,1,0:T(8,128)(2,1)S(1)}, u32[]{:S(2)}, u32[]{:S(2)}) collective-permute-start(bf16[8,128,128]{2,1,0:T(8,128)(2,1)S(1)} %shard_map.32), channel_id=1, source_target_pairs={{0,2},{1,3},{2,0},{3,1},{4,6},{5,7},{6,4},{7,5},{8,10},{9,11},{10,... | collective-permute-start | bytes 786440 | tf_op jit(solution)/shard_map/ppermute | solution.py:370
  7.4 14.4 %collective-permute-start.5 = (bf16[8,128,128]{2,1,0:T(8,128)(2,1)S(1)}, bf16[8,128,128]{2,1,0:T(8,128)(2,1)S(1)}, u32[]{:S(2)}, u32[]{:S(2)}) collective-permute-start(bf16[8,128,128]{2,1,0:T(8,128)(2,1)S(1)} %shard_map.33), channel_id=1, source_target_pairs={{0,6},{1,7},{2,4},{3,5},{4,2},{5,3},{6,0},{7,1},{8,14},{9,15},{10,... | collective-permute-start | bytes 786440 | tf_op jit(solution)/shard_map/ppermute | solution.py:370
  8.6 13.2 %collective-permute-start.6 = (bf16[8,128,128]{2,1,0:T(8,128)(2,1)S(1)}, bf16[8,128,128]{2,1,0:T(8,128)(2,1)S(1)}, u32[]{:S(2)}, u32[]{:S(2)}) collective-permute-start(bf16[8,128,128]{2,1,0:T(8,128)(2,1)S(1)} %shard_map.34), channel_id=1, source_target_pairs={{0,4},{1,5},{2,6},{3,7},{4,0},{5,1},{6,2},{7,3},{8,12},{9,13},{10,... | collective-permute-start | bytes 786440 | tf_op jit(solution)/shard_map/ppermute | solution.py:370
  22.0 3.6 %collective-permute-start.7 = (bf16[2,128,128]{2,1,0:T(8,128)(2,1)S(1)}, bf16[2,128,128]{2,1,0:T(8,128)(2,1)S(1)}, u32[]{:S(2)}, u32[]{:S(2)}) collective-permute-start(bf16[2,128,128]{2,1,0:T(8,128)(2,1)S(1)} %get-tuple-element.63), channel_id=1, source_target_pairs={{0,8},{8,0},{16,24},{24,16},{48,56},{56,48},{32,40},{40,32},{64,72... | collective-permute-start | bytes 196616 | tf_op jit(solution)/shard_map/ppermute | solution.py:419
  22.6 5.3 %collective-permute-start.8 = (bf16[2,128,128]{2,1,0:T(8,128)(2,1)S(1)}, bf16[2,128,128]{2,1,0:T(8,128)(2,1)S(1)}, u32[]{:S(2)}, u32[]{:S(2)}) collective-permute-start(bf16[2,128,128]{2,1,0:T(8,128)(2,1)S(1)} %get-tuple-element.64), channel_id=1, source_target_pairs={{0,16},{8,24},{16,0},{24,8},{48,32},{56,40},{32,48},{40,56},{64,80... | collective-permute-start | bytes 196616 | tf_op jit(solution)/shard_map/ppermute | solution.py:419
  25.6 4.9 %collective-permute-start.9 = (bf16[2,128,128]{2,1,0:T(8,128)(2,1)S(1)}, bf16[2,128,128]{2,1,0:T(8,128)(2,1)S(1)}, u32[]{:S(2)}, u32[]{:S(2)}) collective-permute-start(bf16[2,128,128]{2,1,0:T(8,128)(2,1)S(1)} %get-tuple-element.65), channel_id=1, source_target_pairs={{0,24},{8,16},{16,8},{24,0},{48,40},{56,32},{32,56},{40,48},{64,88... | collective-permute-start | bytes 196616 | tf_op jit(solution)/shard_map/ppermute | solution.py:419
  30.6 5.9 %collective-permute-start.10 = (bf16[2,128,128]{2,1,0:T(8,128)(2,1)S(1)}, bf16[2,128,128]{2,1,0:T(8,128)(2,1)S(1)}, u32[]{:S(2)}, u32[]{:S(2)}) collective-permute-start(bf16[2,128,128]{2,1,0:T(8,128)(2,1)S(1)} %shard_map.36), channel_id=1, source_target_pairs={{0,48},{8,56},{16,32},{24,40},{32,16},{40,24},{48,0},{56,8},{64,11... | collective-permute-start | bytes 196616 | tf_op jit(solution)/shard_map/ppermute | solution.py:423
  36.5 4.5 %collective-permute-start.13 = (bf16[2,128,128]{2,1,0:T(8,128)(2,1)S(1)}, bf16[2,128,128]{2,1,0:T(8,128)(2,1)S(1)}, u32[]{:S(2)}, u32[]{:S(2)}) collective-permute-start(bf16[2,128,128]{2,1,0:T(8,128)(2,1)S(1)} %add_convert_fusion), channel_id=1, source_target_pairs={{0,192},{8,200},{16,208},{24,216},{32,224},{40,232},{48,240},{56,2... | collective-permute-start | bytes 196616 | tf_op jit(solution)/shard_map/ppermute | solution.py:425
  39.3 4.6 %collective-permute-start.12 = (bf16[2,128,128]{2,1,0:T(8,128)(2,1)S(1)}, bf16[2,128,128]{2,1,0:T(8,128)(2,1)S(1)}, u32[]{:S(2)}, u32[]{:S(2)}) collective-permute-start(bf16[2,128,128]{2,1,0:T(8,128)(2,1)S(1)} %add_convert_fusion), channel_id=1, source_target_pairs={{0,128},{8,136},{16,144},{24,152},{32,160},{40,168},{48,176},{56,1... | collective-permute-start | bytes 196616 | tf_op jit(solution)/shard_map/ppermute | solution.py:425
  39.7 4.3 %collective-permute-start.11 = (bf16[2,128,128]{2,1,0:T(8,128)(2,1)S(1)}, bf16[2,128,128]{2,1,0:T(8,128)(2,1)S(1)}, u32[]{:S(2)}, u32[]{:S(2)}) collective-permute-start(bf16[2,128,128]{2,1,0:T(8,128)(2,1)S(1)} %add_convert_fusion), channel_id=1, source_target_pairs={{0,64},{8,72},{16,80},{24,88},{32,96},{40,104},{48,112},{56,120},{... | collective-permute-start | bytes 196616 | tf_op jit(solution)/shard_map/ppermute | solution.py:425
  44.1 3.6 %collective-permute-start.14 = (bf16[2,128,128]{2,1,0:T(8,128)(2,1)S(1)}, bf16[2,128,128]{2,1,0:T(8,128)(2,1)S(1)}, u32[]{:S(2)}, u32[]{:S(2)}) collective-permute-start(bf16[2,128,128]{2,1,0:T(8,128)(2,1)S(1)} %get-tuple-element.67), channel_id=1, source_target_pairs={{0,8},{8,0},{16,24},{24,16},{48,56},{56,48},{32,40},{40,32},{64,72... | collective-permute-start | bytes 196616 | tf_op jit(solution)/shard_map/ppermute | solution.py:435
  44.3 4.3 %collective-permute-start.15 = (bf16[2,128,128]{2,1,0:T(8,128)(2,1)S(1)}, bf16[2,128,128]{2,1,0:T(8,128)(2,1)S(1)}, u32[]{:S(2)}, u32[]{:S(2)}) collective-permute-start(bf16[2,128,128]{2,1,0:T(8,128)(2,1)S(1)} %get-tuple-element.68), channel_id=1, source_target_pairs={{0,16},{8,24},{16,0},{24,8},{48,32},{56,40},{32,48},{40,56},{64,80... | collective-permute-start | bytes 196616 | tf_op jit(solution)/shard_map/ppermute | solution.py:435
  45.6 5.0 %collective-permute-start.16 = (bf16[2,128,128]{2,1,0:T(8,128)(2,1)S(1)}, bf16[2,128,128]{2,1,0:T(8,128)(2,1)S(1)}, u32[]{:S(2)}, u32[]{:S(2)}) collective-permute-start(bf16[2,128,128]{2,1,0:T(8,128)(2,1)S(1)} %get-tuple-element.69), channel_id=1, source_target_pairs={{0,24},{8,16},{16,8},{24,0},{48,40},{56,32},{32,56},{40,48},{64,88... | collective-permute-start | bytes 196616 | tf_op jit(solution)/shard_map/ppermute | solution.py:435
  50.8 11.3 %collective-permute-start.17 = (bf16[8,128,128]{2,1,0:T(8,128)(2,1)S(1)}, bf16[8,128,128]{2,1,0:T(8,128)(2,1)S(1)}, u32[]{:S(2)}, u32[]{:S(2)}) collective-permute-start(bf16[8,128,128]{2,1,0:T(8,128)(2,1)S(1)} %get-tuple-element.70), channel_id=1, source_target_pairs={{0,2},{1,3},{2,0},{3,1},{4,6},{5,7},{6,4},{7,5},{8,10},{9,11},{10,... | collective-permute-start | bytes 786440 | tf_op jit(solution)/shard_map/ppermute | solution.py:453
  51.3 13.0 %collective-permute-start.18 = (bf16[8,128,128]{2,1,0:T(8,128)(2,1)S(1)}, bf16[8,128,128]{2,1,0:T(8,128)(2,1)S(1)}, u32[]{:S(2)}, u32[]{:S(2)}) collective-permute-start(bf16[8,128,128]{2,1,0:T(8,128)(2,1)S(1)} %get-tuple-element.71), channel_id=1, source_target_pairs={{0,6},{1,7},{2,4},{3,5},{4,2},{5,3},{6,0},{7,1},{8,14},{9,15},{10,... | collective-permute-start | bytes 786440 | tf_op jit(solution)/shard_map/ppermute | solution.py:453
  52.8 14.1 %collective-permute-start.19 = (bf16[8,128,128]{2,1,0:T(8,128)(2,1)S(1)}, bf16[8,128,128]{2,1,0:T(8,128)(2,1)S(1)}, u32[]{:S(2)}, u32[]{:S(2)}) collective-permute-start(bf16[8,128,128]{2,1,0:T(8,128)(2,1)S(1)} %get-tuple-element.72), channel_id=1, source_target_pairs={{0,4},{1,5},{2,6},{3,7},{4,0},{5,1},{6,2},{7,3},{8,12},{9,13},{10,... | collective-permute-start | bytes 786440 | tf_op jit(solution)/shard_map/ppermute | solution.py:453
  54.1 15.0 %collective-permute-start.23 = (bf16[8,128,128]{2,1,0:T(8,128)(2,1)S(1)}, bf16[8,128,128]{2,1,0:T(8,128)(2,1)S(1)}, u32[]{:S(2)}, u32[]{:S(2)}) collective-permute-start(bf16[8,128,128]{2,1,0:T(8,128)(2,1)S(1)} %shard_map.43), channel_id=1, source_target_pairs={{0,1},{1,0},{2,3},{3,2},{4,5},{5,4},{6,7},{7,6},{8,9},{9,8},{10,11... | collective-permute-start | bytes 786440 | tf_op jit(solution)/shard_map/ppermute | solution.py:465
  62.0 7.1 %collective-permute-start.20 = (bf16[8,128,128]{2,1,0:T(8,128)(2,1)S(1)}, bf16[8,128,128]{2,1,0:T(8,128)(2,1)S(1)}, u32[]{:S(2)}, u32[]{:S(2)}) collective-permute-start(bf16[8,128,128]{2,1,0:T(8,128)(2,1)S(1)} %shard_map.40), channel_id=1, source_target_pairs={{0,1},{1,0},{2,3},{3,2},{4,5},{5,4},{6,7},{7,6},{8,9},{9,8},{10,11... | collective-permute-start | bytes 786440 | tf_op jit(solution)/shard_map/ppermute | solution.py:465
  64.3 4.9 %collective-permute-start.21 = (bf16[8,128,128]{2,1,0:T(8,128)(2,1)S(1)}, bf16[8,128,128]{2,1,0:T(8,128)(2,1)S(1)}, u32[]{:S(2)}, u32[]{:S(2)}) collective-permute-start(bf16[8,128,128]{2,1,0:T(8,128)(2,1)S(1)} %shard_map.41), channel_id=1, source_target_pairs={{0,1},{1,0},{2,3},{3,2},{4,5},{5,4},{6,7},{7,6},{8,9},{9,8},{10,11... | collective-permute-start | bytes 786440 | tf_op jit(solution)/shard_map/ppermute | solution.py:465
  66.9 2.9 %collective-permute-start.22 = (bf16[8,128,128]{2,1,0:T(8,128)(2,1)S(1)}, bf16[8,128,128]{2,1,0:T(8,128)(2,1)S(1)}, u32[]{:S(2)}, u32[]{:S(2)}) collective-permute-start(bf16[8,128,128]{2,1,0:T(8,128)(2,1)S(1)} %shard_map.42), channel_id=1, source_target_pairs={{0,1},{1,0},{2,3},{3,2},{4,5},{5,4},{6,7},{7,6},{8,9},{9,8},{10,11... | collective-permute-start | bytes 786440 | tf_op jit(solution)/shard_map/ppermute | solution.py:465
  (1 other events, 3.3 us)

commit v8 on v6

--- a/solution.py
+++ b/solution.py
@@ -288,8 +288,9 @@
     meansq = jnp.sum(total, axis=-1, keepdims=True) / out_ref.shape[1]
     scale = jnp.broadcast_to(lax.rsqrt(meansq + 1e-06), total.shape)
     copies = []
-    for (side, chunk), source in zip(sources, (*kept, other)):
-        for i, d in enumerate(ORDER):
+    for (side, chunk, blocks), source in zip(sources, (*kept, other)):
+        for i, block in enumerate(blocks):
+            d = ORDER[block]
             slot = len(copies)
             for h in range(few):
                 value = source[:, head_cols(i * few + h)]
@@ -472,38 +473,38 @@
         own_heads = [
             (i * each + c * few + h, i, h) for i in range(nx) for h in range(few)
         ]
+        soon, late = [0, nx - 1], list(range(1, nx - 1))
         other_heads = [
-            (i * each + c * few + h, g, k * few + h)
-            for g, group in enumerate(groups)
-            for k, i in enumerate(group)
-            for h in range(few)
+            [(i * each + c * few + h, g, h) for g, i in enumerate(which) for h in range(few)]
+            for which in (soon, late)
         ]
-        sides = [(0, 0, nx, own_heads)]
-        if not last:
-            sides.append((1, nx, len(others), other_heads))
-        sources += [(side[0], c) for side in sides]
-        priors = parts[c] + ([] if last else others)
-        out = jax.ShapeDtypeStruct((rows, nx * few * DH), F32)
+        sides = [(0, 0, nx, own_heads), (1, nx, len(soon), other_heads[0])]
+        sources += [(0, c, list(range(nx))), (1, c, soon)]
+        priors = parts[c] + [others[i] for i in soon]
+        outs = [
+            jax.ShapeDtypeStruct((rows, len(heads) * DH), F32) for _, _, _, heads in sides
+        ]
         *outs, sq = call(
             functools.partial(attend_body, sides),
             [VMEM] * (3 + len(priors)),
             [VMEM] * (len(sides) + 1),
-            [out] * len(sides) + [square],
+            outs + [square],
             half,
             5 * mib,
         )(queries, inside, gains, *priors)
         kept += outs
         sqs.append(sq)
-    sources.append((1, CHUNKS - 1))
+    sources.append((1, CHUNKS - 1, late))
+    others = [others[i] for i in late]
     return call(
-        functools.partial(finish_body, other_heads, sources, few),
+        functools.partial(finish_body, other_heads[1], sources, few),
         [VMEM] * (3 + len(kept) + len(sqs) + len(others)),
         HBM,
         jax.ShapeDtypeStruct((rows, width), BF16),
         half,
         7 * mib,
         scratch=[
-            pltpu.VMEM((rows, nx * few * DH), F32),
+            pltpu.VMEM((rows, len(late) * few * DH), F32),
             pltpu.VMEM((2 * nx * CHUNKS, rows, few * DH), BF16),
             pltpu.SemaphoreType.DMA((2 * nx * CHUNKS,)),
         ],

time: 72.7 us -> 72.3 us (level)
  no operation moved by 1% of the time
where the time goes in v8:
time: 72.3 us; the launch traced here: 72.2 us
  starting transfers between devices  38.7 us (54%)
  waiting for transfers between devices  22.4 us (31%)
  Pallas kernels  10.9 us (15%)
    ppermute x4, starting transfers between devices, give(): return lax.ppermute(given, 'tp', swap)  14.3 us
    ppermute x3, waiting for transfers between devices, per_device(): lax.ppermute(t, 'tp', shift(d))  5.69 us
    ppermute x3, waiting for transfers between devices, per_device(): lax.ppermute(t, 'ctx', line(d))  4.91 us
    ppermute x3, starting transfers between devices, per_device(): lax.ppermute(t, 'ctx', line(d))  4.71 us
    pallas_call x1, Pallas kernels, local(): call(inside_body, [HBM] + [VMEM] * 7, [VMEM] * 3, [jax.ShapeDtypeStruct(w...  4.5 us
    ppermute x3, waiting for transfers between devices, per_device(): rows_before = [lax.ppermute(whole, 'ctx', row(d)) for d in range(1, ny)]  3.94 us
    ppermute x3, starting transfers between devices, per_device(): lax.ppermute(b, 'ctx', line(k % LINE))  3.63 us
    ppermute x3, starting transfers between devices, per_device(): rows_before = [lax.ppermute(whole, 'ctx', row(d)) for d in range(1, ny)]  3.5 us
  transfers between devices with their start and end apart: 22, of which 11 were waited for; matrix products, arithmetic and copies ran while one was open for 0% of the time, Pallas kernels for 8%

profile of v8, /device:TPU:1, one launch (start us, length us, event | category | flops | bytes accessed | tf_op | source)
XLA Modules:
  0.0 72.2 jit_solution(12134811160235941161)
XLA Ops:
  0.0 2.5 %shard_map.28 = (bf16[16,128,128]{2,1,0:T(8,128)(2,1)S(1)}, bf16[16,128,128]{2,1,0:T(8,128)(2,1)S(1)}, bf16[128,4096]{1,0:T(8,128)(2,1)S(1)}, bf16[128,4096]{1,0...) custom-call(bf16[3,128,8192]{2,1,0:T(8,128)(2,1)} %bitcast.3), custom_call_target="tpu_custom_call" | custom-call | flops 134217728 | bytes 5242880 | tf_op jit(solution)/shard_map/pallas_call | solution.py:341
  2.5 3.3 %collective-permute-start = (bf16[16,128,128]{2,1,0:T(8,128)(2,1)S(1)}, bf16[16,128,128]{2,1,0:T(8,128)(2,1)S(1)}, u32[]{:S(2)}, u32[]{:S(2)}) collective-permute-start(bf16[16,128,128]{2,1,0:T(8,128)(2,1)S(1)} %get-tuple-element.48), channel_id=1, source_target_pairs={{0,1},{1,0},{2,3},{3,2},{4,5},{5,4},{6,7},{7,6},{8,9},{9,8},{10,11... | collective-permute-start | bytes 1572872 | tf_op jit(solution)/shard_map/ppermute | solution.py:350
  7.6 1.3 %collective-permute-start.3 = (bf16[8,128,128]{2,1,0:T(8,128)(2,1)S(1)}, bf16[8,128,128]{2,1,0:T(8,128)(2,1)S(1)}, u32[]{:S(2)}, u32[]{:S(2)}) collective-permute-start(bf16[8,128,128]{2,1,0:T(8,128)(2,1)S(1)} %get-tuple-element.57), channel_id=1, source_target_pairs={{0,6},{1,7},{2,4},{3,5},{4,2},{5,3},{6,0},{7,1},{8,14},{9,15},{10,... | collective-permute-start | bytes 786440 | tf_op jit(solution)/shard_map/ppermute | solution.py:370
  8.9 2.0 %collective-permute-start.4 = (bf16[8,128,128]{2,1,0:T(8,128)(2,1)S(1)}, bf16[8,128,128]{2,1,0:T(8,128)(2,1)S(1)}, u32[]{:S(2)}, u32[]{:S(2)}) collective-permute-start(bf16[8,128,128]{2,1,0:T(8,128)(2,1)S(1)} %get-tuple-element.58), channel_id=1, source_target_pairs={{0,4},{1,5},{2,6},{3,7},{4,0},{5,1},{6,2},{7,3},{8,12},{9,13},{10,... | collective-permute-start | bytes 786440 | tf_op jit(solution)/shard_map/ppermute | solution.py:370
  11.0 4.5 %shard_map.31 = (f32[2,128,4096]{2,1,0:T(8,128)S(1)}, bf16[2,128,4096]{2,1,0:T(8,128)(2,1)S(1)}, f32[2,1,4096]{2,1,0:T(1,128)S(1)}) custom-call(bf16[3,128,8192]{2,1,0:T(8,128)(2,1)} %bitcast.4, bf16[128,4096]{1,0:T(8,128)(2,1)S(1)} %get-tuple-element.44.k_ref.refs_0_, bf16[128,4096]{1,0:T(8,128)(2,1)S(1)} %get-tuple-element.45.v_ref.refs_1_, ...), custom_call_target="tpu_custom_call" | custom-call | flops 536870912 | bytes 12582912 | tf_op jit(solution)/shard_map/pallas_call | solution.py:376
  15.5 1.7 %collective-permute-done.3.refs_1_.refs_5_ = bf16[8,128,128]{2,1,0:T(8,128)(2,1)S(1)} collective-permute-done((bf16[8,128,128]{2,1,0:T(8,128)(2,1)S(1)}, bf16[8,128,128]{2,1,0:T(8,128)(2,1)S(1)}, u32[]{:S(2)}, u32[]{:S(2)}) %collective-permute-start.3) | collective-permute-done | bytes 262176 | tf_op jit(solution)/shard_map/ppermute | solution.py:370
  17.2 4.0 %collective-permute-done.4.refs_2_.refs_6_ = bf16[8,128,128]{2,1,0:T(8,128)(2,1)S(1)} collective-permute-done((bf16[8,128,128]{2,1,0:T(8,128)(2,1)S(1)}, bf16[8,128,128]{2,1,0:T(8,128)(2,1)S(1)}, u32[]{:S(2)}, u32[]{:S(2)}) %collective-permute-start.4) | collective-permute-done | bytes 262176 | tf_op jit(solution)/shard_map/ppermute | solution.py:370
  21.3 1.7 %collective-permute-start.5 = (bf16[2,128,128]{2,1,0:T(8,128)(2,1)S(1)}, bf16[2,128,128]{2,1,0:T(8,128)(2,1)S(1)}, u32[]{:S(2)}, u32[]{:S(2)}) collective-permute-start(bf16[2,128,128]{2,1,0:T(8,128)(2,1)S(1)} %get-tuple-element.68), channel_id=1, source_target_pairs={{0,8},{8,0},{16,24},{24,16},{48,56},{56,48},{32,40},{40,32},{64,72... | collective-permute-start | bytes 196616 | tf_op jit(solution)/shard_map/ppermute | solution.py:419
  23.0 3.0 %collective-permute-start.6 = (bf16[2,128,128]{2,1,0:T(8,128)(2,1)S(1)}, bf16[2,128,128]{2,1,0:T(8,128)(2,1)S(1)}, u32[]{:S(2)}, u32[]{:S(2)}) collective-permute-start(bf16[2,128,128]{2,1,0:T(8,128)(2,1)S(1)} %get-tuple-element.69), channel_id=1, source_target_pairs={{0,16},{8,24},{16,0},{24,8},{48,32},{56,40},{32,48},{40,56},{64,80... | collective-permute-start | bytes 196616 | tf_op jit(solution)/shard_map/ppermute | solution.py:419
  26.0 2.3 %collective-permute-done.6.refs_2_.refs_5_ = bf16[2,128,128]{2,1,0:T(8,128)(2,1)S(1)} collective-permute-done((bf16[2,128,128]{2,1,0:T(8,128)(2,1)S(1)}, bf16[2,128,128]{2,1,0:T(8,128)(2,1)S(1)}, u32[]{:S(2)}, u32[]{:S(2)}) %collective-permute-start.6) | collective-permute-done | bytes 65568 | tf_op jit(solution)/shard_map/ppermute | solution.py:419
  28.4 2.6 %collective-permute-done.7.refs_3_.refs_6_ = bf16[2,128,128]{2,1,0:T(8,128)(2,1)S(1)} collective-permute-done((bf16[2,128,128]{2,1,0:T(8,128)(2,1)S(1)}, bf16[2,128,128]{2,1,0:T(8,128)(2,1)S(1)}, u32[]{:S(2)}, u32[]{:S(2)}) %collective-permute-start.7) | collective-permute-done | bytes 65568 | tf_op jit(solution)/shard_map/ppermute | solution.py:419
  31.0 2.3 %collective-permute-start.8 = (bf16[2,128,128]{2,1,0:T(8,128)(2,1)S(1)}, bf16[2,128,128]{2,1,0:T(8,128)(2,1)S(1)}, u32[]{:S(2)}, u32[]{:S(2)}) collective-permute-start(bf16[2,128,128]{2,1,0:T(8,128)(2,1)S(1)} %shard_map.34), channel_id=1, source_target_pairs={{0,48},{8,56},{16,32},{24,40},{32,16},{40,24},{48,0},{56,8},{64,11... | collective-permute-start | bytes 196616 | tf_op jit(solution)/shard_map/ppermute | solution.py:423
  33.3 3.5 %collective-permute-done.8.mirror_ref = bf16[2,128,128]{2,1,0:T(8,128)(2,1)S(1)} collective-permute-done((bf16[2,128,128]{2,1,0:T(8,128)(2,1)S(1)}, bf16[2,128,128]{2,1,0:T(8,128)(2,1)S(1)}, u32[]{:S(2)}, u32[]{:S(2)}) %collective-permute-start.8) | collective-permute-done | bytes 65568 | tf_op jit(solution)/shard_map/ppermute | solution.py:423
  36.7 2.8 %collective-permute-start.11 = (bf16[2,128,128]{2,1,0:T(8,128)(2,1)S(1)}, bf16[2,128,128]{2,1,0:T(8,128)(2,1)S(1)}, u32[]{:S(2)}, u32[]{:S(2)}) collective-permute-start(bf16[2,128,128]{2,1,0:T(8,128)(2,1)S(1)} %add_convert_fusion), channel_id=1, source_target_pairs={{0,192},{8,200},{16,208},{24,216},{32,224},{40,232},{48,240},{56,2... | collective-permute-start | bytes 196616 | tf_op jit(solution)/shard_map/ppermute | solution.py:425
  41.2 3.0 %collective-permute-done.10.refs_1_ = bf16[2,128,128]{2,1,0:T(8,128)(2,1)S(1)} collective-permute-done((bf16[2,128,128]{2,1,0:T(8,128)(2,1)S(1)}, bf16[2,128,128]{2,1,0:T(8,128)(2,1)S(1)}, u32[]{:S(2)}, u32[]{:S(2)}) %collective-permute-start.10) | collective-permute-done | bytes 65568 | tf_op jit(solution)/shard_map/ppermute | solution.py:425
  46.0 2.0 %collective-permute-start.14 = (bf16[2,128,128]{2,1,0:T(8,128)(2,1)S(1)}, bf16[2,128,128]{2,1,0:T(8,128)(2,1)S(1)}, u32[]{:S(2)}, u32[]{:S(2)}) collective-permute-start(bf16[2,128,128]{2,1,0:T(8,128)(2,1)S(1)} %get-tuple-element.74), channel_id=1, source_target_pairs={{0,24},{8,16},{16,8},{24,0},{48,40},{56,32},{32,56},{40,48},{64,88... | collective-permute-start | bytes 196616 | tf_op jit(solution)/shard_map/ppermute | solution.py:435
  49.0 2.0 %collective-permute-done.14.refs_3_ = bf16[2,128,128]{2,1,0:T(8,128)(2,1)S(1)} collective-permute-done((bf16[2,128,128]{2,1,0:T(8,128)(2,1)S(1)}, bf16[2,128,128]{2,1,0:T(8,128)(2,1)S(1)}, u32[]{:S(2)}, u32[]{:S(2)}) %collective-permute-start.14) | collective-permute-done | bytes 65568 | tf_op jit(solution)/shard_map/ppermute | solution.py:435
  51.7 1.3 %collective-permute-start.16 = (bf16[8,128,128]{2,1,0:T(8,128)(2,1)S(1)}, bf16[8,128,128]{2,1,0:T(8,128)(2,1)S(1)}, u32[]{:S(2)}, u32[]{:S(2)}) collective-permute-start(bf16[8,128,128]{2,1,0:T(8,128)(2,1)S(1)} %get-tuple-element.76), channel_id=1, source_target_pairs={{0,6},{1,7},{2,4},{3,5},{4,2},{5,3},{6,0},{7,1},{8,14},{9,15},{10,... | collective-permute-start | bytes 786440 | tf_op jit(solution)/shard_map/ppermute | solution.py:453
  53.0 1.6 %collective-permute-start.17 = (bf16[8,128,128]{2,1,0:T(8,128)(2,1)S(1)}, bf16[8,128,128]{2,1,0:T(8,128)(2,1)S(1)}, u32[]{:S(2)}, u32[]{:S(2)}) collective-permute-start(bf16[8,128,128]{2,1,0:T(8,128)(2,1)S(1)} %get-tuple-element.77), channel_id=1, source_target_pairs={{0,4},{1,5},{2,6},{3,7},{4,0},{5,1},{6,2},{7,3},{8,12},{9,13},{10,... | collective-permute-start | bytes 786440 | tf_op jit(solution)/shard_map/ppermute | solution.py:453
  54.6 7.8 %collective-permute-start.19 = (bf16[8,128,128]{2,1,0:T(8,128)(2,1)S(1)}, bf16[8,128,128]{2,1,0:T(8,128)(2,1)S(1)}, u32[]{:S(2)}, u32[]{:S(2)}) collective-permute-start(bf16[8,128,128]{2,1,0:T(8,128)(2,1)S(1)} %shard_map.38), channel_id=1, source_target_pairs={{0,1},{1,0},{2,3},{3,2},{4,5},{5,4},{6,7},{7,6},{8,9},{9,8},{10,11... | collective-permute-start | bytes 786440 | tf_op jit(solution)/shard_map/ppermute | solution.py:465
  62.4 2.3 %collective-permute-start.18 = (bf16[8,128,128]{2,1,0:T(8,128)(2,1)S(1)}, bf16[8,128,128]{2,1,0:T(8,128)(2,1)S(1)}, u32[]{:S(2)}, u32[]{:S(2)}) collective-permute-start(bf16[8,128,128]{2,1,0:T(8,128)(2,1)S(1)} %shard_map.37), channel_id=1, source_target_pairs={{0,1},{1,0},{2,3},{3,2},{4,5},{5,4},{6,7},{7,6},{8,9},{9,8},{10,11... | collective-permute-start | bytes 786440 | tf_op jit(solution)/shard_map/ppermute | solution.py:465
  64.7 2.5 %collective-permute-start.20 = (bf16[8,128,128]{2,1,0:T(8,128)(2,1)S(1)}, bf16[8,128,128]{2,1,0:T(8,128)(2,1)S(1)}, u32[]{:S(2)}, u32[]{:S(2)}) collective-permute-start(bf16[8,128,128]{2,1,0:T(8,128)(2,1)S(1)} %shard_map.40), channel_id=1, source_target_pairs={{0,1},{1,0},{2,3},{3,2},{4,5},{5,4},{6,7},{7,6},{8,9},{9,8},{10,11... | collective-permute-start | bytes 786440 | tf_op jit(solution)/shard_map/ppermute | solution.py:465
  67.3 1.8 %collective-permute-start.21 = (bf16[8,128,128]{2,1,0:T(8,128)(2,1)S(1)}, bf16[8,128,128]{2,1,0:T(8,128)(2,1)S(1)}, u32[]{:S(2)}, u32[]{:S(2)}) collective-permute-start(bf16[8,128,128]{2,1,0:T(8,128)(2,1)S(1)} %shard_map.41), channel_id=1, source_target_pairs={{0,1},{1,0},{2,3},{3,2},{4,5},{5,4},{6,7},{7,6},{8,9},{9,8},{10,11... | collective-permute-start | bytes 786440 | tf_op jit(solution)/shard_map/ppermute | solution.py:465
  70.2 1.9 %shard_map.42 = bf16[128,8192]{1,0:T(8,128)(2,1)} custom-call(bf16[2,128,4096]{2,1,0:T(8,128)(2,1)S(1)} %get-tuple-element.60.q_ref, f32[2,128,4096]{2,1,0:T(8,128)S(1)} %get-tuple-element.61.inside_ref, f32[2,1,4096]{2,1,0:T(1,128)S(1)} %get-tuple-element.62.gain_ref, f32[128,4096]{1,0:T(8,128)S(1)} %get-tuple-element.80.refs_0_, ...), custom_call_target="tpu_custom_call" | custom-call | flops 134217728 | bytes 7340032 | tf_op jit(solution)/shard_map/pallas_call | solution.py:499
  (38 shorter events, 8.4 us)
Async XLA Ops:
  2.5 4.9 %collective-permute-start = (bf16[16,128,128]{2,1,0:T(8,128)(2,1)S(1)}, bf16[16,128,128]{2,1,0:T(8,128)(2,1)S(1)}, u32[]{:S(2)}, u32[]{:S(2)}) collective-permute-start(bf16[16,128,128]{2,1,0:T(8,128)(2,1)S(1)} %get-tuple-element.48), channel_id=1, source_target_pairs={{0,1},{1,0},{2,3},{3,2},{4,5},{5,4},{6,7},{7,6},{8,9},{9,8},{10,11... | collective-permute-start | bytes 1572872 | tf_op jit(solution)/shard_map/ppermute | solution.py:350
  5.8 3.0 %collective-permute-start.1 = (bf16[16,128,128]{2,1,0:T(8,128)(2,1)S(1)}, bf16[16,128,128]{2,1,0:T(8,128)(2,1)S(1)}, u32[]{:S(2)}, u32[]{:S(2)}) collective-permute-start(bf16[16,128,128]{2,1,0:T(8,128)(2,1)S(1)} %get-tuple-element.49), channel_id=1, source_target_pairs={{0,1},{1,0},{2,3},{3,2},{4,5},{5,4},{6,7},{7,6},{8,9},{9,8},{10,11... | collective-permute-start | bytes 1572872 | tf_op jit(solution)/shard_map/ppermute | solution.py:350
  7.4 3.6 %copy-start = (f32[8192]{0:T(1024)S(1)}, f32[8192]{0:T(1024)}, u32[]{:S(2)}) copy-start(f32[8192]{0:T(1024)} %param.3) | copy-start | bytes 98308
  7.5 8.0 %collective-permute-start.2 = (bf16[8,128,128]{2,1,0:T(8,128)(2,1)S(1)}, bf16[8,128,128]{2,1,0:T(8,128)(2,1)S(1)}, u32[]{:S(2)}, u32[]{:S(2)}) collective-permute-start(bf16[8,128,128]{2,1,0:T(8,128)(2,1)S(1)} %get-tuple-element.56), channel_id=1, source_target_pairs={{0,2},{1,3},{2,0},{3,1},{4,6},{5,7},{6,4},{7,5},{8,10},{9,11},{10,... | collective-permute-start | bytes 786440 | tf_op jit(solution)/shard_map/ppermute | solution.py:370
  7.6 9.6 %collective-permute-start.3 = (bf16[8,128,128]{2,1,0:T(8,128)(2,1)S(1)}, bf16[8,128,128]{2,1,0:T(8,128)(2,1)S(1)}, u32[]{:S(2)}, u32[]{:S(2)}) collective-permute-start(bf16[8,128,128]{2,1,0:T(8,128)(2,1)S(1)} %get-tuple-element.57), channel_id=1, source_target_pairs={{0,6},{1,7},{2,4},{3,5},{4,2},{5,3},{6,0},{7,1},{8,14},{9,15},{10,... | collective-permute-start | bytes 786440 | tf_op jit(solution)/shard_map/ppermute | solution.py:370
  8.9 12.3 %collective-permute-start.4 = (bf16[8,128,128]{2,1,0:T(8,128)(2,1)S(1)}, bf16[8,128,128]{2,1,0:T(8,128)(2,1)S(1)}, u32[]{:S(2)}, u32[]{:S(2)}) collective-permute-start(bf16[8,128,128]{2,1,0:T(8,128)(2,1)S(1)} %get-tuple-element.58), channel_id=1, source_target_pairs={{0,4},{1,5},{2,6},{3,7},{4,0},{5,1},{6,2},{7,3},{8,12},{9,13},{10,... | collective-permute-start | bytes 786440 | tf_op jit(solution)/shard_map/ppermute | solution.py:370
  21.3 4.7 %collective-permute-start.5 = (bf16[2,128,128]{2,1,0:T(8,128)(2,1)S(1)}, bf16[2,128,128]{2,1,0:T(8,128)(2,1)S(1)}, u32[]{:S(2)}, u32[]{:S(2)}) collective-permute-start(bf16[2,128,128]{2,1,0:T(8,128)(2,1)S(1)} %get-tuple-element.68), channel_id=1, source_target_pairs={{0,8},{8,0},{16,24},{24,16},{48,56},{56,48},{32,40},{40,32},{64,72... | collective-permute-start | bytes 196616 | tf_op jit(solution)/shard_map/ppermute | solution.py:419
  23.0 5.3 %collective-permute-start.6 = (bf16[2,128,128]{2,1,0:T(8,128)(2,1)S(1)}, bf16[2,128,128]{2,1,0:T(8,128)(2,1)S(1)}, u32[]{:S(2)}, u32[]{:S(2)}) collective-permute-start(bf16[2,128,128]{2,1,0:T(8,128)(2,1)S(1)} %get-tuple-element.69), channel_id=1, source_target_pairs={{0,16},{8,24},{16,0},{24,8},{48,32},{56,40},{32,48},{40,56},{64,80... | collective-permute-start | bytes 196616 | tf_op jit(solution)/shard_map/ppermute | solution.py:419
  26.0 4.9 %collective-permute-start.7 = (bf16[2,128,128]{2,1,0:T(8,128)(2,1)S(1)}, bf16[2,128,128]{2,1,0:T(8,128)(2,1)S(1)}, u32[]{:S(2)}, u32[]{:S(2)}) collective-permute-start(bf16[2,128,128]{2,1,0:T(8,128)(2,1)S(1)} %get-tuple-element.70), channel_id=1, source_target_pairs={{0,24},{8,16},{16,8},{24,0},{48,40},{56,32},{32,56},{40,48},{64,88... | collective-permute-start | bytes 196616 | tf_op jit(solution)/shard_map/ppermute | solution.py:419
  31.0 5.7 %collective-permute-start.8 = (bf16[2,128,128]{2,1,0:T(8,128)(2,1)S(1)}, bf16[2,128,128]{2,1,0:T(8,128)(2,1)S(1)}, u32[]{:S(2)}, u32[]{:S(2)}) collective-permute-start(bf16[2,128,128]{2,1,0:T(8,128)(2,1)S(1)} %shard_map.34), channel_id=1, source_target_pairs={{0,48},{8,56},{16,32},{24,40},{32,16},{40,24},{48,0},{56,8},{64,11... | collective-permute-start | bytes 196616 | tf_op jit(solution)/shard_map/ppermute | solution.py:423
  36.7 4.5 %collective-permute-start.11 = (bf16[2,128,128]{2,1,0:T(8,128)(2,1)S(1)}, bf16[2,128,128]{2,1,0:T(8,128)(2,1)S(1)}, u32[]{:S(2)}, u32[]{:S(2)}) collective-permute-start(bf16[2,128,128]{2,1,0:T(8,128)(2,1)S(1)} %add_convert_fusion), channel_id=1, source_target_pairs={{0,192},{8,200},{16,208},{24,216},{32,224},{40,232},{48,240},{56,2... | collective-permute-start | bytes 196616 | tf_op jit(solution)/shard_map/ppermute | solution.py:425
  39.6 4.6 %collective-permute-start.10 = (bf16[2,128,128]{2,1,0:T(8,128)(2,1)S(1)}, bf16[2,128,128]{2,1,0:T(8,128)(2,1)S(1)}, u32[]{:S(2)}, u32[]{:S(2)}) collective-permute-start(bf16[2,128,128]{2,1,0:T(8,128)(2,1)S(1)} %add_convert_fusion), channel_id=1, source_target_pairs={{0,128},{8,136},{16,144},{24,152},{32,160},{40,168},{48,176},{56,1... | collective-permute-start | bytes 196616 | tf_op jit(solution)/shard_map/ppermute | solution.py:425
  39.9 4.3 %collective-permute-start.9 = (bf16[2,128,128]{2,1,0:T(8,128)(2,1)S(1)}, bf16[2,128,128]{2,1,0:T(8,128)(2,1)S(1)}, u32[]{:S(2)}, u32[]{:S(2)}) collective-permute-start(bf16[2,128,128]{2,1,0:T(8,128)(2,1)S(1)} %add_convert_fusion), channel_id=1, source_target_pairs={{0,64},{8,72},{16,80},{24,88},{32,96},{40,104},{48,112},{56,120},{... | collective-permute-start | bytes 196616 | tf_op jit(solution)/shard_map/ppermute | solution.py:425
  44.4 3.6 %collective-permute-start.12 = (bf16[2,128,128]{2,1,0:T(8,128)(2,1)S(1)}, bf16[2,128,128]{2,1,0:T(8,128)(2,1)S(1)}, u32[]{:S(2)}, u32[]{:S(2)}) collective-permute-start(bf16[2,128,128]{2,1,0:T(8,128)(2,1)S(1)} %get-tuple-element.72), channel_id=1, source_target_pairs={{0,8},{8,0},{16,24},{24,16},{48,56},{56,48},{32,40},{40,32},{64,72... | collective-permute-start | bytes 196616 | tf_op jit(solution)/shard_map/ppermute | solution.py:435
  44.9 4.1 %collective-permute-start.13 = (bf16[2,128,128]{2,1,0:T(8,128)(2,1)S(1)}, bf16[2,128,128]{2,1,0:T(8,128)(2,1)S(1)}, u32[]{:S(2)}, u32[]{:S(2)}) collective-permute-start(bf16[2,128,128]{2,1,0:T(8,128)(2,1)S(1)} %get-tuple-element.73), channel_id=1, source_target_pairs={{0,16},{8,24},{16,0},{24,8},{48,32},{56,40},{32,48},{40,56},{64,80... | collective-permute-start | bytes 196616 | tf_op jit(solution)/shard_map/ppermute | solution.py:435
  46.0 5.0 %collective-permute-start.14 = (bf16[2,128,128]{2,1,0:T(8,128)(2,1)S(1)}, bf16[2,128,128]{2,1,0:T(8,128)(2,1)S(1)}, u32[]{:S(2)}, u32[]{:S(2)}) collective-permute-start(bf16[2,128,128]{2,1,0:T(8,128)(2,1)S(1)} %get-tuple-element.74), channel_id=1, source_target_pairs={{0,24},{8,16},{16,8},{24,0},{48,40},{56,32},{32,56},{40,48},{64,88... | collective-permute-start | bytes 196616 | tf_op jit(solution)/shard_map/ppermute | solution.py:435
  51.2 11.2 %collective-permute-start.15 = (bf16[8,128,128]{2,1,0:T(8,128)(2,1)S(1)}, bf16[8,128,128]{2,1,0:T(8,128)(2,1)S(1)}, u32[]{:S(2)}, u32[]{:S(2)}) collective-permute-start(bf16[8,128,128]{2,1,0:T(8,128)(2,1)S(1)} %get-tuple-element.75), channel_id=1, source_target_pairs={{0,2},{1,3},{2,0},{3,1},{4,6},{5,7},{6,4},{7,5},{8,10},{9,11},{10,... | collective-permute-start | bytes 786440 | tf_op jit(solution)/shard_map/ppermute | solution.py:453
  51.7 12.9 %collective-permute-start.16 = (bf16[8,128,128]{2,1,0:T(8,128)(2,1)S(1)}, bf16[8,128,128]{2,1,0:T(8,128)(2,1)S(1)}, u32[]{:S(2)}, u32[]{:S(2)}) collective-permute-start(bf16[8,128,128]{2,1,0:T(8,128)(2,1)S(1)} %get-tuple-element.76), channel_id=1, source_target_pairs={{0,6},{1,7},{2,4},{3,5},{4,2},{5,3},{6,0},{7,1},{8,14},{9,15},{10,... | collective-permute-start | bytes 786440 | tf_op jit(solution)/shard_map/ppermute | solution.py:453
  53.0 14.2 %collective-permute-start.17 = (bf16[8,128,128]{2,1,0:T(8,128)(2,1)S(1)}, bf16[8,128,128]{2,1,0:T(8,128)(2,1)S(1)}, u32[]{:S(2)}, u32[]{:S(2)}) collective-permute-start(bf16[8,128,128]{2,1,0:T(8,128)(2,1)S(1)} %get-tuple-element.77), channel_id=1, source_target_pairs={{0,4},{1,5},{2,6},{3,7},{4,0},{5,1},{6,2},{7,3},{8,12},{9,13},{10,... | collective-permute-start | bytes 786440 | tf_op jit(solution)/shard_map/ppermute | solution.py:453
  54.6 14.4 %collective-permute-start.19 = (bf16[8,128,128]{2,1,0:T(8,128)(2,1)S(1)}, bf16[8,128,128]{2,1,0:T(8,128)(2,1)S(1)}, u32[]{:S(2)}, u32[]{:S(2)}) collective-permute-start(bf16[8,128,128]{2,1,0:T(8,128)(2,1)S(1)} %shard_map.38), channel_id=1, source_target_pairs={{0,1},{1,0},{2,3},{3,2},{4,5},{5,4},{6,7},{7,6},{8,9},{9,8},{10,11... | collective-permute-start | bytes 786440 | tf_op jit(solution)/shard_map/ppermute | solution.py:465
  62.4 6.6 %collective-permute-start.18 = (bf16[8,128,128]{2,1,0:T(8,128)(2,1)S(1)}, bf16[8,128,128]{2,1,0:T(8,128)(2,1)S(1)}, u32[]{:S(2)}, u32[]{:S(2)}) collective-permute-start(bf16[8,128,128]{2,1,0:T(8,128)(2,1)S(1)} %shard_map.37), channel_id=1, source_target_pairs={{0,1},{1,0},{2,3},{3,2},{4,5},{5,4},{6,7},{7,6},{8,9},{9,8},{10,11... | collective-permute-start | bytes 786440 | tf_op jit(solution)/shard_map/ppermute | solution.py:465
  64.7 5.1 %collective-permute-start.20 = (bf16[8,128,128]{2,1,0:T(8,128)(2,1)S(1)}, bf16[8,128,128]{2,1,0:T(8,128)(2,1)S(1)}, u32[]{:S(2)}, u32[]{:S(2)}) collective-permute-start(bf16[8,128,128]{2,1,0:T(8,128)(2,1)S(1)} %shard_map.40), channel_id=1, source_target_pairs={{0,1},{1,0},{2,3},{3,2},{4,5},{5,4},{6,7},{7,6},{8,9},{9,8},{10,11... | collective-permute-start | bytes 786440 | tf_op jit(solution)/shard_map/ppermute | solution.py:465
  67.3 2.9 %collective-permute-start.21 = (bf16[8,128,128]{2,1,0:T(8,128)(2,1)S(1)}, bf16[8,128,128]{2,1,0:T(8,128)(2,1)S(1)}, u32[]{:S(2)}, u32[]{:S(2)}) collective-permute-start(bf16[8,128,128]{2,1,0:T(8,128)(2,1)S(1)} %shard_map.41), channel_id=1, source_target_pairs={{0,1},{1,0},{2,3},{3,2},{4,5},{5,4},{6,7},{7,6},{8,9},{9,8},{10,11... | collective-permute-start | bytes 786440 | tf_op jit(solution)/shard_map/ppermute | solution.py:465
